TPU v7x, 32 devices: a whole 2x2x4 slice. The times are simulated.
32 devices in a mesh: dp: 4 (over y, x), fsdp: 8 (over z, core).
Axes of the slice: x: 2, y: 2, z: 4, core: 2. Of those that a mesh axis runs over, the one named last changes fastest.
Arguments:
- images: bfloat16 [128, 197, 768], P(('dp', 'fsdp')), may hold values from -6 to 6
- counts: int32 [32], P(('dp', 'fsdp')), may hold values from 1 to 4, 96 in all
- cotangent: bfloat16 [128, 197, 768], P(('dp', 'fsdp')), may hold values from -6 to 6
- w_qkv: bfloat16 [2, 768, 2304], P(None, None, ('dp', 'fsdp')), may hold values from -0.21875 to 0.21875
- w_proj: bfloat16 [2, 768, 768], P(None, None, ('dp', 'fsdp')), may hold values from -1.75 to 1.75
- w_fc1: bfloat16 [2, 768, 3072], P(None, None, ('dp', 'fsdp')), may hold values from -0.21875 to 0.21875
- w_fc2: bfloat16 [2, 3072, 768], P(None, None, ('dp', 'fsdp')), may hold values from -0.109375 to 0.109375
- gains: bfloat16 [2, 2, 768], P(None, None, ('dp', 'fsdp')), may hold values from 0.25 to 1.75
- biases: bfloat16 [2, 6, 768], P(None, None, ('dp', 'fsdp')), may hold values from -1.5 to 1.5
- fc1_bias: bfloat16 [2, 1, 3072], P(None, None, ('dp', 'fsdp')), may hold values from -1.5 to 1.5
Outputs:
- block_output: bfloat16 [128, 197, 768], P(('dp', 'fsdp'))
- grad_images: float32 [128, 197, 768], P(('dp', 'fsdp'))
- grad_w_qkv: float32 [2, 768, 2304], P(None, None, ('dp', 'fsdp'))
- grad_w_proj: float32 [2, 768, 768], P(None, None, ('dp', 'fsdp'))
- grad_w_fc1: float32 [2, 768, 3072], P(None, None, ('dp', 'fsdp'))
- grad_w_fc2: float32 [2, 3072, 768], P(None, None, ('dp', 'fsdp'))
- grad_gains: float32 [2, 2, 768], P(None, None, ('dp', 'fsdp'))
- grad_biases: float32 [2, 6, 768], P(None, None, ('dp', 'fsdp'))
- grad_fc1_bias: float32 [2, 1, 3072], P(None, None, ('dp', 'fsdp'))
Inputs may be any that keep to these rules, and one draw needn't show every extreme that they name: counts[i] is how many of device i's 4 image slots hold live images, which come first; the counts add up to 96 and the largest is 4.
All inputs are finite; a program needn't handle non-finite values.
Results may differ from a plain program's by a relative error of at most 0.013.
Values may be sent and summed in bfloat16 or wider, within the bound.
No kernel may reach another device: no remote copies, remote signals or barrier semaphores. Data moves between devices by JAX's collectives and lax.ppermute only.
A program may use at most 256 MiB of HBM per device.

v0:
```python
from functools import partial

import jax
import jax.numpy as jnp
from jax import lax
from jax.sharding import PartitionSpec as P

HEAD_DIM = 64


def inner_rows(left, right):
    return lax.dot_general(
        left, right, (((0,), (0,)), ((), ())), preferred_element_type=jnp.float32
    )


def times_transposed(left, right):
    return lax.dot_general(
        left, right, (((1,), (1,)), ((), ())), preferred_element_type=jnp.float32
    )


def norm_parts(token_rows):
    row_mean = jnp.mean(token_rows, -1, keepdims=True)
    centered = token_rows - row_mean
    inv_std = lax.rsqrt(jnp.mean(centered * centered, -1, keepdims=True) + 1e-06)
    return (centered * inv_std, inv_std)


def norm_back(grad_normed, scaled, inv_std, gain_row):
    grad_scaled = grad_normed * gain_row
    return inv_std * (
        grad_scaled
        - jnp.mean(grad_scaled, -1, keepdims=True)
        - scaled * jnp.mean(grad_scaled * scaled, -1, keepdims=True)
    )


def layer_forward(state, full_weights, heads):
    w_qkv, w_proj, w_fc1, w_fc2, gains, biases, fc1_bias = full_weights
    gains = gains.astype(jnp.float32)
    biases = biases.astype(jnp.float32)
    slots, seq_len, width = state.shape
    head_shape = (slots, seq_len, heads, width // heads)
    token_rows = state.reshape(-1, width)
    scaled_one, inv_one = norm_parts(token_rows)
    normed_one = (scaled_one * gains[0] + biases[0]).astype(jnp.bfloat16)
    mixed = jnp.dot(normed_one, w_qkv, preferred_element_type=jnp.float32)
    query_heads = (mixed[:, :width] + biases[1]).astype(jnp.bfloat16).reshape(head_shape)
    key_heads = mixed[:, width : 2 * width].astype(jnp.bfloat16).reshape(head_shape)
    value_heads = (mixed[:, 2 * width :] + biases[2]).astype(jnp.bfloat16).reshape(head_shape)
    scores = jnp.einsum(
        "bqhd,bkhd->bhqk", query_heads, key_heads, preferred_element_type=jnp.float32
    )
    scores = scores * HEAD_DIM ** (-0.5)
    top_score = jnp.max(scores, -1, keepdims=True)
    expo_score = jnp.exp(scores - top_score)
    total_score = jnp.sum(expo_score, -1, keepdims=True)
    attn_probs = (expo_score / total_score).astype(jnp.bfloat16)
    log_total = top_score + jnp.log(total_score)
    attended = jnp.einsum(
        "bhqk,bkhd->bqhd", attn_probs, value_heads, preferred_element_type=jnp.float32
    )
    attended = attended.reshape(-1, width).astype(jnp.bfloat16)
    middle = token_rows + jnp.dot(attended, w_proj, preferred_element_type=jnp.float32) + biases[3]
    scaled_two, inv_two = norm_parts(middle)
    normed_two = (scaled_two * gains[1] + biases[4]).astype(jnp.bfloat16)
    hidden_pre = jnp.dot(normed_two, w_fc1, preferred_element_type=jnp.float32) + fc1_bias[
        0
    ].astype(jnp.float32)
    hidden = jax.nn.gelu(hidden_pre, approximate=False).astype(jnp.bfloat16)
    final = middle + jnp.dot(hidden, w_fc2, preferred_element_type=jnp.float32) + biases[5]
    kept = (
        token_rows,
        query_heads,
        key_heads,
        value_heads,
        log_total,
        attended,
        middle,
        hidden_pre,
    )
    return (final.reshape(state.shape), kept)


def layer_backward(grad_final, kept, full_weights):
    w_qkv, w_proj, w_fc1, w_fc2, gains, biases, fc1_bias = full_weights
    gains = gains.astype(jnp.float32)
    biases = biases.astype(jnp.float32)
    token_rows, query_heads, key_heads, value_heads, log_total, attended, middle, hidden_pre = kept
    width = token_rows.shape[1]
    scaled_one, inv_one = norm_parts(token_rows)
    normed_one = (scaled_one * gains[0] + biases[0]).astype(jnp.bfloat16)
    scaled_two, inv_two = norm_parts(middle)
    normed_two = (scaled_two * gains[1] + biases[4]).astype(jnp.bfloat16)
    gelu_value, gelu_pull = jax.vjp(partial(jax.nn.gelu, approximate=False), hidden_pre)
    hidden = gelu_value.astype(jnp.bfloat16)
    branch_two = grad_final.astype(jnp.bfloat16)
    grad_fc2 = inner_rows(hidden, branch_two)
    grad_fc2_bias = jnp.sum(branch_two.astype(jnp.float32), 0)
    grad_hidden = times_transposed(branch_two, w_fc2)
    grad_pre = gelu_pull(grad_hidden)[0].astype(jnp.bfloat16)
    grad_fc1 = inner_rows(normed_two, grad_pre)
    grad_fc1_bias = jnp.sum(grad_pre.astype(jnp.float32), 0)
    grad_normed_two = times_transposed(grad_pre, w_fc1)
    grad_gain_two = jnp.sum(grad_normed_two * scaled_two, 0)
    grad_shift_two = jnp.sum(grad_normed_two, 0)
    grad_middle = grad_final + norm_back(grad_normed_two, scaled_two, inv_two, gains[1])
    branch_one = grad_middle.astype(jnp.bfloat16)
    grad_proj = inner_rows(attended, branch_one)
    grad_proj_bias = jnp.sum(branch_one.astype(jnp.float32), 0)
    grad_attended = (
        times_transposed(branch_one, w_proj).astype(jnp.bfloat16).reshape(query_heads.shape)
    )
    scores = jnp.einsum(
        "bqhd,bkhd->bhqk", query_heads, key_heads, preferred_element_type=jnp.float32
    )
    scores = scores * HEAD_DIM ** (-0.5)
    attn_exact = jnp.exp(scores - log_total)
    attn_probs = attn_exact.astype(jnp.bfloat16)
    grad_values = jnp.einsum(
        "bhqk,bqhd->bkhd", attn_probs, grad_attended, preferred_element_type=jnp.float32
    )
    grad_probs = jnp.einsum(
        "bqhd,bkhd->bhqk", grad_attended, value_heads, preferred_element_type=jnp.float32
    )
    row_inner = jnp.sum(grad_probs * attn_exact, -1, keepdims=True)
    grad_scores = (attn_exact * (grad_probs - row_inner)).astype(jnp.bfloat16)
    grad_query = jnp.einsum(
        "bhqk,bkhd->bqhd", grad_scores, key_heads, preferred_element_type=jnp.float32
    )
    grad_keys = jnp.einsum(
        "bhqk,bqhd->bkhd", grad_scores, query_heads, preferred_element_type=jnp.float32
    )
    grad_mixed = jnp.concatenate(
        [
            (grad_query * HEAD_DIM ** (-0.5)).reshape(-1, width),
            (grad_keys * HEAD_DIM ** (-0.5)).reshape(-1, width),
            grad_values.reshape(-1, width),
        ],
        1,
    ).astype(jnp.bfloat16)
    grad_qkv = inner_rows(normed_one, grad_mixed)
    grad_columns = jnp.sum(grad_mixed.astype(jnp.float32), 0)
    grad_normed_one = times_transposed(grad_mixed, w_qkv)
    grad_gain_one = jnp.sum(grad_normed_one * scaled_one, 0)
    grad_shift_one = jnp.sum(grad_normed_one, 0)
    grad_input = grad_middle + norm_back(grad_normed_one, scaled_one, inv_one, gains[0])
    gains_grad = jnp.stack([grad_gain_one, grad_gain_two])
    biases_grad = jnp.stack(
        [
            grad_shift_one,
            grad_columns[:width],
            grad_columns[2 * width :],
            grad_proj_bias,
            grad_shift_two,
            grad_fc2_bias,
        ]
    )
    grads = (grad_qkv, grad_proj, grad_fc1, grad_fc2, gains_grad, biases_grad, grad_fc1_bias[None])
    return (grad_input, grads)


def on_device(images, counts, cotangent, w_qkv, w_proj, w_fc1, w_fc2, gains, biases, fc1_bias):
    slots, seq_len, width = images.shape
    heads = width // HEAD_DIM
    layer_count = w_qkv.shape[0]
    live = (jnp.arange(slots) < counts[0]).astype(jnp.float32)[:, None, None]
    state = images.astype(jnp.float32)
    kept_layers = []
    gathered_layers = []
    for layer_index in range(layer_count):
        full_weights = (
            lax.all_gather(w_qkv[layer_index], ("dp", "fsdp"), axis=1, tiled=True),
            lax.all_gather(w_proj[layer_index], ("dp", "fsdp"), axis=1, tiled=True),
            lax.all_gather(w_fc1[layer_index], ("dp", "fsdp"), axis=1, tiled=True),
            lax.all_gather(w_fc2[layer_index], ("dp", "fsdp"), axis=1, tiled=True),
            lax.all_gather(gains[layer_index], ("dp", "fsdp"), axis=1, tiled=True),
            lax.all_gather(biases[layer_index], ("dp", "fsdp"), axis=1, tiled=True),
            lax.all_gather(fc1_bias[layer_index], ("dp", "fsdp"), axis=1, tiled=True),
        )
        state, kept = layer_forward(state, full_weights, heads)
        kept_layers.append(kept)
        gathered_layers.append(full_weights)
    block_output = (state * live).astype(jnp.bfloat16)
    grad_state = (cotangent.astype(jnp.float32) * live).reshape(-1, width)
    layer_grads = [None] * layer_count
    for layer_index in reversed(range(layer_count)):
        full_weights = (
            lax.all_gather(w_qkv[layer_index], ("dp", "fsdp"), axis=1, tiled=True),
            lax.all_gather(w_proj[layer_index], ("dp", "fsdp"), axis=1, tiled=True),
            lax.all_gather(w_fc1[layer_index], ("dp", "fsdp"), axis=1, tiled=True),
            lax.all_gather(w_fc2[layer_index], ("dp", "fsdp"), axis=1, tiled=True),
            lax.all_gather(gains[layer_index], ("dp", "fsdp"), axis=1, tiled=True),
            lax.all_gather(biases[layer_index], ("dp", "fsdp"), axis=1, tiled=True),
            lax.all_gather(fc1_bias[layer_index], ("dp", "fsdp"), axis=1, tiled=True),
        )
        grad_state, grads = layer_backward(grad_state, kept_layers[layer_index], full_weights)
        grad_qkv, grad_proj, grad_fc1, grad_fc2, gains_grad, biases_grad, fc1_grad = grads
        layer_grads[layer_index] = (
            lax.psum_scatter(grad_qkv, ("dp", "fsdp"), scatter_dimension=1, tiled=True),
            lax.psum_scatter(grad_proj, ("dp", "fsdp"), scatter_dimension=1, tiled=True),
            lax.psum_scatter(grad_fc1, ("dp", "fsdp"), scatter_dimension=1, tiled=True),
            lax.psum_scatter(grad_fc2, ("dp", "fsdp"), scatter_dimension=1, tiled=True),
            lax.psum_scatter(gains_grad, ("dp", "fsdp"), scatter_dimension=1, tiled=True),
            lax.psum_scatter(biases_grad, ("dp", "fsdp"), scatter_dimension=1, tiled=True),
            lax.psum_scatter(fc1_grad, ("dp", "fsdp"), scatter_dimension=1, tiled=True),
        )
    stacked = tuple((jnp.stack([entry[member] for entry in layer_grads]) for member in range(7)))
    grad_images = grad_state.reshape(images.shape)
    return (
        block_output,
        grad_images,
        stacked[0],
        stacked[1],
        stacked[2],
        stacked[3],
        stacked[4],
        stacked[5],
        stacked[6],
    )


def solution(mesh):
    placed = (
        P(("dp", "fsdp"), None, None),
        P(("dp", "fsdp")),
        P(("dp", "fsdp"), None, None),
        P(None, None, ("dp", "fsdp")),
        P(None, None, ("dp", "fsdp")),
        P(None, None, ("dp", "fsdp")),
        P(None, None, ("dp", "fsdp")),
        P(None, None, ("dp", "fsdp")),
        P(None, None, ("dp", "fsdp")),
        P(None, None, ("dp", "fsdp")),
    )
    return jax.shard_map(
        on_device,
        mesh=mesh,
        in_specs=placed,
        out_specs=(
            P(("dp", "fsdp"), None, None),
            P(("dp", "fsdp"), None, None),
            P(None, None, ("dp", "fsdp")),
            P(None, None, ("dp", "fsdp")),
            P(None, None, ("dp", "fsdp")),
            P(None, None, ("dp", "fsdp")),
            P(None, None, ("dp", "fsdp")),
            P(None, None, ("dp", "fsdp")),
            P(None, None, ("dp", "fsdp")),
        ),
        check_vma=False,
    )
```

profile of v0, /device:TPU:0, one launch (start us, length us, event | category | flops | bytes accessed | tf_op | source)
XLA Modules:
  0.0 1828.1 jit_solution(7288019010313021280)
XLA Ops:
  21.9 42.3 %all-reduce.7 = (bf16[3072]{0:T(1024)(128)(2,1)S(1)}, bf16[3072]{0:T(1024)(128)(2,1)S(1)}) all-reduce(bf16[3072]{0:T(1024)(128)(2,1)S(1)} %dynamic-update-slice, bf16[3072]{0:T(1024)(128)(2,1)S(1)} %dynamic-update-slice.1), channel_id=7, replica_groups=mesh['dp'=4,'fsdp'=8] {'dp','fsdp'}, use_global_device_ids=true, to_apply=%add | all-reduce | flops 6144 | bytes 24576
  65.5 42.0 %all-gather = bf16[1,2,768]{1,0,2:T(2,128)(2,1)S(1)} all-gather(bf16[1,2,24]{1,0,2:T(2,128)(2,1)S(1)} %copy.283), channel_id=2, replica_groups=mesh['dp'=4,'fsdp'=8] {'dp','fsdp'}, dimensions={2}, use_global_device_ids=true | all-gather | bytes 3168 | tf_op jit(solution)/shard_map/all_gather | solution.py:178
  112.5 38.7 %all-gather.1 = bf16[1,6,768]{1,0,2:T(2,128)(2,1)S(1)} all-gather(bf16[1,6,24]{1,0,2:T(2,128)(2,1)S(1)} %copy.284), channel_id=3, replica_groups=mesh['dp'=4,'fsdp'=8] {'dp','fsdp'}, dimensions={2}, use_global_device_ids=true | all-gather | bytes 9504 | tf_op jit(solution)/shard_map/all_gather | solution.py:179
  151.7 12.8 slice_reduce_fusion.8
  164.5 40.3 %all-gather.7 = bf16[1,2,768]{1,0,2:T(2,128)(2,1)S(1)} all-gather(bf16[1,2,24]{1,0,2:T(2,128)(2,1)S(1)} %copy.285), channel_id=9, replica_groups=mesh['dp'=4,'fsdp'=8] {'dp','fsdp'}, dimensions={2}, use_global_device_ids=true | all-gather | bytes 3168 | tf_op jit(solution)/shard_map/all_gather | solution.py:178
  209.8 39.3 %all-gather.8 = bf16[1,6,768]{1,0,2:T(2,128)(2,1)S(1)} all-gather(bf16[1,6,24]{1,0,2:T(2,128)(2,1)S(1)} %copy.286), channel_id=10, replica_groups=mesh['dp'=4,'fsdp'=8] {'dp','fsdp'}, dimensions={2}, use_global_device_ids=true | all-gather | bytes 9504 | tf_op jit(solution)/shard_map/all_gather | solution.py:179
  249.6 13.4 slice_reduce_fusion
  317.2 29.9 %multiply_convert_fusion.3 = (bf16[788,3072]{1,0:T(8,128)(2,1)}, f32[788,3072]{1,0:T(8,128)}, f32[788,3072]{1,0:T(8,128)}) fusion(f32[3072]{0:T(1024)S(1)} %add.333, bf16[1,768,3072]{1,2,0:T(8,128)(2,1)} %all-gather.27.cloned.1.call-done, f32[788,768]{1,0:T(8,128)} %copy-done.16, f32[768]{0:T(1024)S(1)} %get-tuple-element.79, ...), kind=kOutput, calls=%fused_computation.31 | convolution fusion | flops 3881044992 | bytes 31371424 | tf_op jit(solution)/shard_map/dot_general | solution.py:68
  405.3 44.4 %all-gather.35.cloned.1.call-done = bf16[1,768,3072]{1,2,0:T(8,128)(2,1)} async-done(((bf16[1,768,96]{1,2,0:T(8,128)(2,1)}), bf16[1,768,3072]{1,2,0:T(8,128)(2,1)}) %all-gather.35.cloned.1.call-update) | async-done | bytes 4718608 | tf_op jit(solution)/shard_map/all_gather | solution.py:176
  449.8 28.7 %multiply_convert_fusion.2 = (bf16[788,3072]{1,0:T(8,128)(2,1)}, f32[788,3072]{1,0:T(8,128)}, f32[788,3072]{1,0:T(8,128)}) fusion(f32[3072]{0:T(1024)S(1)} %copy-done.73, bf16[1,768,3072]{1,2,0:T(8,128)(2,1)} %all-gather.35.cloned.1.call-done, f32[788,768]{1,0:T(8,128)S(1)} %get-tuple-element.137, f32[768]{0:T(1024)S(1)} %copy-done.79, ...), kind=kOutput, calls=%fused_computation.18 | convolution fusion | flops 3881044992 | bytes 31371424 | tf_op jit(solution)/shard_map/dot_general | solution.py:68
  478.4 37.4 %all-gather.37.cloned.1.call-done = bf16[1,3072,768]{1,2,0:T(8,128)(2,1)} async-done(((bf16[1,3072,24]{1,2,0:T(8,128)(2,1)}), bf16[1,3072,768]{1,2,0:T(8,128)(2,1)}) %all-gather.37.cloned.1.call-update) | async-done | bytes 4718608 | tf_op jit(solution)/shard_map/all_gather | solution.py:177
  533.2 13.5 convert_reduce_fusion
  581.4 11.6 multiply_convert_fusion.1
  625.8 13.5 convert_reduce_fusion.1
  702.3 11.7 multiply_convert_fusion
  796.6 40.7 %all-reduce.6 = (f32[2,768]{1,0:T(2,128)S(1)}, f32[2,768]{1,0:T(2,128)S(1)}, f32[6,768]{1,0:T(8,128)S(1)}, f32[6,768]{1,0:T(8,128)S(1)}) all-reduce(f32[2,768]{1,0:T(2,128)S(1)} %pad_maximum_fusion.6, f32[2,768]{1,0:T(2,128)S(1)} %pad_maximum_fusion.5, ...), channel_id=25, replica_groups=mesh['dp'=4,'fsdp'=8] {'dp','fsdp'}, use_global_device_ids=true, to_apply=%region_35.0.clone | all-reduce | flops 12288 | bytes 98304
  849.3 53.6 %reduce-scatter.25.cloned.1.call-done = f32[768,24]{0,1:T(8,128)} async-done(((f32[768,768]{0,1:T(8,128)}), f32[768,24]{0,1:T(8,128)}) %reduce-scatter.25.cloned.1.call-update) | async-done | bytes 73744 | tf_op jit(solution)/shard_map/reduce_scatter | solution.py:202
  902.9 104.1 %reduce-scatter.23.cloned.1.call-done = f32[768,24]{0,1:T(8,128)} async-done(((f32[768,768]{0,1:T(8,128)}), f32[768,24]{0,1:T(8,128)}) %reduce-scatter.23.cloned.1.call-update) | async-done | bytes 73744 | tf_op jit(solution)/shard_map/reduce_scatter | solution.py:202
  1008.6 122.0 %reduce-scatter.21.cloned.1.call-done = f32[768,72]{0,1:T(8,128)} async-done(((f32[768,2304]{0,1:T(8,128)}), f32[768,72]{0,1:T(8,128)}) %reduce-scatter.21.cloned.1.call-update) | async-done | bytes 221200 | tf_op jit(solution)/shard_map/reduce_scatter | solution.py:201
  1130.6 125.0 %reduce-scatter.19.cloned.1.call-done = f32[768,72]{0,1:T(8,128)} async-done(((f32[768,2304]{0,1:T(8,128)}), f32[768,72]{0,1:T(8,128)}) %reduce-scatter.19.cloned.1.call-update) | async-done | bytes 221200 | tf_op jit(solution)/shard_map/reduce_scatter | solution.py:201
  1257.4 138.6 %reduce-scatter.29.cloned.1.call-done = f32[768,96]{0,1:T(8,128)} async-done(((f32[768,3072]{0,1:T(8,128)}), f32[768,96]{0,1:T(8,128)}) %reduce-scatter.29.cloned.1.call-update) | async-done | bytes 294928 | tf_op jit(solution)/shard_map/reduce_scatter | solution.py:203
  1396.0 141.3 %reduce-scatter.27.cloned.1.call-done = f32[768,96]{0,1:T(8,128)} async-done(((f32[768,3072]{0,1:T(8,128)}), f32[768,96]{0,1:T(8,128)}) %reduce-scatter.27.cloned.1.call-update) | async-done | bytes 294928 | tf_op jit(solution)/shard_map/reduce_scatter | solution.py:203
  1539.2 138.6 %reduce-scatter.33.cloned.1.call-done = f32[3072,24]{0,1:T(8,128)} async-done(((f32[3072,768]{0,1:T(8,128)}), f32[3072,24]{0,1:T(8,128)}) %reduce-scatter.33.cloned.1.call-update) | async-done | bytes 294928 | tf_op jit(solution)/shard_map/reduce_scatter | solution.py:204
  1677.8 141.4 %reduce-scatter.31.cloned.1.call-done = f32[3072,24]{0,1:T(8,128)} async-done(((f32[3072,768]{0,1:T(8,128)}), f32[3072,24]{0,1:T(8,128)}) %reduce-scatter.31.cloned.1.call-update) | async-done | bytes 294928 | tf_op jit(solution)/shard_map/reduce_scatter | solution.py:204
  (411 shorter events, 386.8 us)
Async XLA Ops:
  7.2 257.5 %all-gather.23.cloned.1.call-start = ((), (), s32[]{:S(2)}) async-start(), calls=%async_computation.18 | async-start | bytes 3649536 | tf_op jit(solution)/shard_map/all_gather | solution.py:174
  9.0 303.2 %all-gather.25.cloned.1.call-start = ((), (), s32[]{:S(2)}) async-start(), calls=%async_computation.19 | async-start | bytes 1216512 | tf_op jit(solution)/shard_map/all_gather | solution.py:175
  10.5 306.7 %all-gather.27.cloned.1.call-start = ((), (), s32[]{:S(2)}) async-start(), calls=%async_computation.20 | async-start | bytes 4866048 | tf_op jit(solution)/shard_map/all_gather | solution.py:176
  12.3 334.8 %all-gather.29.cloned.1.call-start = ((), (), s32[]{:S(2)}) async-start(), calls=%async_computation.21 | async-start | bytes 4866048 | tf_op jit(solution)/shard_map/all_gather | solution.py:177
  14.1 342.9 %all-gather.31.cloned.1.call-start = ((), (), s32[]{:S(2)}) async-start(), calls=%async_computation.22 | async-start | bytes 3649536 | tf_op jit(solution)/shard_map/all_gather | solution.py:174
  14.6 386.3 %all-gather.33.cloned.1.call-start = ((), (), s32[]{:S(2)}) async-start(), calls=%async_computation.23 | async-start | bytes 1216512 | tf_op jit(solution)/shard_map/all_gather | solution.py:175
  15.2 434.5 %all-gather.35.cloned.1.call-start = ((), (), s32[]{:S(2)}) async-start(), calls=%async_computation.24 | async-start | bytes 4866048 | tf_op jit(solution)/shard_map/all_gather | solution.py:176
  16.0 499.9 %all-gather.37.cloned.1.call-start = ((), (), s32[]{:S(2)}) async-start(), calls=%async_computation.25 | async-start | bytes 4866048 | tf_op jit(solution)/shard_map/all_gather | solution.py:177
  16.7 830.3 %reduce-scatter.37.cloned.1.call-start = ((), (), s32[]{:S(2)}) async-start(), calls=%async_computation.27 | async-start | bytes 1622016
  64.2 253.0 %copy-start.71 = (f32[3072]{0:T(1024)}, f32[3072]{0:T(1024)S(1)}, u32[]{:S(2)}) copy-start(f32[3072]{0:T(1024)S(1)} %add.333) | copy-start | bytes 36868
  65.3 199.4 %copy-start.63 = (f32[788]{0:T(1024)}, f32[788]{0:T(1024)S(1)}, u32[]{:S(2)}) copy-start(f32[788]{0:T(1024)S(1)} %div.75) | copy-start | bytes 9460
  65.5 199.2 %copy-start.65 = (f32[788]{0:T(1024)}, f32[788]{0:T(1024)S(1)}, u32[]{:S(2)}) copy-start(f32[788]{0:T(1024)S(1)} %rsqrt.40) | copy-start | bytes 9460
  112.5 152.2 %copy-start.54 = (f32[768]{0:T(1024)}, f32[768]{0:T(1024)S(1)}, u32[]{:S(2)}) copy-start(f32[768]{0:T(1024)S(1)} %get-tuple-element.85) | copy-start | bytes 9220
  112.5 204.6 %copy-start.56 = (f32[768]{0:T(1024)}, f32[768]{0:T(1024)S(1)}, u32[]{:S(2)}) copy-start(f32[768]{0:T(1024)S(1)} %get-tuple-element.84) | copy-start | bytes 9220
  164.5 152.6 %copy-start.75 = (f32[768]{0:T(1024)}, f32[768]{0:T(1024)S(1)}, u32[]{:S(2)}) copy-start(f32[768]{0:T(1024)S(1)} %get-tuple-element.79) | copy-start | bytes 9220
  602.3 245.6 %reduce-scatter.35.cloned.1.call-start = ((), (), s32[]{:S(2)}) async-start(), calls=%async_computation.26 | async-start | bytes 1622016
  641.1 261.8 %reduce-scatter.25.cloned.1.call-start = ((), (), s32[]{:S(2)}) async-start(), calls=%async_computation.13 | async-start | bytes 2433024 | tf_op jit(solution)/shard_map/reduce_scatter | solution.py:202
  646.3 360.6 %reduce-scatter.23.cloned.1.call-start = ((), (), s32[]{:S(2)}) async-start(), calls=%async_computation.12 | async-start | bytes 2433024 | tf_op jit(solution)/shard_map/reduce_scatter | solution.py:202
  659.3 471.3 %reduce-scatter.21.cloned.1.call-start = ((), (), s32[]{:S(2)}) async-start(), calls=%async_computation.11 | async-start | bytes 7299072 | tf_op jit(solution)/shard_map/reduce_scatter | solution.py:201
  669.3 586.3 %reduce-scatter.19.cloned.1.call-start = ((), (), s32[]{:S(2)}) async-start(), calls=%async_computation.10 | async-start | bytes 7299072 | tf_op jit(solution)/shard_map/reduce_scatter | solution.py:201
  739.0 657.1 %reduce-scatter.29.cloned.1.call-start = ((), (), s32[]{:S(2)}) async-start(), calls=%async_computation.15 | async-start | bytes 9732096 | tf_op jit(solution)/shard_map/reduce_scatter | solution.py:203
  750.1 787.2 %reduce-scatter.27.cloned.1.call-start = ((), (), s32[]{:S(2)}) async-start(), calls=%async_computation.14 | async-start | bytes 9732096 | tf_op jit(solution)/shard_map/reduce_scatter | solution.py:203
  761.2 916.6 %reduce-scatter.33.cloned.1.call-start = ((), (), s32[]{:S(2)}) async-start(), calls=%async_computation.17 | async-start | bytes 9732096 | tf_op jit(solution)/shard_map/reduce_scatter | solution.py:204
  771.6 1047.5 %reduce-scatter.31.cloned.1.call-start = ((), (), s32[]{:S(2)}) async-start(), calls=%async_computation.16 | async-start | bytes 9732096 | tf_op jit(solution)/shard_map/reduce_scatter | solution.py:204
  (88 other events, 1305.3 us)
Sparse Core Ops, SparseCore 0:
  11.6 63.9 all-gather.22
  78.6 52.7 all-gather.24
  135.0 63.1 all-gather.26
  201.6 63.4 all-gather.28
  268.6 59.0 all-gather.30
  330.5 52.9 all-gather.32
  387.1 62.5 all-gather.34
  453.3 62.4 all-gather.36
  602.4 95.8 reduce-scatter.36
  703.4 96.0 reduce-scatter.34
  804.8 98.0 reduce-scatter.24
  908.9 98.0 reduce-scatter.22
  1012.6 117.8 reduce-scatter.20
  1137.1 118.4 reduce-scatter.18
  1261.3 134.6 reduce-scatter.28
  1402.8 134.4 reduce-scatter.26
  1543.0 134.6 reduce-scatter.32
  1684.5 134.5 reduce-scatter.30
where the time goes:
time: 1840 us; the launch traced here: 1830 us
  waiting for transfers between devices  1050 us (57%)
  matrix products  274 us (15%)
  blocking collectives  243 us (13%)
  local copies, waits for them, and re-layouts  184 us (10%)
  other arithmetic  59.9 us (3%)
    reduce_scatter x2, waiting for transfers between devices, on_device(): lax.psum_scatter(grad_fc2, ('dp', 'fsdp'), scatter_dimension=1, tiled=True)  280 us
    reduce_scatter x2, waiting for transfers between devices, on_device(): lax.psum_scatter(grad_fc1, ('dp', 'fsdp'), scatter_dimension=1, tiled=True)  280 us
    reduce_scatter x2, waiting for transfers between devices, on_device(): lax.psum_scatter(grad_qkv, ('dp', 'fsdp'), scatter_dimension=1, tiled=True)  247 us
    reduce_scatter x2, waiting for transfers between devices, on_device(): lax.psum_scatter(grad_proj, ('dp', 'fsdp'), scatter_dimension=1, tiled=True)  158 us
    unnamed x2, blocking collectives  83 us
    all_gather x2, blocking collectives, on_device(): lax.all_gather(gains[layer_index], ('dp', 'fsdp'), axis=1, tiled=True)  82.3 us
    all_gather x2, blocking collectives, on_device(): lax.all_gather(biases[layer_index], ('dp', 'fsdp'), axis=1, tiled=True)  78.1 us
    dot_general x8, matrix products, inner_rows(): lax.dot_general(left, right, (((0,), (0,)), ((), ())), preferred_element_...  66 us
  transfers between devices with their start and end apart: 18, of which 10 were waited for; matrix products, arithmetic and copies ran while one was open for 23% of the time, Pallas kernels for 0%

commit v1 on v0

--- a/solution.py
+++ b/solution.py
@@ -45,7 +45,7 @@
     token_rows = state.reshape(-1, width)
     scaled_one, inv_one = norm_parts(token_rows)
     normed_one = (scaled_one * gains[0] + biases[0]).astype(jnp.bfloat16)
-    mixed = jnp.dot(normed_one, w_qkv, preferred_element_type=jnp.float32)
+    mixed = times_transposed(normed_one, w_qkv)
     query_heads = (mixed[:, :width] + biases[1]).astype(jnp.bfloat16).reshape(head_shape)
     key_heads = mixed[:, width : 2 * width].astype(jnp.bfloat16).reshape(head_shape)
     value_heads = (mixed[:, 2 * width :] + biases[2]).astype(jnp.bfloat16).reshape(head_shape)
@@ -62,14 +62,14 @@
         "bhqk,bkhd->bqhd", attn_probs, value_heads, preferred_element_type=jnp.float32
     )
     attended = attended.reshape(-1, width).astype(jnp.bfloat16)
-    middle = token_rows + jnp.dot(attended, w_proj, preferred_element_type=jnp.float32) + biases[3]
+    middle = token_rows + times_transposed(attended, w_proj) + biases[3]
     scaled_two, inv_two = norm_parts(middle)
     normed_two = (scaled_two * gains[1] + biases[4]).astype(jnp.bfloat16)
-    hidden_pre = jnp.dot(normed_two, w_fc1, preferred_element_type=jnp.float32) + fc1_bias[
+    hidden_pre = times_transposed(normed_two, w_fc1) + fc1_bias[
         0
     ].astype(jnp.float32)
     hidden = jax.nn.gelu(hidden_pre, approximate=False).astype(jnp.bfloat16)
-    final = middle + jnp.dot(hidden, w_fc2, preferred_element_type=jnp.float32) + biases[5]
+    final = middle + times_transposed(hidden, w_fc2) + biases[5]
     kept = (
         token_rows,
         query_heads,
@@ -96,21 +96,21 @@
     gelu_value, gelu_pull = jax.vjp(partial(jax.nn.gelu, approximate=False), hidden_pre)
     hidden = gelu_value.astype(jnp.bfloat16)
     branch_two = grad_final.astype(jnp.bfloat16)
-    grad_fc2 = inner_rows(hidden, branch_two)
+    grad_fc2 = inner_rows(branch_two, hidden)
     grad_fc2_bias = jnp.sum(branch_two.astype(jnp.float32), 0)
-    grad_hidden = times_transposed(branch_two, w_fc2)
+    grad_hidden = jnp.dot(branch_two, w_fc2, preferred_element_type=jnp.float32)
     grad_pre = gelu_pull(grad_hidden)[0].astype(jnp.bfloat16)
-    grad_fc1 = inner_rows(normed_two, grad_pre)
+    grad_fc1 = inner_rows(grad_pre, normed_two)
     grad_fc1_bias = jnp.sum(grad_pre.astype(jnp.float32), 0)
-    grad_normed_two = times_transposed(grad_pre, w_fc1)
+    grad_normed_two = jnp.dot(grad_pre, w_fc1, preferred_element_type=jnp.float32)
     grad_gain_two = jnp.sum(grad_normed_two * scaled_two, 0)
     grad_shift_two = jnp.sum(grad_normed_two, 0)
     grad_middle = grad_final + norm_back(grad_normed_two, scaled_two, inv_two, gains[1])
     branch_one = grad_middle.astype(jnp.bfloat16)
-    grad_proj = inner_rows(attended, branch_one)
+    grad_proj = inner_rows(branch_one, attended)
     grad_proj_bias = jnp.sum(branch_one.astype(jnp.float32), 0)
     grad_attended = (
-        times_transposed(branch_one, w_proj).astype(jnp.bfloat16).reshape(query_heads.shape)
+        jnp.dot(branch_one, w_proj, preferred_element_type=jnp.float32).astype(jnp.bfloat16).reshape(query_heads.shape)
     )
     scores = jnp.einsum(
         "bqhd,bkhd->bhqk", query_heads, key_heads, preferred_element_type=jnp.float32
@@ -140,9 +140,9 @@
         ],
         1,
     ).astype(jnp.bfloat16)
-    grad_qkv = inner_rows(normed_one, grad_mixed)
+    grad_qkv = inner_rows(grad_mixed, normed_one)
     grad_columns = jnp.sum(grad_mixed.astype(jnp.float32), 0)
-    grad_normed_one = times_transposed(grad_mixed, w_qkv)
+    grad_normed_one = jnp.dot(grad_mixed, w_qkv, preferred_element_type=jnp.float32)
     grad_gain_one = jnp.sum(grad_normed_one * scaled_one, 0)
     grad_shift_one = jnp.sum(grad_normed_one, 0)
     grad_input = grad_middle + norm_back(grad_normed_one, scaled_one, inv_one, gains[0])
@@ -161,64 +161,112 @@
     return (grad_input, grads)
 
 
-def on_device(images, counts, cotangent, w_qkv, w_proj, w_fc1, w_fc2, gains, biases, fc1_bias):
+AXES = ("dp", "fsdp")
+
+
+def pack_layer(w_qkv, w_proj, w_fc1, w_fc2, gains, biases, fc1_bias):
+    width, tall = w_qkv.shape[0], w_fc2.shape[0]
+    cut = w_fc2.T.reshape(w_fc2.shape[1], tall // width, width).transpose(1, 0, 2)
+    small = jnp.concatenate([gains.reshape(-1), biases.reshape(-1), fc1_bias.reshape(-1)])
+    small = jnp.pad(small, (0, -small.size % width)).reshape(-1, width)
+    small = jnp.pad(small, ((0, -small.shape[0] % 16), (0, 0)))
+    return jnp.concatenate([w_qkv.T, w_proj.T, w_fc1.T, cut.reshape(-1, width), small], 0)
+
+
+def unpack_layer(blob, shapes):
+    devices, _, width = blob.shape
+    qkv, proj, fc1, fc2, gains, biases, fc1_bias = shapes
+    at = 0
+    parts = []
+    for columns in (qkv[1], proj[1], fc1[1]):
+        parts.append(blob[:, at : at + columns].reshape(-1, width))
+        at += columns
+    blocks = fc2[0] // width
+    cut = blob[:, at : at + blocks * fc2[1]].reshape(devices, blocks, fc2[1], width)
+    parts.append(cut.transpose(0, 2, 1, 3).reshape(devices * fc2[1], fc2[0]))
+    at += blocks * fc2[1]
+    small = blob[:, at:].reshape(devices, -1)
+    start = 0
+    for rows, columns in (gains, biases, fc1_bias):
+        piece = small[:, start : start + rows * columns].reshape(devices, rows, columns)
+        parts.append(piece.transpose(1, 0, 2).reshape(rows, devices * columns))
+        start += rows * columns
+    return tuple(parts)
+
+
+def pack_grads(grads, shapes, total_rows, devices):
+    grad_qkv, grad_proj, grad_fc1, grad_fc2, gains_grad, biases_grad, fc1_grad = grads
+    width = grad_qkv.shape[1]
+    qkv, proj, fc1, fc2, gains, biases, fc1_bias = shapes
+    blob = jnp.zeros((devices, total_rows, width), jnp.bfloat16)
+    at = 0
+    for value in (grad_qkv, grad_proj, grad_fc1):
+        rows = value.shape[0] // devices
+        blob = blob.at[:, at : at + rows].set(
+            value.astype(jnp.bfloat16).reshape(devices, rows, width)
+        )
+        at += rows
+    blocks = fc2[0] // width
+    cut = grad_fc2.astype(jnp.bfloat16).reshape(devices, fc2[1], blocks, width).transpose(0, 2, 1, 3)
+    blob = blob.at[:, at : at + blocks * fc2[1]].set(cut.reshape(devices, -1, width))
+    at += blocks * fc2[1]
+    small = []
+    for value, (rows, columns) in ((gains_grad, gains), (biases_grad, biases), (fc1_grad, fc1_bias)):
+        small.append(value.reshape(rows, devices, columns).transpose(1, 0, 2).reshape(devices, -1))
+    small = jnp.concatenate(small, 1).astype(jnp.bfloat16)
+    small = jnp.pad(small, ((0, 0), (0, -small.shape[1] % width))).reshape(devices, -1, width)
+    return blob.at[:, at : at + small.shape[1]].set(small)
+
+
+def unpack_grads(blob, shapes):
+    width = blob.shape[1]
+    qkv, proj, fc1, fc2, gains, biases, fc1_bias = shapes
+    blob = blob.astype(jnp.float32)
+    at = 0
+    parts = []
+    for columns in (qkv[1], proj[1], fc1[1]):
+        parts.append(blob[at : at + columns].T)
+        at += columns
+    blocks = fc2[0] // width
+    cut = blob[at : at + blocks * fc2[1]].reshape(blocks, fc2[1], width)
+    parts.append(cut.transpose(0, 2, 1).reshape(fc2))
+    at += blocks * fc2[1]
+    small = blob[at:].reshape(-1)
+    start = 0
+    for rows, columns in (gains, biases, fc1_bias):
+        parts.append(small[start : start + rows * columns].reshape(rows, columns))
+        start += rows * columns
+    return tuple(parts)
+
+
+def on_device(images, counts, cotangent, *weights):
     slots, seq_len, width = images.shape
     heads = width // HEAD_DIM
-    layer_count = w_qkv.shape[0]
+    layer_count = weights[0].shape[0]
+    shapes = [w.shape[1:] for w in weights]
     live = (jnp.arange(slots) < counts[0]).astype(jnp.float32)[:, None, None]
     state = images.astype(jnp.float32)
     kept_layers = []
     gathered_layers = []
     for layer_index in range(layer_count):
-        full_weights = (
-            lax.all_gather(w_qkv[layer_index], ("dp", "fsdp"), axis=1, tiled=True),
-            lax.all_gather(w_proj[layer_index], ("dp", "fsdp"), axis=1, tiled=True),
-            lax.all_gather(w_fc1[layer_index], ("dp", "fsdp"), axis=1, tiled=True),
-            lax.all_gather(w_fc2[layer_index], ("dp", "fsdp"), axis=1, tiled=True),
-            lax.all_gather(gains[layer_index], ("dp", "fsdp"), axis=1, tiled=True),
-            lax.all_gather(biases[layer_index], ("dp", "fsdp"), axis=1, tiled=True),
-            lax.all_gather(fc1_bias[layer_index], ("dp", "fsdp"), axis=1, tiled=True),
-        )
-        state, kept = layer_forward(state, full_weights, heads)
+        share = pack_layer(*(w[layer_index] for w in weights))
+        blob = lax.all_gather(share, AXES, axis=0, tiled=False)
+        gathered_layers.append(unpack_layer(blob, shapes))
+    for layer_index in range(layer_count):
+        state, kept = layer_forward(state, gathered_layers[layer_index], heads)
         kept_layers.append(kept)
-        gathered_layers.append(full_weights)
     block_output = (state * live).astype(jnp.bfloat16)
     grad_state = (cotangent.astype(jnp.float32) * live).reshape(-1, width)
     layer_grads = [None] * layer_count
     for layer_index in reversed(range(layer_count)):
-        full_weights = (
-            lax.all_gather(w_qkv[layer_index], ("dp", "fsdp"), axis=1, tiled=True),
-            lax.all_gather(w_proj[layer_index], ("dp", "fsdp"), axis=1, tiled=True),
-            lax.all_gather(w_fc1[layer_index], ("dp", "fsdp"), axis=1, tiled=True),
-            lax.all_gather(w_fc2[layer_index], ("dp", "fsdp"), axis=1, tiled=True),
-            lax.all_gather(gains[layer_index], ("dp", "fsdp"), axis=1, tiled=True),
-            lax.all_gather(biases[layer_index], ("dp", "fsdp"), axis=1, tiled=True),
-            lax.all_gather(fc1_bias[layer_index], ("dp", "fsdp"), axis=1, tiled=True),
+        grad_state, grads = layer_backward(
+            grad_state, kept_layers[layer_index], gathered_layers[layer_index]
         )
-        grad_state, grads = layer_backward(grad_state, kept_layers[layer_index], full_weights)
-        grad_qkv, grad_proj, grad_fc1, grad_fc2, gains_grad, biases_grad, fc1_grad = grads
-        layer_grads[layer_index] = (
-            lax.psum_scatter(grad_qkv, ("dp", "fsdp"), scatter_dimension=1, tiled=True),
-            lax.psum_scatter(grad_proj, ("dp", "fsdp"), scatter_dimension=1, tiled=True),
-            lax.psum_scatter(grad_fc1, ("dp", "fsdp"), scatter_dimension=1, tiled=True),
-            lax.psum_scatter(grad_fc2, ("dp", "fsdp"), scatter_dimension=1, tiled=True),
-            lax.psum_scatter(gains_grad, ("dp", "fsdp"), scatter_dimension=1, tiled=True),
-            lax.psum_scatter(biases_grad, ("dp", "fsdp"), scatter_dimension=1, tiled=True),
-            lax.psum_scatter(fc1_grad, ("dp", "fsdp"), scatter_dimension=1, tiled=True),
-        )
+        packed = pack_grads(grads, shapes, share.shape[0], blob.shape[0])
+        summed = lax.psum_scatter(packed, AXES, scatter_dimension=0, tiled=False)
+        layer_grads[layer_index] = unpack_grads(summed, shapes)
     stacked = tuple((jnp.stack([entry[member] for entry in layer_grads]) for member in range(7)))
-    grad_images = grad_state.reshape(images.shape)
-    return (
-        block_output,
-        grad_images,
-        stacked[0],
-        stacked[1],
-        stacked[2],
-        stacked[3],
-        stacked[4],
-        stacked[5],
-        stacked[6],
-    )
+    return (block_output, grad_state.reshape(images.shape), *stacked)
 
 
 def solution(mesh):

time: 1840 us -> 1070 us (0.58)
  waiting for transfers between devices: 1050 us -> 464 us
  blocking collectives: 243 us -> 0 us
  local copies, waits for them, and re-layouts: 184 us -> 280 us
  matrix products: 274 us -> 227 us
    reduce_scatter x8 -> x2, waiting for transfers between devices: 964 us -> 262 us  [on_device(): summed = lax.psum_scatter(packed, AXES, scatter_dimension=0, tiled=False)]
    all_gather x4 -> x0, blocking collectives: 160 us -> none  [the longest x2 82.3 us: on_device(): lax.all_gather(gains[layer_index], ('dp', 'fsdp'), axis=1, tiled=True)]
    all_gather x8 -> x2, waiting for transfers between devices: 81.9 us -> 202 us  [on_device(): blob = lax.all_gather(share, AXES, axis=0, tiled=False)]
    unnamed x2 -> x0, blocking collectives: 83 us -> none
    scatter x0 -> x10, local copies, waits for them, and re-layouts: none -> 34.6 us  [the longest x6 23.5 us: pack_grads(): blob.at[:, at:at + rows]]
    dot_general x8, matrix products: 94.6 us -> 65.7 us  [the longest x2 41.1 us: layer_backward(): grad_hidden = jnp.dot(branch_two, w_fc2, preferred_element_type=jnp.float32)]
    transpose x0 -> x11, local copies, waits for them, and re-layouts: none -> 19.7 us  [the longest x2 11.1 us: pack_grads(): grad_fc2.astype(jnp.bfloat16).reshape(devices, fc2[1], blocks, width)]
    reshape x5 -> x19, local copies, waits for them, and re-layouts: 18.3 us -> 37.5 us  [the longest x2 19.7 us: pack_grads(): grad_fc2.astype(jnp.bfloat16).reshape(devices, fc2[1], blocks, width)]
  transfers between devices with their start and end apart: 18 -> 4, of which waited for: 10 -> 4; matrix products, arithmetic and copies ran while one was open for 23% -> 8% of each run, Pallas kernels for 0% -> 0%
where the time goes in v1:
time: 1070 us
  waiting for transfers between devices  464 us (43%)
  local copies, waits for them, and re-layouts  280 us (26%)
  matrix products  227 us (21%)
  other arithmetic  77.5 us (7%)
  between operations  16.9 us (2%)
    reduce_scatter x2, waiting for transfers between devices, on_device(): summed = lax.psum_scatter(packed, AXES, scatter_dimension=0, tiled=False)  262 us
    all_gather x2, waiting for transfers between devices, on_device(): blob = lax.all_gather(share, AXES, axis=0, tiled=False)  202 us
    dot_general x8, matrix products, times_transposed(): lax.dot_general(left, right, (((1,), (1,)), ((), ())), preferred_element_...  62.4 us
    dot_general x8, matrix products, inner_rows(): lax.dot_general(left, right, (((0,), (0,)), ((), ())), preferred_element_...  48.9 us
    dot_general x2, matrix products, layer_backward(): grad_hidden = jnp.dot(branch_two, w_fc2, preferred_element_type=jnp.float32)  41.1 us
    unnamed x274, local copies, waits for them, and re-layouts  28.9 us
    reshape x4, local copies, waits for them, and re-layouts, layer_forward(): (mixed[:, :width] + biases[1]).astype(jnp.bfloat16).reshape(head_shape)  26.6 us
    scatter x6, local copies, waits for them, and re-layouts, pack_grads(): blob.at[:, at:at + rows]  23.5 us
  transfers between devices with their start and end apart: 4, of which 4 were waited for; matrix products, arithmetic and copies ran while one was open for 8% of the time, Pallas kernels for 0%

profile of v1, /device:TPU:0, one launch (start us, length us, event | category | flops | bytes accessed | tf_op | source)
XLA Modules:
  0.0 1065.8 jit_solution(16845095579974548114)
XLA Ops:
  29.2 95.0 %all-gather.5.cloned.1.call-done = bf16[9728,768]{1,0:T(8,128)(2,1)} async-done(((bf16[304,768]{1,0:T(8,128)(2,1)}), bf16[9728,768]{1,0:T(8,128)(2,1)}) %all-gather.5.cloned.1.call-update) | async-done | bytes 14942224 | tf_op jit(solution)/shard_map/all_gather | solution.py:253
  125.8 106.8 %all-gather.7.cloned.1.call-done = bf16[9728,768]{1,0:T(8,128)(2,1)} async-done(((bf16[304,768]{1,0:T(8,128)(2,1)}), bf16[9728,768]{1,0:T(8,128)(2,1)}) %all-gather.7.cloned.1.call-update) | async-done | bytes 14942224 | tf_op jit(solution)/shard_map/all_gather | solution.py:253
  242.9 8.0 fusion.100
  254.9 7.9 fusion.99
  295.3 15.6 %copy.321 = bf16[4,197,12,64]{1,3,2,0:T(8,128)(2,1)S(1)} copy(bf16[4,197,12,64]{3,2,1,0:T(8,128)(2,1)} %reshape.864) | data formatting | bytes 2420736 | tf_op jit(solution)/shard_map/reshape | solution.py:49
  346.5 29.0 %multiply_convert_fusion.3 = (bf16[788,3072]{1,0:T(8,128)(2,1)S(1)}, f32[788,3072]{1,0:T(8,128)}, f32[788,3072]{1,0:T(8,128)}) fusion(f32[3072]{0:T(1024)S(1)} %reshape.855, bf16[3072,768]{1,0:T(8,128)(2,1)} %bitcast.274, f32[788,768]{1,0:T(8,128)S(1)} %get-tuple-element.250, f32[768]{0:T(1024)S(1)} %add.290, f32[768]{0:T(1024)S(1)} %mul.363, ...), kind=kOutput, calls=%fused_computation.29 | convolution fusion | flops 3881044992 | bytes 31371424 | tf_op jit(solution)/shard_map/dot_general | solution.py:18
  428.3 7.4 fusion.93
  435.7 28.0 %fusion.96 = (bf16[3072]{0:T(1024)(128)(2,1)}, bf16[788,3072]{1,0:T(8,128)(2,1)S(1)}, f32[788,3072]{1,0:T(8,128)}) fusion(f32[788,3072]{1,0:T(8,128)S(1)} %fusion.93, f32[3072]{0:T(1024)S(1)} %copy-done.56, bf16[788,768]{1,0:T(8,128)(2,1)S(1)} %copy-done.48, bf16[768,3072]{1,0:T(8,128)(2,1)S(1)} %bitcast.272), kind=kOutput, calls=%fused_computation.262 | convolution fusion | flops 3897381888 | bytes 30154752 | tf_op jit(solution)/shard_map/dot_general | solution.py:101
  470.0 11.4 %multiply_convert_fusion.2 = bf16[788,3072]{1,0:T(8,128)(2,1)} fusion(f32[788,3072]{1,0:T(8,128)} %get-tuple-element.202, f32[788,3072]{1,0:T(8,128)} %copy-done.29, f32[3072]{0:T(1024)S(1)} %copy-done.56), kind=kLoop, calls=%fused_computation.16 | loop fusion | flops 9682944 | bytes 24219648 | tf_op jit(solution)/shard_map/convert_element_type | solution.py:71
  481.4 9.2 add_add_fusion
  519.6 7.6 multiply_reduce_fusion.1
  527.3 11.7 %multiply_convert_fusion.1 = bf16[4,12,197,197]{2,3,1,0:T(8,128)(2,1)} fusion(f32[4,12,197,197]{2,3,1,0:T(8,128)} %get-tuple-element.260, f32[4,12,197,197]{2,3,1,0:T(8,128)} %copy-done.1, f32[4,12,197]{2,1,0:T(8,128)S(1)} %get-tuple-element.259, f32[4,12,197]{2,1,0:T(8,128)S(1)} %copy-done.53), kind=kLoop, calls=%fused_computation.5 | loop fusion | flops 9314160 | bytes 18703968 | tf_op jit(solution)/shard_map/convert_element_type | solution.py:128
  567.4 7.2 convolution_convert_fusion.3
  574.6 13.1 %fusion.111 = (bf16[3072]{0:T(1024)(128)(2,1)S(1)}, bf16[788,3072]{1,0:T(8,128)(2,1)}) fusion(f32[788,3072]{1,0:T(8,128)} %get-tuple-element.204, bf16[768,3072]{1,0:T(8,128)(2,1)S(1)} %bitcast.267, f32[788,768]{1,0:T(8,128)S(1)} %get-tuple-element.193, f32[788,3072]{1,0:T(8,128)} %get-tuple-element.251, f32[3072]{0:T(1024)S(1)} %copy-done.84), kind=kOutput, calls=%fused_computation.275 | convolution fusion | flops 3757584384 | bytes 31365120 | tf_op jit(solution)/shard_map/dot_general | solution.py:101
  587.8 7.0 multiply_reduce_fusion.6
  594.8 7.7 convolution_convert_fusion.4
  621.1 7.4 multiply_reduce_fusion
  628.5 11.7 %multiply_convert_fusion = bf16[4,12,197,197]{2,3,1,0:T(8,128)(2,1)} fusion(f32[4,12,197,197]{2,3,1,0:T(8,128)} %get-tuple-element.264, f32[4,12,197,197]{2,3,1,0:T(8,128)} %copy-done, f32[4,12,197]{2,1,0:T(8,128)S(1)} %get-tuple-element.263, f32[4,12,197]{2,1,0:T(8,128)S(1)} %copy-done.52), kind=kLoop, calls=%fused_computation.2 | loop fusion | flops 9314160 | bytes 18703968 | tf_op jit(solution)/shard_map/convert_element_type | solution.py:128
  674.6 9.8 reshape.838
  717.1 9.9 convolution_convert_fusion
  727.0 9.9 reshape.846
  743.7 7.7 convolution_convert_fusion.2
  785.9 92.4 %reduce-scatter.3.cloned.1.call-done = bf16[1,304,768]{2,1,0:T(8,128)(2,1)} async-done(((bf16[32,304,768]{2,1,0:T(8,128)(2,1)}), bf16[1,304,768]{2,1,0:T(8,128)(2,1)}) %reduce-scatter.3.cloned.1.call-update) | async-done | bytes 466960 | tf_op jit(solution)/shard_map/reduce_scatter | solution.py:266
  880.8 170.0 %reduce-scatter.5.cloned.1.call-done = bf16[1,304,768]{2,1,0:T(8,128)(2,1)} async-done(((bf16[32,304,768]{2,1,0:T(8,128)(2,1)}), bf16[1,304,768]{2,1,0:T(8,128)(2,1)}) %reduce-scatter.5.cloned.1.call-update) | async-done | bytes 466960 | tf_op jit(solution)/shard_map/reduce_scatter | solution.py:266
  (554 shorter events, 357.7 us)
Async XLA Ops:
  7.2 117.0 %all-gather.5.cloned.1.call-start = ((), (), s32[]{:S(2)}) async-start(), calls=%async_computation.4 | async-start | bytes 15409152 | tf_op jit(solution)/shard_map/all_gather | solution.py:253
  14.7 217.9 %all-gather.7.cloned.1.call-start = ((), (), s32[]{:S(2)}) async-start(), calls=%async_computation.5 | async-start | bytes 15409152 | tf_op jit(solution)/shard_map/all_gather | solution.py:253
  15.7 862.6 %reduce-scatter.3.cloned.1.call-start = ((), (), s32[]{:S(2)}) async-start(), calls=%async_computation.2 | async-start | bytes 15409152 | tf_op jit(solution)/shard_map/reduce_scatter | solution.py:266
  262.9 83.6 %copy-start.83 = (f32[3072]{0:T(1024)}, f32[3072]{0:T(1024)S(1)}, u32[]{:S(2)}) copy-start(f32[3072]{0:T(1024)S(1)} %reshape.855) | copy-start | bytes 36868
  263.1 83.3 %copy-start.69 = (f32[768]{0:T(1024)}, f32[768]{0:T(1024)S(1)}, u32[]{:S(2)}) copy-start(f32[768]{0:T(1024)S(1)} %mul.363) | copy-start | bytes 9220
  263.8 82.7 %copy-start.92 = (f32[768]{0:T(1024)}, f32[768]{0:T(1024)S(1)}, u32[]{:S(2)}) copy-start(f32[768]{0:T(1024)S(1)} %add.290) | copy-start | bytes 9220
  310.9 17.4 %copy-start.5 = (bf16[4,197,12,64]{1,3,2,0:T(8,128)(2,1)}, bf16[4,197,12,64]{1,3,2,0:T(8,128)(2,1)S(1)}, u32[]{:S(2)}) copy-start(bf16[4,197,12,64]{1,3,2,0:T(8,128)(2,1)S(1)} %copy.321) | copy-start | bytes 3631108
  342.7 32.8 %slice-start.6 = ((s8[4718592]{0:T(1024)(128)(4,1)}), s8[4194304]{0:T(1024)(128)(4,1)S(1)}, s32[]{:S(2)}) async-start(s8[4718592]{0:T(1024)(128)(4,1)} %bitcast.262), calls=%async_computation.12 | async-start | bytes 8388608
  345.9 29.6 %copy-start.27 = (f32[788,768]{1,0:T(8,128)}, f32[788,768]{1,0:T(8,128)S(1)}, u32[]{:S(2)}) copy-start(f32[788,768]{1,0:T(8,128)S(1)} %get-tuple-element.250) | copy-start | bytes 7262212
  345.9 29.5 %copy-start.61 = (f32[788]{0:T(1024)}, f32[788]{0:T(1024)S(1)}, u32[]{:S(2)}) copy-start(f32[788]{0:T(1024)S(1)} %broadcast_multiply_fusion.11) | copy-start | bytes 9460
  346.4 29.1 %copy-start.77 = (f32[788]{0:T(1024)}, f32[788]{0:T(1024)S(1)}, u32[]{:S(2)}) copy-start(f32[788]{0:T(1024)S(1)} %add_rsqrt_fusion.3) | copy-start | bytes 9460
  346.5 29.1 %slice-start.7 = ((s8[4718592]{0:T(1024)(128)(4,1)}), s8[524288]{0:T(1024)(128)(4,1)S(1)}, s32[]{:S(2)}) async-start(s8[4718592]{0:T(1024)(128)(4,1)} %bitcast.262), calls=%async_computation.13 | async-start | bytes 1048576
  392.7 17.5 %copy-start.9 = (bf16[4,197,12,64]{1,3,2,0:T(8,128)(2,1)}, bf16[4,197,12,64]{1,3,2,0:T(8,128)(2,1)S(1)}, u32[]{:S(2)}) copy-start(bf16[4,197,12,64]{1,3,2,0:T(8,128)(2,1)S(1)} %copy.341) | copy-start | bytes 3631108
  427.7 36.0 %copy-start.23 = (f32[788,768]{1,0:T(8,128)}, f32[788,768]{1,0:T(8,128)S(1)}, u32[]{:S(2)}) copy-start(f32[788,768]{1,0:T(8,128)S(1)} %get-tuple-element.257) | copy-start | bytes 7262212
  427.7 72.1 %copy-start.59 = (f32[788]{0:T(1024)}, f32[788]{0:T(1024)S(1)}, u32[]{:S(2)}) copy-start(f32[788]{0:T(1024)S(1)} %broadcast_multiply_fusion.9) | copy-start | bytes 9460
  428.2 71.6 %copy-start.75 = (f32[788]{0:T(1024)}, f32[788]{0:T(1024)S(1)}, u32[]{:S(2)}) copy-start(f32[788]{0:T(1024)S(1)} %add_rsqrt_fusion.1) | copy-start | bytes 9460
  428.2 35.5 %slice-start.14 = ((s8[4718592]{0:T(1024)(128)(4,1)}), s8[4194304]{0:T(1024)(128)(4,1)S(1)}, s32[]{:S(2)}) async-start(s8[4718592]{0:T(1024)(128)(4,1)} %bitcast.279), calls=%async_computation.20 | async-start | bytes 8388608
  435.6 28.1 %copy-start.29 = (f32[788,3072]{1,0:T(8,128)}, f32[788,3072]{1,0:T(8,128)S(1)}, u32[]{:S(2)}) copy-start(f32[788,3072]{1,0:T(8,128)S(1)} %fusion.93) | copy-start | bytes 29048836
  435.7 28.0 %slice-start.15 = ((s8[4718592]{0:T(1024)(128)(4,1)}), s8[524288]{0:T(1024)(128)(4,1)S(1)}, s32[]{:S(2)}) async-start(s8[4718592]{0:T(1024)(128)(4,1)} %bitcast.279), calls=%async_computation.21 | async-start | bytes 1048576
  567.4 20.3 %slice-start.12 = ((s8[4718592]{0:T(1024)(128)(4,1)}), s8[4194304]{0:T(1024)(128)(4,1)S(1)}, s32[]{:S(2)}) async-start(s8[4718592]{0:T(1024)(128)(4,1)} %bitcast.275), calls=%async_computation.18 | async-start | bytes 8388608
  574.6 13.1 %copy-start.28 = (f32[788,768]{1,0:T(8,128)S(1)}, f32[788,768]{1,0:T(8,128)}, u32[]{:S(2)}) copy-start(f32[788,768]{1,0:T(8,128)} %copy-done.27) | copy-start | bytes 7262212
  713.2 337.6 %reduce-scatter.5.cloned.1.call-start = ((), (), s32[]{:S(2)}) async-start(), calls=%async_computation.3 | async-start | bytes 15409152 | tf_op jit(solution)/shard_map/reduce_scatter | solution.py:266
  743.7 17.1 %slice-start.18 = ((s8[4866048]{0:T(1024)(128)(4,1)}), s8[4194304]{0:T(1024)(128)(4,1)S(1)}, s32[]{:S(2)}) async-start(s8[4866048]{0:T(1024)(128)(4,1)} %bitcast.322), calls=%async_computation.24 | async-start | bytes 8388608
  878.3 175.2 %copy-start.44 = (bf16[1,304,768]{2,1,0:T(8,128)(2,1)S(1)}, bf16[1,304,768]{2,1,0:T(8,128)(2,1)}, u32[]{:S(2)}) copy-start(bf16[1,304,768]{2,1,0:T(8,128)(2,1)} %reduce-scatter.3.cloned.1.call-done) | copy-start | bytes 1400836
  (103 other events, 576.4 us)
Sparse Core Ops, SparseCore 0:
  14.8 109.3 all-gather.4
  127.8 104.7 all-gather.6
  713.3 164.8 reduce-scatter.2
  885.3 165.4 reduce-scatter.4

commit v2 on v1

v2 whole, which is shorter than its diff:
```python
import math
from functools import partial

import jax
import jax.numpy as jnp
from jax import lax
from jax.experimental import pallas as pl
from jax.experimental.pallas import tpu as pltpu
from jax.sharding import PartitionSpec as P

HEAD_DIM = 64
MATMUL_NT = (((1,), (1,)), ((), ()))
MATMUL_NN = (((1,), (0,)), ((), ()))
MATMUL_TN = (((0,), (0,)), ((), ()))
VMEM_BYTES = 60 * 1024 * 1024
TILE_ROWS = 16
LANES = 128
MASKED = -1e30


def dot(left, right, dims):
    return lax.dot_general(left, right, dims, preferred_element_type=jnp.float32)


def norm_parts(token_rows):
    row_mean = jnp.mean(token_rows, -1, keepdims=True)
    centered = token_rows - row_mean
    inv_std = lax.rsqrt(jnp.mean(centered * centered, -1, keepdims=True) + 1e-06)
    return (centered * inv_std, inv_std)


def norm_back(grad_normed, scaled, inv_std, gain_row):
    grad_scaled = grad_normed * gain_row
    return inv_std * (
        grad_scaled
        - jnp.mean(grad_scaled, -1, keepdims=True)
        - scaled * jnp.mean(grad_scaled * scaled, -1, keepdims=True)
    )


def column_sums(rows):
    return jnp.sum(rows.astype(jnp.float32), 0, keepdims=True)


def side_of(pair, side):
    lane = lax.broadcasted_iota(jnp.int32, pair.shape, 1)
    mine = (lane >= HEAD_DIM) if side else (lane < HEAD_DIM)
    return jnp.where(mine, pair, jnp.zeros_like(pair))


def attn_forward_kernel(seq_len, x_ref, w_qkv_ref, w_proj_ref, gains_ref, biases_ref,
                        normed_ref, mixed_ref, probs_ref, attended_ref, middle_ref):
    width = x_ref.shape[2]
    token_rows = x_ref[0]
    scaled, _ = norm_parts(token_rows)
    normed = (scaled * gains_ref[0:1] + biases_ref[0:1]).astype(jnp.bfloat16)
    normed_ref[0] = normed
    for part in range(3):
        columns = slice(part * width, (part + 1) * width)
        mixed = dot(normed, w_qkv_ref[columns, :], MATMUL_NT)
        if part == 0:
            mixed = mixed + biases_ref[1:2]
        if part == 2:
            mixed = mixed + biases_ref[2:3]
        mixed = mixed.astype(jnp.bfloat16)
        if part == 0:
            mixed = mixed * jnp.bfloat16(HEAD_DIM ** (-0.5))
        mixed_ref[0, :, columns] = mixed
    padded = x_ref.shape[1]
    real_key = lax.broadcasted_iota(jnp.int32, (padded, padded), 1) < seq_len
    for pair in range(width // LANES):
        at = pair * LANES
        query = mixed_ref[0, :, at : at + LANES]
        key = mixed_ref[0, :, width + at : width + at + LANES]
        value = mixed_ref[0, :, 2 * width + at : 2 * width + at + LANES]
        total = None
        for side in range(2):
            scores = dot(side_of(query, side), key, MATMUL_NT)
            scores = jnp.where(real_key, scores, MASKED)
            top = jnp.max(scores, -1, keepdims=True)
            expo = jnp.exp(scores - top)
            probs = (expo / jnp.sum(expo, -1, keepdims=True)).astype(jnp.bfloat16)
            probs_ref[0, 2 * pair + side] = probs
            part = dot(probs, side_of(value, side), MATMUL_NN)
            total = part if total is None else total + part
        attended_ref[0, :, at : at + LANES] = total.astype(jnp.bfloat16)
    middle_ref[0] = (
        token_rows + dot(attended_ref[0], w_proj_ref[...], MATMUL_NT) + biases_ref[3:4]
    )


def whole(shape):
    return pl.BlockSpec(shape, lambda i: (0,) * len(shape))


def slot_block(shape):
    return pl.BlockSpec((1, *shape[1:]), lambda i: (i,) + (0,) * (len(shape) - 1))


def worth(microseconds):
    return pl.CostEstimate(
        flops=int(microseconds * 1e9), bytes_accessed=1 << 20, transcendentals=0
    )


def params():
    return pltpu.CompilerParams(
        dimension_semantics=("arbitrary",), vmem_limit_bytes=VMEM_BYTES
    )


def attn_forward(state, w_qkv, w_proj, gains, biases, seq_len):
    slots, padded, width = state.shape
    heads = width // HEAD_DIM
    outs = [
        jax.ShapeDtypeStruct((slots, padded, width), jnp.bfloat16),
        jax.ShapeDtypeStruct((slots, padded, 3 * width), jnp.bfloat16),
        jax.ShapeDtypeStruct((slots, heads, padded, padded), jnp.bfloat16),
        jax.ShapeDtypeStruct((slots, padded, width), jnp.bfloat16),
        jax.ShapeDtypeStruct((slots, padded, width), jnp.float32),
    ]
    return pl.pallas_call(
        partial(attn_forward_kernel, seq_len),
        grid=(slots,),
        in_specs=[slot_block(state.shape)]
        + [whole(v.shape) for v in (w_qkv, w_proj, gains, biases)],
        out_specs=[slot_block(o.shape) for o in outs],
        out_shape=outs,
        compiler_params=params(),
        cost_estimate=worth(18),
        name="attn_forward",
    )(state, w_qkv, w_proj, gains, biases)


def mlp_forward_kernel(middle_ref, w_fc1_ref, w_fc2_ref, gains_ref, biases_ref, fc1_bias_ref,
                       normed_ref, hidden_ref, slope_ref, final_ref):
    block = pl.program_id(0)
    slots = middle_ref.shape[0]

    @pl.when(block == 0)
    def _():
        def first(slot, carry):
            middle = middle_ref[slot]
            scaled, _ = norm_parts(middle)
            normed_ref[slot] = (scaled * gains_ref[1:2] + biases_ref[4:5]).astype(jnp.bfloat16)
            final_ref[slot] = middle + biases_ref[5:6]
            return carry

        lax.fori_loop(0, slots, first, 0)

    def rows(slot, carry):
        pre = dot(normed_ref[slot], w_fc1_ref[...], MATMUL_NT) + fc1_bias_ref[0]
        below = 0.5 * (1.0 + lax.erf(pre * 0.5**0.5))
        hidden = (pre * below).astype(jnp.bfloat16)
        bell = jnp.exp(-0.5 * (pre * pre)) * (2.0 * math.pi) ** -0.5
        slope_ref[slot] = (below + pre * bell).astype(jnp.bfloat16)
        hidden_ref[slot] = hidden
        final_ref[slot] += dot(hidden, w_fc2_ref[0], MATMUL_NT)
        return carry

    lax.fori_loop(0, slots, rows, 0)


def mlp_forward(middle, w_fc1, w_fc2, gains, biases, fc1_bias):
    slots, padded, width = middle.shape
    blocks = w_fc2.shape[0]
    wide = (slots, padded, blocks * width)
    outs = [
        jax.ShapeDtypeStruct(middle.shape, jnp.bfloat16),
        jax.ShapeDtypeStruct(wide, jnp.bfloat16),
        jax.ShapeDtypeStruct(wide, jnp.bfloat16),
        jax.ShapeDtypeStruct(middle.shape, jnp.float32),
    ]
    wide_spec = pl.BlockSpec((slots, padded, width), lambda i: (0, 0, i))
    return pl.pallas_call(
        mlp_forward_kernel,
        grid=(blocks,),
        in_specs=[
            whole(middle.shape),
            pl.BlockSpec((width, width), lambda i: (i, 0)),
            pl.BlockSpec((1, width, width), lambda i: (i, 0, 0)),
            whole(gains.shape),
            whole(biases.shape),
            pl.BlockSpec((1, 1, width), lambda i: (i, 0, 0)),
        ],
        out_specs=[whole(middle.shape), wide_spec, wide_spec, whole(middle.shape)],
        out_shape=outs,
        compiler_params=params(),
        cost_estimate=worth(24),
        name="mlp_forward",
    )(middle, w_fc1, w_fc2, gains, biases, fc1_bias)


def mlp_backward_kernel(grad_ref, middle_ref, normed_ref, hidden_ref, slope_ref, w_fc1_ref,
                        w_fc2_ref, gains_ref,
                        grad_fc1_ref, grad_fc2_ref, fc1_sums_ref, sums_ref, out_ref,
                        branch_ref, pre_ref, total_ref):
    block = pl.program_id(0)
    slots, padded, width = grad_ref.shape

    @pl.when(block == 0)
    def _():
        sums_ref[...] = jnp.zeros_like(sums_ref)

        def first(slot, carry):
            branch = grad_ref[slot].astype(jnp.bfloat16)
            branch_ref[pl.ds(pl.multiple_of(slot * padded, TILE_ROWS), padded), :] = branch
            sums_ref[2:3] += column_sums(branch)
            return carry

        lax.fori_loop(0, slots, first, 0)

    fc1_sums_ref[...] = jnp.zeros_like(fc1_sums_ref)

    def rows(slot, carry):
        here = pl.ds(pl.multiple_of(slot * padded, TILE_ROWS), padded)
        grad_hidden = dot(branch_ref[here, :], w_fc2_ref[0], MATMUL_NN)
        grad_pre = (grad_hidden * slope_ref[slot].astype(jnp.float32)).astype(jnp.bfloat16)
        pre_ref[here, :] = grad_pre
        fc1_sums_ref[0, 0:1] += column_sums(grad_pre)
        part = dot(grad_pre, w_fc1_ref[...], MATMUL_NN)

        @pl.when(block == 0)
        def _():
            total_ref[slot] = part

        @pl.when(block != 0)
        def _():
            total_ref[slot] += part

        return carry

    lax.fori_loop(0, slots, rows, 0)
    step = 2 * LANES
    hidden = hidden_ref[...].reshape(slots * padded, width)
    normed = normed_ref[...].reshape(slots * padded, width)
    for at in range(0, width, step):
        grad_fc2_ref[0, at : at + step, :] = dot(
            branch_ref[:, at : at + step], hidden, MATMUL_TN
        ).astype(jnp.bfloat16)
        grad_fc1_ref[at : at + step, :] = dot(
            pre_ref[:, at : at + step], normed, MATMUL_TN
        ).astype(jnp.bfloat16)

    @pl.when(block == pl.num_programs(0) - 1)
    def _():
        def last(slot, carry):
            grad_normed = total_ref[slot]
            scaled, inv_std = norm_parts(middle_ref[slot])
            sums_ref[0:1] += column_sums(grad_normed * scaled)
            sums_ref[1:2] += column_sums(grad_normed)
            out_ref[slot] = grad_ref[slot] + norm_back(
                grad_normed, scaled, inv_std, gains_ref[1:2]
            )
            return carry

        lax.fori_loop(0, slots, last, 0)


def mlp_backward(grad, middle, normed, hidden, slope, w_fc1, w_fc2, gains):
    slots, padded, width = grad.shape
    blocks = w_fc2.shape[0]
    outs = [
        jax.ShapeDtypeStruct(w_fc1.shape, jnp.bfloat16),
        jax.ShapeDtypeStruct(w_fc2.shape, jnp.bfloat16),
        jax.ShapeDtypeStruct((blocks, 8, width), jnp.float32),
        jax.ShapeDtypeStruct((8, width), jnp.float32),
        jax.ShapeDtypeStruct(grad.shape, jnp.float32),
    ]
    wide_spec = pl.BlockSpec((slots, padded, width), lambda i: (0, 0, i))
    fc1_spec = pl.BlockSpec((width, width), lambda i: (i, 0))
    fc2_spec = pl.BlockSpec((1, width, width), lambda i: (i, 0, 0))
    return pl.pallas_call(
        mlp_backward_kernel,
        grid=(blocks,),
        in_specs=[whole(grad.shape), whole(grad.shape), whole(grad.shape)]
        + [wide_spec, wide_spec, fc1_spec, fc2_spec, whole(gains.shape)],
        out_specs=[
            fc1_spec,
            fc2_spec,
            pl.BlockSpec((1, 8, width), lambda i: (i, 0, 0)),
            whole((8, width)),
            whole(grad.shape),
        ],
        out_shape=outs,
        scratch_shapes=[
            pltpu.VMEM((slots * padded, width), jnp.bfloat16),
            pltpu.VMEM((slots * padded, width), jnp.bfloat16),
            pltpu.VMEM(grad.shape, jnp.float32),
        ],
        compiler_params=params(),
        cost_estimate=worth(34),
        name="mlp_backward",
    )(grad, middle, normed, hidden, slope, w_fc1, w_fc2, gains)


def attn_backward_kernel(grad_ref, x_ref, normed_ref, mixed_ref, probs_ref, attended_ref,
                         w_qkv_ref, w_proj_ref, gains_ref,
                         grad_qkv_ref, grad_proj_ref, sums_ref, out_ref,
                         mixed_all, normed_all, attended_all, branch_all):
    slot = pl.program_id(0)
    _, padded, width = grad_ref.shape
    here = pl.ds(pl.multiple_of(slot * padded, TILE_ROWS), padded)

    @pl.when(slot == 0)
    def _():
        sums_ref[...] = jnp.zeros_like(sums_ref)

    branch = grad_ref[0].astype(jnp.bfloat16)
    branch_all[here, :] = branch
    normed_all[here, :] = normed_ref[0]
    attended_all[here, :] = attended_ref[0]
    grad_attended = dot(branch, w_proj_ref[...], MATMUL_NN).astype(jnp.bfloat16)
    for pair in range(width // LANES):
        at = pair * LANES
        query = mixed_ref[0, :, at : at + LANES]
        key = mixed_ref[0, :, width + at : width + at + LANES]
        value = mixed_ref[0, :, 2 * width + at : 2 * width + at + LANES]
        grad_pair = grad_attended[:, at : at + LANES]
        grad_query = grad_key = grad_value = 0.0
        for side in range(2):
            probs = probs_ref[0, 2 * pair + side]
            wide_probs = probs.astype(jnp.float32)
            grad_side = side_of(grad_pair, side)
            grad_value += dot(probs, grad_side, MATMUL_TN)
            grad_probs = dot(grad_side, value, MATMUL_NT)
            row_inner = jnp.sum(grad_probs * wide_probs, -1, keepdims=True)
            grad_scores = (wide_probs * (grad_probs - row_inner)).astype(jnp.bfloat16)
            grad_query += dot(grad_scores, side_of(key, side), MATMUL_NN)
            grad_key += dot(grad_scores, side_of(query, side), MATMUL_TN)
        grad_query = (grad_query * HEAD_DIM ** (-0.5)).astype(jnp.bfloat16)
        mixed_all[here, at : at + LANES] = grad_query
        mixed_all[here, width + at : width + at + LANES] = grad_key.astype(jnp.bfloat16)
        mixed_all[here, 2 * width + at : 2 * width + at + LANES] = grad_value.astype(jnp.bfloat16)
    grad_mixed = mixed_all[here, :]
    sums_ref[2:3] += column_sums(grad_mixed[:, :width])
    sums_ref[3:4] += column_sums(grad_mixed[:, 2 * width :])
    sums_ref[4:5] += column_sums(branch)
    grad_normed = dot(grad_mixed, w_qkv_ref[...], MATMUL_NN)
    scaled, inv_std = norm_parts(x_ref[0])
    sums_ref[0:1] += column_sums(grad_normed * scaled)
    sums_ref[1:2] += column_sums(grad_normed)
    out_ref[0] = grad_ref[0] + norm_back(grad_normed, scaled, inv_std, gains_ref[0:1])

    @pl.when(slot == pl.num_programs(0) - 1)
    def _():
        step = 2 * LANES
        for at in range(0, 3 * width, step):
            grad_qkv_ref[at : at + step, :] = dot(
                mixed_all[:, at : at + step], normed_all[...], MATMUL_TN
            ).astype(jnp.bfloat16)
        for at in range(0, width, step):
            grad_proj_ref[at : at + step, :] = dot(
                branch_all[:, at : at + step], attended_all[...], MATMUL_TN
            ).astype(jnp.bfloat16)


def attn_backward(grad, state, normed, mixed, probs, attended, w_qkv, w_proj, gains):
    slots, padded, width = grad.shape
    outs = [
        jax.ShapeDtypeStruct(w_qkv.shape, jnp.bfloat16),
        jax.ShapeDtypeStruct(w_proj.shape, jnp.bfloat16),
        jax.ShapeDtypeStruct((8, width), jnp.float32),
        jax.ShapeDtypeStruct(grad.shape, jnp.float32),
    ]
    sliced = (grad, state, normed, mixed, probs, attended)
    return pl.pallas_call(
        attn_backward_kernel,
        grid=(slots,),
        in_specs=[slot_block(v.shape) for v in sliced]
        + [whole(v.shape) for v in (w_qkv, w_proj, gains)],
        out_specs=[whole(o.shape) for o in outs[:3]] + [slot_block(grad.shape)],
        out_shape=outs,
        scratch_shapes=[
            pltpu.VMEM((slots * padded, 3 * width), jnp.bfloat16),
            pltpu.VMEM((slots * padded, width), jnp.bfloat16),
            pltpu.VMEM((slots * padded, width), jnp.bfloat16),
            pltpu.VMEM((slots * padded, width), jnp.bfloat16),
        ],
        compiler_params=params(),
        cost_estimate=worth(29),
        name="attn_backward",
    )(*sliced, w_qkv, w_proj, gains)


AXES = ("dp", "fsdp")


def pack_layer(w_qkv, w_proj, w_fc1, w_fc2, gains, biases, fc1_bias):
    width, tall = w_qkv.shape[0], w_fc2.shape[0]
    cut = w_fc2.T.reshape(w_fc2.shape[1], tall // width, width).transpose(1, 0, 2)
    small = jnp.concatenate([gains.reshape(-1), biases.reshape(-1), fc1_bias.reshape(-1)])
    small = jnp.pad(small, (0, -small.size % width)).reshape(-1, width)
    small = jnp.pad(small, ((0, -small.shape[0] % 16), (0, 0)))
    return jnp.concatenate([w_qkv.T, w_proj.T, w_fc1.T, cut.reshape(-1, width), small], 0)


def unpack_layer(blob, shapes):
    devices, _, width = blob.shape
    qkv, proj, fc1, fc2, gains, biases, fc1_bias = shapes
    at = 0
    parts = []
    for columns in (qkv[1], proj[1], fc1[1]):
        parts.append(blob[:, at : at + columns].reshape(-1, width))
        at += columns
    blocks = fc2[0] // width
    cut = blob[:, at : at + blocks * fc2[1]].reshape(devices, blocks, fc2[1], width)
    parts.append(cut.transpose(1, 0, 2, 3).reshape(blocks, devices * fc2[1], width))
    at += blocks * fc2[1]
    small = blob[:, at:].reshape(devices, -1)
    start = 0
    for rows, columns in (gains, biases, fc1_bias):
        piece = small[:, start : start + rows * columns].reshape(devices, rows, columns)
        piece = piece.transpose(1, 0, 2).astype(jnp.float32)
        parts.append(piece.reshape(rows, devices * columns))
        start += rows * columns
    parts[-1] = parts[-1].reshape(blocks, 1, width)
    return tuple(parts)


def pack_grads(grads, shapes, total_rows, devices):
    grad_qkv, grad_proj, grad_fc1, grad_fc2, gains_grad, biases_grad, fc1_grad = grads
    width = grad_qkv.shape[1]
    qkv, proj, fc1, fc2, gains, biases, fc1_bias = shapes
    blob = jnp.zeros((devices, total_rows, width), jnp.bfloat16)
    at = 0
    for value in (grad_qkv, grad_proj, grad_fc1):
        rows = value.shape[0] // devices
        blob = blob.at[:, at : at + rows].set(
            value.astype(jnp.bfloat16).reshape(devices, rows, width)
        )
        at += rows
    blocks = fc2[0] // width
    cut = grad_fc2.reshape(blocks, devices, fc2[1], width).transpose(1, 0, 2, 3)
    blob = blob.at[:, at : at + blocks * fc2[1]].set(cut.reshape(devices, -1, width))
    at += blocks * fc2[1]
    small = []
    for value, (rows, columns) in ((gains_grad, gains), (biases_grad, biases), (fc1_grad, fc1_bias)):
        small.append(value.reshape(rows, devices, columns).transpose(1, 0, 2).reshape(devices, -1))
    small = jnp.concatenate(small, 1).astype(jnp.bfloat16)
    small = jnp.pad(small, ((0, 0), (0, -small.shape[1] % width))).reshape(devices, -1, width)
    return blob.at[:, at : at + small.shape[1]].set(small)


def unpack_grads(blob, shapes):
    width = blob.shape[1]
    qkv, proj, fc1, fc2, gains, biases, fc1_bias = shapes
    blob = blob.astype(jnp.float32)
    at = 0
    parts = []
    for columns in (qkv[1], proj[1], fc1[1]):
        parts.append(blob[at : at + columns].T)
        at += columns
    blocks = fc2[0] // width
    cut = blob[at : at + blocks * fc2[1]].reshape(blocks, fc2[1], width)
    parts.append(cut.transpose(0, 2, 1).reshape(fc2))
    at += blocks * fc2[1]
    small = blob[at:].reshape(-1)
    start = 0
    for rows, columns in (gains, biases, fc1_bias):
        parts.append(small[start : start + rows * columns].reshape(rows, columns))
        start += rows * columns
    return tuple(parts)


def on_device(images, counts, cotangent, *weights):
    slots, seq_len, width = images.shape
    layer_count = weights[0].shape[0]
    shapes = [w.shape[1:] for w in weights]
    live = (jnp.arange(slots) < counts[0]).astype(jnp.float32)[:, None, None]
    extra = ((0, 0), (0, -seq_len % TILE_ROWS), (0, 0))
    state = jnp.pad(images.astype(jnp.float32), extra)
    gathered = []
    for layer_index in range(layer_count):
        share = pack_layer(*(w[layer_index] for w in weights))
        blob = lax.all_gather(share, AXES, axis=0, tiled=False)
        gathered.append(blob)
    kept = []
    for layer_index in range(layer_count):
        blob, state = lax.optimization_barrier((gathered[layer_index], state))
        gathered[layer_index] = unpack_layer(blob, shapes)
        w_qkv, w_proj, w_fc1, w_fc2, gains, biases, fc1_bias = gathered[layer_index]
        normed_one, mixed, probs, attended, middle = attn_forward(
            state, w_qkv, w_proj, gains, biases, seq_len
        )
        normed_two, hidden, slope, final = mlp_forward(
            middle, w_fc1, w_fc2, gains, biases, fc1_bias
        )
        kept.append((state, normed_one, mixed, probs, attended, middle, normed_two, hidden, slope))
        state = final
    block_output = (state[:, :seq_len] * live).astype(jnp.bfloat16)
    grad_state = jnp.pad(cotangent.astype(jnp.float32) * live, extra)
    layer_grads = [None] * layer_count
    for layer_index in reversed(range(layer_count)):
        w_qkv, w_proj, w_fc1, w_fc2, gains, biases, fc1_bias = gathered[layer_index]
        entry, normed_one, mixed, probs, attended, middle, normed_two, hidden, slope = kept[
            layer_index
        ]
        grad_fc1, grad_fc2, fc1_sums, mlp_sums, grad_middle = mlp_backward(
            grad_state, middle, normed_two, hidden, slope, w_fc1, w_fc2, gains
        )
        grad_qkv, grad_proj, attn_sums, grad_state = attn_backward(
            grad_middle, entry, normed_one, mixed, probs, attended, w_qkv, w_proj, gains
        )
        gains_grad = jnp.stack([attn_sums[0], mlp_sums[0]])
        biases_grad = jnp.stack(
            [attn_sums[1], attn_sums[2], attn_sums[3], attn_sums[4], mlp_sums[1], mlp_sums[2]]
        )
        grads = (
            grad_qkv,
            grad_proj,
            grad_fc1,
            grad_fc2,
            gains_grad,
            biases_grad,
            fc1_sums[:, 0].reshape(1, -1),
        )
        packed = pack_grads(grads, shapes, share.shape[0], blob.shape[0])
        summed = lax.psum_scatter(packed, AXES, scatter_dimension=0, tiled=False)
        layer_grads[layer_index] = unpack_grads(summed, shapes)
    stacked = tuple((jnp.stack([entry[member] for entry in layer_grads]) for member in range(7)))
    return (block_output, grad_state[:, :seq_len], *stacked)


def solution(mesh):
    placed = (
        P(("dp", "fsdp"), None, None),
        P(("dp", "fsdp")),
        P(("dp", "fsdp"), None, None),
        P(None, None, ("dp", "fsdp")),
        P(None, None, ("dp", "fsdp")),
        P(None, None, ("dp", "fsdp")),
        P(None, None, ("dp", "fsdp")),
        P(None, None, ("dp", "fsdp")),
        P(None, None, ("dp", "fsdp")),
        P(None, None, ("dp", "fsdp")),
    )
    return jax.shard_map(
        on_device,
        mesh=mesh,
        in_specs=placed,
        out_specs=(
            P(("dp", "fsdp"), None, None),
            P(("dp", "fsdp"), None, None),
            P(None, None, ("dp", "fsdp")),
            P(None, None, ("dp", "fsdp")),
            P(None, None, ("dp", "fsdp")),
            P(None, None, ("dp", "fsdp")),
            P(None, None, ("dp", "fsdp")),
            P(None, None, ("dp", "fsdp")),
            P(None, None, ("dp", "fsdp")),
        ),
        check_vma=False,
    )
```

time: 1070 us -> 761 us (0.71)
  matrix products: 227 us -> 0 us
  Pallas kernels: 0 us -> 212 us
  local copies, waits for them, and re-layouts: 280 us -> 121 us
  waiting for transfers between devices: 464 us -> 391 us
  other arithmetic: 77.5 us -> 17.8 us
    dot_general x36 -> x0, matrix products: 227 us -> none  [the longest x8 62.4 us: times_transposed(): lax.dot_general(left, right, (((1,), (1,)), ((), ())), preferred_element_...]
    pallas_call x0 -> x8, Pallas kernels: none -> 212 us  [the longest x2 67.5 us: mlp_backward(): pl.pallas_call(mlp_backward_kernel, grid=(blocks,), in_specs=[whole(grad....]
    reshape x28 -> x14, local copies, waits for them, and re-layouts: 120 us -> 10.8 us  [the longest x2 7.32 us: unpack_layer(): blob[:, at:at + blocks * fc2[1]].reshape(devices, blocks, fc2[1], width)]
    all_gather x2, waiting for transfers between devices: 202 us -> 151 us  [on_device(): blob = lax.all_gather(share, AXES, axis=0, tiled=False)]
    convert_element_type x12 -> x0, other arithmetic: 39.6 us -> none  [the longest x2 23.4 us: layer_backward(): grad_scores = (attn_exact * (grad_probs - row_inner)).astype(jnp.bfloat16)]
    reduce_scatter x2, waiting for transfers between devices: 262 us -> 239 us  [on_device(): summed = lax.psum_scatter(packed, AXES, scatter_dimension=0, tiled=False)]
    reduce_sum x13 -> x0, other arithmetic: 21.3 us -> none  [the longest x2 5.68 us: layer_backward(): grad_columns = jnp.sum(grad_mixed.astype(jnp.float32), 0)]
    unnamed x274 -> x47, local copies, waits for them, and re-layouts: 28.9 us -> 11.2 us
  transfers between devices with their start and end apart: 4 -> 4, of which waited for: 4 -> 4; matrix products, arithmetic and copies ran while one was open for 8% -> 7% of each run, Pallas kernels for 0% -> 14%
where the time goes in v2:
time: 761 us; the launch traced here: 756 us
  waiting for transfers between devices  391 us (51%)
  Pallas kernels  212 us (28%)
  local copies, waits for them, and re-layouts  121 us (16%)
  other arithmetic  17.8 us (2%)
  between operations  15.2 us (2%)
    reduce_scatter x2, waiting for transfers between devices, on_device(): summed = lax.psum_scatter(packed, AXES, scatter_dimension=0, tiled=False)  239 us
    all_gather x2, waiting for transfers between devices, on_device(): blob = lax.all_gather(share, AXES, axis=0, tiled=False)  151 us
    pallas_call x2, Pallas kernels, mlp_backward(): pl.pallas_call(mlp_backward_kernel, grid=(blocks,), in_specs=[whole(grad....  67.5 us
    pallas_call x2, Pallas kernels, attn_backward(): pl.pallas_call(attn_backward_kernel, grid=(slots,), in_specs=[slot_block(...  58.8 us
    pallas_call x2, Pallas kernels, mlp_forward(): pl.pallas_call(mlp_forward_kernel, grid=(blocks,), in_specs=[whole(middle...  49.2 us
    pallas_call x2, Pallas kernels, attn_forward(): pl.pallas_call(partial(attn_forward_kernel, seq_len), grid=(slots,), in_s...  36.3 us
    scatter x6, local copies, waits for them, and re-layouts, pack_grads(): blob.at[:, at:at + rows]  25.2 us
  transfers between devices with their start and end apart: 4, of which 4 were waited for; matrix products, arithmetic and copies ran while one was open for 7% of the time, Pallas kernels for 14%

profile of v2, /device:TPU:0, one launch (start us, length us, event | category | flops | bytes accessed | tf_op | source)
XLA Modules:
  0.0 756.3 jit_solution(3502118569227949136)
XLA Ops:
  18.3 105.9 %all-gather.7.cloned.1.call-done = bf16[9728,768]{1,0:T(8,128)(2,1)} async-done(((bf16[304,768]{1,0:T(8,128)(2,1)}), bf16[9728,768]{1,0:T(8,128)(2,1)}) %all-gather.7.cloned.1.call-update) | async-done | bytes 14942224 | tf_op jit(solution)/shard_map/all_gather | solution.py:476
  124.2 4.0 slice.456
  133.8 6.8 fusion.25
  143.9 18.2 %attn_forward.2 = (bf16[4,208,768]{2,1,0:T(8,128)(2,1)}, bf16[4,208,2304]{2,1,0:T(8,128)(2,1)}, bf16[4,12,208,208]{3,2,1,0:T(8,128)(2,1)}, bf16[4,208,768]{2,1,0:T(8,128)(2,1)}, f32[4,208,768]{2,1,0:T(8,128)}) custom-call(f32[4,208,768]{2,1,0:T(8,128)} %pad_convert_fusion.x_ref, bf16[2304,768]{1,0:T(8,128)(2,1)} %bitcast.182, bf16[768,768]{1,0:T(8,128)(2,1)} %bitcast.190, ...), custom_call_target="tpu_custom_call" | custom-call | flops 17999998976 | bytes 1048576 | tf_op jit(solution)/shard_map/attn_forward/pallas_call | solution.py:122
  162.1 25.0 %mlp_forward.2 = (bf16[4,208,768]{2,1,0:T(8,128)(2,1)}, bf16[4,208,3072]{2,1,0:T(8,128)(2,1)}, bf16[4,208,3072]{2,1,0:T(8,128)(2,1)}, f32[4,208,768]{2,1,0:T(8,128)}) custom-call(f32[4,208,768]{2,1,0:T(8,128)} %get-tuple-element.171.middle_ref, bf16[3072,768]{1,0:T(8,128)(2,1)} %bitcast.178, bf16[4,768,768]{2,1,0:T(8,128)(2,1)} %bitcast.168, ...), custom_call_target="tpu_custom_call" | custom-call | flops 24000000000 | bytes 1048576 | tf_op jit(solution)/shard_map/mlp_forward/pallas_call | solution.py:175
  187.1 45.5 %all-gather.5.cloned.1.call-done = bf16[9728,768]{1,0:T(8,128)(2,1)} async-done(((bf16[304,768]{1,0:T(8,128)(2,1)}), bf16[9728,768]{1,0:T(8,128)(2,1)}) %all-gather.5.cloned.1.call-update) | async-done | bytes 14942224 | tf_op jit(solution)/shard_map/all_gather | solution.py:476
  232.6 4.1 slice.464
  240.6 7.9 %fusion.24 = (bf16[32,96,768]{2,1,0:T(8,128)(2,1)}, bf16[32,96,768]{2,1,0:T(8,128)(2,1)}) fusion(bf16[32,304,768]{2,1,0:T(8,128)(2,1)} %bitcast.163), kind=kLoop, calls=%fused_computation.81 | loop fusion | bytes 18874368 | tf_op jit(solution)/shard_map/slice | solution.py:407
  250.4 4.8 copy.111
  255.9 18.1 %attn_forward.3 = (bf16[4,208,768]{2,1,0:T(8,128)(2,1)}, bf16[4,208,2304]{2,1,0:T(8,128)(2,1)}, bf16[4,12,208,208]{3,2,1,0:T(8,128)(2,1)}, bf16[4,208,768]{2,1,0:T(8,128)(2,1)}, f32[4,208,768]{2,1,0:T(8,128)}) custom-call(f32[4,208,768]{2,1,0:T(8,128)} %get-tuple-element.173.x_ref, bf16[2304,768]{1,0:T(8,128)(2,1)} %bitcast.184, bf16[768,768]{1,0:T(8,128)(2,1)} %bitcast.192, ...), custom_call_target="tpu_custom_call" | custom-call | flops 17999998976 | bytes 1048576 | tf_op jit(solution)/shard_map/attn_forward/pallas_call | solution.py:122
  274.0 24.2 %mlp_forward.3 = (bf16[4,208,768]{2,1,0:T(8,128)(2,1)}, bf16[4,208,3072]{2,1,0:T(8,128)(2,1)}, bf16[4,208,3072]{2,1,0:T(8,128)(2,1)}, f32[4,208,768]{2,1,0:T(8,128)}) custom-call(f32[4,208,768]{2,1,0:T(8,128)} %get-tuple-element.175.middle_ref, bf16[3072,768]{1,0:T(8,128)(2,1)} %bitcast.180, bf16[4,768,768]{2,1,0:T(8,128)(2,1)} %bitcast.176, ...), custom_call_target="tpu_custom_call" | custom-call | flops 24000000000 | bytes 1048576 | tf_op jit(solution)/shard_map/mlp_forward/pallas_call | solution.py:175
  298.1 3.1 convert_multiply_fusion
  303.0 33.7 %mlp_backward.2 = (bf16[3072,768]{1,0:T(8,128)(2,1)}, bf16[4,768,768]{2,1,0:T(8,128)(2,1)}, f32[4,8,768]{2,1,0:T(8,128)}, f32[8,768]{1,0:T(8,128)}, f32[4,208,768]{2,1,0:T(8,128)}) custom-call(f32[4,208,768]{2,1,0:T(8,128)} %pad.59.grad_ref, f32[4,208,768]{2,1,0:T(8,128)} %get-tuple-element.175.middle_ref, ...), custom_call_target="tpu_custom_call" | custom-call | flops 33999998976 | bytes 1048576 | tf_op jit(solution)/shard_map/mlp_backward/pallas_call | solution.py:273
  338.0 29.0 %attn_backward.2 = (bf16[2304,768]{1,0:T(8,128)(2,1)}, bf16[768,768]{1,0:T(8,128)(2,1)}, f32[8,768]{1,0:T(8,128)}, f32[4,208,768]{2,1,0:T(8,128)}) custom-call(f32[4,208,768]{2,1,0:T(8,128)} %get-tuple-element.180.grad_ref, f32[4,208,768]{2,1,0:T(8,128)} %get-tuple-element.173.x_ref, bf16[4,208,768]{2,1,0:T(8,128)(2,1)} %get-tuple-element.181.normed_ref, ...), custom_call_target="tpu_custom_call" | custom-call | flops 28999999488 | bytes 1048576 | tf_op jit(solution)/shard_map/attn_backward/pallas_call | solution.py:367
  369.0 5.3 copy.119
  386.6 7.1 scatter.41
  400.1 2.9 scatter.49
  403.1 33.8 %mlp_backward.3 = (bf16[3072,768]{1,0:T(8,128)(2,1)}, bf16[4,768,768]{2,1,0:T(8,128)(2,1)}, f32[4,8,768]{2,1,0:T(8,128)}, f32[8,768]{1,0:T(8,128)}, f32[4,208,768]{2,1,0:T(8,128)}) custom-call(f32[4,208,768]{2,1,0:T(8,128)} %get-tuple-element.185.grad_ref, f32[4,208,768]{2,1,0:T(8,128)} %get-tuple-element.171.middle_ref, ...), custom_call_target="tpu_custom_call" | custom-call | flops 33999998976 | bytes 1048576 | tf_op jit(solution)/shard_map/mlp_backward/pallas_call | solution.py:273
  437.7 29.8 %attn_backward.3 = (bf16[2304,768]{1,0:T(8,128)(2,1)}, bf16[768,768]{1,0:T(8,128)(2,1)}, f32[8,768]{1,0:T(8,128)}, f32[4,208,768]{2,1,0:T(8,128)}) custom-call(f32[4,208,768]{2,1,0:T(8,128)} %get-tuple-element.189.grad_ref, f32[4,208,768]{2,1,0:T(8,128)} %pad_convert_fusion.x_ref, bf16[4,208,768]{2,1,0:T(8,128)(2,1)} %get-tuple-element.190.normed_ref, ...), custom_call_target="tpu_custom_call" | custom-call | flops 28999999488 | bytes 1048576 | tf_op jit(solution)/shard_map/attn_backward/pallas_call | solution.py:367
  468.2 7.9 %scatter.34 = bf16[32,304,768]{2,1,0:T(8,128)(2,1)} pad(bf16[32,72,768]{2,1,0:T(8,128)(2,1)} %bitcast.187, bf16[]{:T(256)} %constant.237.clone.1), padding=0_0x0_232x0_0 | pad | bytes 18481154 | tf_op jit(solution)/shard_map/scatter | solution.py:429
  482.0 5.5 constant_dynamic-update-slice_fusion.6
  489.9 2.9 scatter.40
  500.1 68.0 %reduce-scatter.5.cloned.1.call-done = bf16[1,304,768]{2,1,0:T(8,128)(2,1)} async-done(((bf16[32,304,768]{2,1,0:T(8,128)(2,1)}), bf16[1,304,768]{2,1,0:T(8,128)(2,1)}) %reduce-scatter.5.cloned.1.call-update) | async-done | bytes 466960 | tf_op jit(solution)/shard_map/reduce_scatter | solution.py:519
  569.3 171.3 %reduce-scatter.3.cloned.1.call-done = bf16[1,304,768]{2,1,0:T(8,128)(2,1)} async-done(((bf16[32,304,768]{2,1,0:T(8,128)(2,1)}), bf16[1,304,768]{2,1,0:T(8,128)(2,1)}) %reduce-scatter.3.cloned.1.call-update) | async-done | bytes 466960 | tf_op jit(solution)/shard_map/reduce_scatter | solution.py:519
  (181 shorter events, 76.2 us)
Async XLA Ops:
  7.2 9.2 %copy-start.5 = (bf16[4,197,768]{2,0,1:T(4,128)(2,1)S(1)}, bf16[4,197,768]{2,0,1:T(4,128)(2,1)}, u32[]{:S(2)}) copy-start(bf16[4,197,768]{2,0,1:T(4,128)(2,1)} %param.30) | copy-start | bytes 3631108
  7.2 117.0 %all-gather.7.cloned.1.call-start = ((), (), s32[]{:S(2)}) async-start(), calls=%async_computation.5 | async-start | bytes 15409152 | tf_op jit(solution)/shard_map/all_gather | solution.py:476
  13.9 0.8 copy-start.9
  14.7 217.9 %all-gather.5.cloned.1.call-start = ((), (), s32[]{:S(2)}) async-start(), calls=%async_computation.4 | async-start | bytes 15409152 | tf_op jit(solution)/shard_map/all_gather | solution.py:476
  14.9 0.8 copy-start.10
  15.7 552.4 %reduce-scatter.5.cloned.1.call-start = ((), (), s32[]{:S(2)}) async-start(), calls=%async_computation.3 | async-start | bytes 15409152 | tf_op jit(solution)/shard_map/reduce_scatter | solution.py:519
  274.0 24.2 %copy-start.6 = (bf16[4,197,768]{2,0,1:T(4,128)(2,1)S(1)}, bf16[4,197,768]{2,0,1:T(4,128)(2,1)}, u32[]{:S(2)}) copy-start(bf16[4,197,768]{2,0,1:T(4,128)(2,1)} %param.32) | copy-start | bytes 3631108
  369.0 17.6 %copy-start.2 = (bf16[2304,768]{1,0:T(8,128)(2,1)S(1)}, bf16[2304,768]{1,0:T(8,128)(2,1)}, u32[]{:S(2)}) copy-start(bf16[2304,768]{1,0:T(8,128)(2,1)} %get-tuple-element.202) | copy-start | bytes 10616836
  386.6 8.3 %slice-start.4 = ((s8[4718592]{0:T(1024)(128)(4,1)}), s8[4194304]{0:T(1024)(128)(4,1)S(1)}, s32[]{:S(2)}) async-start(s8[4718592]{0:T(1024)(128)(4,1)} %bitcast.171), calls=%async_computation.10 | async-start | bytes 8388608
  386.6 7.2 copy-start.8
  386.6 8.3 %slice-start.5 = ((s8[4718592]{0:T(1024)(128)(4,1)}), s8[524288]{0:T(1024)(128)(4,1)S(1)}, s32[]{:S(2)}) async-start(s8[4718592]{0:T(1024)(128)(4,1)} %bitcast.171), calls=%async_computation.11 | async-start | bytes 1048576
  393.8 3.5 slice-start
  394.9 2.7 slice-start.1
  397.7 2.4 copy-start.11
  403.0 337.6 %reduce-scatter.3.cloned.1.call-start = ((), (), s32[]{:S(2)}) async-start(), calls=%async_computation.2 | async-start | bytes 15409152 | tf_op jit(solution)/shard_map/reduce_scatter | solution.py:519
  468.2 8.0 %copy-start.1 = (bf16[4,768,768]{2,1,0:T(8,128)(2,1)S(1)}, bf16[4,768,768]{2,1,0:T(8,128)(2,1)}, u32[]{:S(2)}) copy-start(bf16[4,768,768]{2,1,0:T(8,128)(2,1)} %get-tuple-element.198) | copy-start | bytes 14155780
  476.2 4.6 copy-start.7
  480.8 6.6 slice-start.2
  482.0 5.5 slice-start.3
  492.8 1.4 copy-start
  568.1 173.8 %copy-start.3 = (bf16[1,304,768]{2,1,0:T(8,128)(2,1)S(1)}, bf16[1,304,768]{2,1,0:T(8,128)(2,1)}, u32[]{:S(2)}) copy-start(bf16[1,304,768]{2,1,0:T(8,128)(2,1)} %reduce-scatter.5.cloned.1.call-done) | copy-start | bytes 1400836
  740.6 3.5 copy-start.4
Sparse Core Ops, SparseCore 0:
  14.8 109.3 all-gather.6
  127.8 104.7 all-gather.4
  403.1 164.9 reduce-scatter.4
  575.1 165.4 reduce-scatter.2

commit v3 on v2

--- a/solution.py
+++ b/solution.py
@@ -15,6 +15,8 @@
 VMEM_BYTES = 60 * 1024 * 1024
 TILE_ROWS = 16
 LANES = 128
+SHARE_STEP = 384
+BACKWARD_WORTH = 1
 MASKED = -1e30
 
 
@@ -46,6 +48,23 @@
     lane = lax.broadcasted_iota(jnp.int32, pair.shape, 1)
     mine = (lane >= HEAD_DIM) if side else (lane < HEAD_DIM)
     return jnp.where(mine, pair, jnp.zeros_like(pair))
+
+
+def put(refs, me_ref, pair, rows, even, odd):
+    if len(refs) == 1:
+        refs[0][2 * pair, rows, :] = even.astype(jnp.bfloat16)
+        refs[0][2 * pair + 1, rows, :] = odd.astype(jnp.bfloat16)
+    else:
+        place = pair ^ (me_ref[0] >> 1)
+        low = (me_ref[0] & 1) == 0
+        refs[0][place, rows, :] = jnp.where(low, even, odd).astype(jnp.bfloat16)
+        refs[1][place, rows, :] = jnp.where(low, odd, even).astype(jnp.bfloat16)
+
+
+def share_shapes(mode, devices, rows, width):
+    if mode == "joined":
+        return [jax.ShapeDtypeStruct((devices, rows, width), jnp.bfloat16)]
+    return [jax.ShapeDtypeStruct((devices // 2, rows, width), jnp.bfloat16)] * 2
 
 
 def attn_forward_kernel(seq_len, x_ref, w_qkv_ref, w_proj_ref, gains_ref, biases_ref,
@@ -90,7 +109,7 @@
 
 
 def whole(shape):
-    return pl.BlockSpec(shape, lambda i: (0,) * len(shape))
+    return pl.BlockSpec(shape, lambda i: (0,) * len(shape), pipeline_mode=pl.Buffered(1))
 
 
 def slot_block(shape):
@@ -191,10 +210,11 @@
     )(middle, w_fc1, w_fc2, gains, biases, fc1_bias)
 
 
-def mlp_backward_kernel(grad_ref, middle_ref, normed_ref, hidden_ref, slope_ref, w_fc1_ref,
-                        w_fc2_ref, gains_ref,
-                        grad_fc1_ref, grad_fc2_ref, fc1_sums_ref, sums_ref, out_ref,
-                        branch_ref, pre_ref, total_ref):
+def mlp_backward_kernel(mode, cut, me_ref, grad_ref, middle_ref, normed_ref, hidden_ref, slope_ref, w_fc1_ref,
+                        w_fc2_ref, gains_ref, *refs):
+    share_count = 1 if mode == "joined" else 2
+    share_refs = refs[:share_count]
+    fc1_sums_ref, sums_ref, out_ref, branch_ref, pre_ref, total_ref, before_ref = refs[share_count:]
     block = pl.program_id(0)
     slots, padded, width = grad_ref.shape
 
@@ -231,16 +251,42 @@
         return carry
 
     lax.fori_loop(0, slots, rows, 0)
-    step = 2 * LANES
     hidden = hidden_ref[...].reshape(slots * padded, width)
     normed = normed_ref[...].reshape(slots * padded, width)
-    for at in range(0, width, step):
-        grad_fc2_ref[0, at : at + step, :] = dot(
-            branch_ref[:, at : at + step], hidden, MATMUL_TN
-        ).astype(jnp.bfloat16)
-        grad_fc1_ref[at : at + step, :] = dot(
-            pre_ref[:, at : at + step], normed, MATMUL_TN
-        ).astype(jnp.bfloat16)
+    if mode == "plain":
+        grad_fc1_ref, grad_fc2_ref = share_refs
+        step = 2 * LANES
+        for at in range(0, width, step):
+            grad_fc2_ref[0, at : at + step, :] = dot(
+                branch_ref[:, at : at + step], hidden, MATMUL_TN
+            ).astype(jnp.bfloat16)
+            grad_fc1_ref[at : at + step, :] = dot(
+                pre_ref[:, at : at + step], normed, MATMUL_TN
+            ).astype(jnp.bfloat16)
+    else:
+        tall = 4 * cut
+        for at in range(0, width, SHARE_STEP):
+            value = dot(pre_ref[:, at : at + SHARE_STEP], normed, MATMUL_TN)
+            value = value.reshape(SHARE_STEP // tall, tall, width)
+            for s in range(0, SHARE_STEP // tall, 2):
+                pair = block * (width // tall // 2) + at // tall // 2 + s // 2
+                put(share_refs, me_ref, pair, slice(0, tall), value[s], value[s + 1])
+            value = dot(branch_ref[:, at : at + SHARE_STEP], hidden, MATMUL_TN)
+
+            @pl.when(block % 2 == 0)
+            def _():
+                before_ref[at : at + SHARE_STEP, :] = value
+
+            for odd in range(1, 4, 2):
+
+                @pl.when(block == odd)
+                def _():
+                    before = before_ref[at : at + SHARE_STEP, :].reshape(-1, cut, width)
+                    both = jnp.concatenate([before, value.reshape(-1, cut, width)], 1)
+                    rows = slice(tall + (odd - 1) * cut, tall + (odd + 1) * cut)
+                    for s in range(0, SHARE_STEP // cut, 2):
+                        pair = at // cut // 2 + s // 2
+                        put(share_refs, me_ref, pair, rows, both[s], both[s + 1])
 
     @pl.when(block == pl.num_programs(0) - 1)
     def _():
@@ -257,27 +303,32 @@
         lax.fori_loop(0, slots, last, 0)
 
 
-def mlp_backward(grad, middle, normed, hidden, slope, w_fc1, w_fc2, gains):
+def mlp_backward(mode, devices, me, grad, middle, normed, hidden, slope, w_fc1, w_fc2, gains):
     slots, padded, width = grad.shape
     blocks = w_fc2.shape[0]
-    outs = [
-        jax.ShapeDtypeStruct(w_fc1.shape, jnp.bfloat16),
-        jax.ShapeDtypeStruct(w_fc2.shape, jnp.bfloat16),
+    cut = width // devices
+    fc1_spec = pl.BlockSpec((width, width), lambda i: (i, 0))
+    fc2_spec = pl.BlockSpec((1, width, width), lambda i: (i, 0, 0))
+    if mode == "plain":
+        shares = [jax.ShapeDtypeStruct(v.shape, jnp.bfloat16) for v in (w_fc1, w_fc2)]
+        share_specs = [fc1_spec, fc2_spec]
+    else:
+        shares = share_shapes(mode, devices, 8 * cut, width)
+        share_specs = [whole(v.shape) for v in shares]
+    outs = shares + [
         jax.ShapeDtypeStruct((blocks, 8, width), jnp.float32),
         jax.ShapeDtypeStruct((8, width), jnp.float32),
         jax.ShapeDtypeStruct(grad.shape, jnp.float32),
     ]
     wide_spec = pl.BlockSpec((slots, padded, width), lambda i: (0, 0, i))
-    fc1_spec = pl.BlockSpec((width, width), lambda i: (i, 0))
-    fc2_spec = pl.BlockSpec((1, width, width), lambda i: (i, 0, 0))
     return pl.pallas_call(
-        mlp_backward_kernel,
+        partial(mlp_backward_kernel, mode, cut),
         grid=(blocks,),
-        in_specs=[whole(grad.shape), whole(grad.shape), whole(grad.shape)]
+        in_specs=[pl.BlockSpec(memory_space=pltpu.SMEM)]
+        + [whole(grad.shape), whole(grad.shape), whole(grad.shape)]
         + [wide_spec, wide_spec, fc1_spec, fc2_spec, whole(gains.shape)],
-        out_specs=[
-            fc1_spec,
-            fc2_spec,
+        out_specs=share_specs
+        + [
             pl.BlockSpec((1, 8, width), lambda i: (i, 0, 0)),
             whole((8, width)),
             whole(grad.shape),
@@ -287,17 +338,19 @@
             pltpu.VMEM((slots * padded, width), jnp.bfloat16),
             pltpu.VMEM((slots * padded, width), jnp.bfloat16),
             pltpu.VMEM(grad.shape, jnp.float32),
+            pltpu.VMEM((width, width), jnp.float32),
         ],
         compiler_params=params(),
-        cost_estimate=worth(34),
+        cost_estimate=worth(BACKWARD_WORTH),
         name="mlp_backward",
-    )(grad, middle, normed, hidden, slope, w_fc1, w_fc2, gains)
-
-
-def attn_backward_kernel(grad_ref, x_ref, normed_ref, mixed_ref, probs_ref, attended_ref,
-                         w_qkv_ref, w_proj_ref, gains_ref,
-                         grad_qkv_ref, grad_proj_ref, sums_ref, out_ref,
-                         mixed_all, normed_all, attended_all, branch_all):
+    )(me, grad, middle, normed, hidden, slope, w_fc1, w_fc2, gains)
+
+
+def attn_backward_kernel(mode, cut, me_ref, grad_ref, x_ref, normed_ref, mixed_ref, probs_ref, attended_ref,
+                         w_qkv_ref, w_proj_ref, gains_ref, *refs):
+    share_count = 1 if mode == "joined" else 2
+    share_refs = refs[:share_count]
+    sums_ref, out_ref, mixed_all, normed_all, attended_all, branch_all = refs[share_count:]
     slot = pl.program_id(0)
     _, padded, width = grad_ref.shape
     here = pl.ds(pl.multiple_of(slot * padded, TILE_ROWS), padded)
@@ -344,32 +397,51 @@
 
     @pl.when(slot == pl.num_programs(0) - 1)
     def _():
-        step = 2 * LANES
-        for at in range(0, 3 * width, step):
-            grad_qkv_ref[at : at + step, :] = dot(
-                mixed_all[:, at : at + step], normed_all[...], MATMUL_TN
-            ).astype(jnp.bfloat16)
-        for at in range(0, width, step):
-            grad_proj_ref[at : at + step, :] = dot(
-                branch_all[:, at : at + step], attended_all[...], MATMUL_TN
-            ).astype(jnp.bfloat16)
-
-
-def attn_backward(grad, state, normed, mixed, probs, attended, w_qkv, w_proj, gains):
+        if mode == "plain":
+            grad_qkv_ref, grad_proj_ref = share_refs
+            step = 2 * LANES
+            for at in range(0, 3 * width, step):
+                grad_qkv_ref[at : at + step, :] = dot(
+                    mixed_all[:, at : at + step], normed_all[...], MATMUL_TN
+                ).astype(jnp.bfloat16)
+            for at in range(0, width, step):
+                grad_proj_ref[at : at + step, :] = dot(
+                    branch_all[:, at : at + step], attended_all[...], MATMUL_TN
+                ).astype(jnp.bfloat16)
+        else:
+            for at in range(0, width, SHARE_STEP):
+                three = slice(3 * at, 3 * (at + SHARE_STEP))
+                value = dot(mixed_all[:, three], normed_all[...], MATMUL_TN)
+                more = dot(
+                    branch_all[:, at : at + SHARE_STEP], attended_all[...], MATMUL_TN
+                )
+                both = jnp.concatenate(
+                    [value.reshape(-1, 3 * cut, width), more.reshape(-1, cut, width)], 1
+                )
+                for s in range(0, SHARE_STEP // cut, 2):
+                    pair = at // cut // 2 + s // 2
+                    put(share_refs, me_ref, pair, slice(0, 4 * cut), both[s], both[s + 1])
+
+
+def attn_backward(mode, devices, me, grad, state, normed, mixed, probs, attended, w_qkv, w_proj, gains, length):
     slots, padded, width = grad.shape
-    outs = [
-        jax.ShapeDtypeStruct(w_qkv.shape, jnp.bfloat16),
-        jax.ShapeDtypeStruct(w_proj.shape, jnp.bfloat16),
+    cut = width // devices
+    if mode == "plain":
+        shares = [jax.ShapeDtypeStruct(v.shape, jnp.bfloat16) for v in (w_qkv, w_proj)]
+    else:
+        shares = share_shapes(mode, devices, 4 * cut + TILE_ROWS, width)
+    outs = shares + [
         jax.ShapeDtypeStruct((8, width), jnp.float32),
         jax.ShapeDtypeStruct(grad.shape, jnp.float32),
     ]
     sliced = (grad, state, normed, mixed, probs, attended)
     return pl.pallas_call(
-        attn_backward_kernel,
+        partial(attn_backward_kernel, mode, cut),
         grid=(slots,),
-        in_specs=[slot_block(v.shape) for v in sliced]
+        in_specs=[pl.BlockSpec(memory_space=pltpu.SMEM)]
+        + [slot_block(v.shape) for v in sliced]
         + [whole(v.shape) for v in (w_qkv, w_proj, gains)],
-        out_specs=[whole(o.shape) for o in outs[:3]] + [slot_block(grad.shape)],
+        out_specs=[whole(o.shape) for o in outs[:-1]] + [slot_block(grad.shape)],
         out_shape=outs,
         scratch_shapes=[
             pltpu.VMEM((slots * padded, 3 * width), jnp.bfloat16),
@@ -378,9 +450,9 @@
             pltpu.VMEM((slots * padded, width), jnp.bfloat16),
         ],
         compiler_params=params(),
-        cost_estimate=worth(29),
+        cost_estimate=worth(length),
         name="attn_backward",
-    )(*sliced, w_qkv, w_proj, gains)
+    )(me, *sliced, w_qkv, w_proj, gains)
 
 
 AXES = ("dp", "fsdp")
@@ -463,11 +535,99 @@
     return tuple(parts)
 
 
-def on_device(images, counts, cotangent, *weights):
+def small_shares(values, devices):
+    cut = [v.reshape(v.shape[0], devices, -1).transpose(1, 0, 2) for v in values]
+    return jnp.concatenate([v.reshape(devices, -1) for v in cut], 1).astype(jnp.bfloat16)
+
+
+def small_rows(row, width):
+    row = jnp.pad(row, ((0, 0), (0, -row.shape[1] % (TILE_ROWS * width))))
+    return row.reshape(row.shape[0], -1, width)
+
+
+def swap(value, axis, mask, size):
+    return lax.ppermute(value, axis, [(i, i ^ mask) for i in range(size)])
+
+
+def total_of(values):
+    return sum(v.astype(jnp.float32) for v in values).astype(jnp.bfloat16)
+
+
+class Exchange:
+    def __init__(self, mine, other, fsdp_size, orders):
+        rows, width = mine.shape[-2:]
+        self.fsdp_size = fsdp_size
+        self.orders = [list(order) for order in orders]
+        self.kept = mine
+        self.shape = (2, 2, fsdp_size // 2, rows // len(orders), width)
+        self.pending = None if other is None else [[swap(other, "fsdp", 1, fsdp_size)]]
+
+    def sums(self):
+        if self.pending is None:
+            return [self.kept]
+        if isinstance(self.kept, list):
+            return [total_of([k, *got]) for k, got in zip(self.kept, self.pending)]
+        got = self.pending[0][0]
+        rows = self.shape[3]
+        cuts = [slice(i * rows, (i + 1) * rows) for i in range(len(self.orders))]
+        return [total_of([self.kept[:, c], got[:, c]]).reshape(self.shape) for c in cuts]
+
+    def step(self):
+        kept, pending = [], []
+        for value, order in zip(self.sums(), self.orders):
+            stage = order.pop(0)
+            if stage == "z":
+                kept.append(value[:, :, :1])
+                pending.append(
+                    [
+                        swap(value[:, :, i : i + 1], "fsdp", 2 * i, self.fsdp_size)
+                        for i in range(1, self.fsdp_size // 2)
+                    ]
+                )
+            elif stage == "x":
+                kept.append(value[:, :1])
+                pending.append([swap(value[:, 1:], "dp", 1, 4)])
+            elif stage == "y":
+                kept.append(value[:1])
+                pending.append([swap(value[1:], "dp", 2, 4)])
+            else:
+                kept.append(value[:1, :1])
+                pending.append(
+                    [
+                        swap(value[i // 2 : i // 2 + 1, i % 2 : i % 2 + 1], "dp", i, 4)
+                        for i in range(1, 4)
+                    ]
+                )
+        self.kept, self.pending = kept, pending
+
+    def result(self):
+        return jnp.concatenate([v.reshape(self.shape[3:]) for v in self.sums()], 0)
+
+
+def gate(values, *exchanges):
+    values, arrived = lax.optimization_barrier((values, [e.pending for e in exchanges]))
+    for exchange, pending in zip(exchanges, arrived):
+        exchange.pending = pending
+    return values
+
+
+HALVES = (("x", "y"), ("y", "x"))
+WHOLE = (("xy", "z"),)
+
+
+def on_device(dp_size, fsdp_size, images, counts, cotangent, *weights):
     slots, seq_len, width = images.shape
     layer_count = weights[0].shape[0]
     shapes = [w.shape[1:] for w in weights]
+    devices = dp_size * fsdp_size
+    cut = width // devices
+    direct = dp_size == 4 and layer_count == 2 and cut % 8 == 0 and SHARE_STEP % (8 * cut) == 0 and devices * cut == width
     live = (jnp.arange(slots) < counts[0]).astype(jnp.float32)[:, None, None]
+    me = lax.axis_index("dp") * fsdp_size + lax.axis_index("fsdp")
+    place = jnp.arange(devices)
+    place = (jnp.bitwise_xor(2 * (place % (devices // 2)) + place // (devices // 2), me))[:, None]
+    relative = (place == jnp.arange(devices)[None]).astype(jnp.bfloat16)
+    me = me.astype(jnp.int32).reshape(1)
     extra = ((0, 0), (0, -seq_len % TILE_ROWS), (0, 0))
     state = jnp.pad(images.astype(jnp.float32), extra)
     gathered = []
@@ -491,33 +651,73 @@
     block_output = (state[:, :seq_len] * live).astype(jnp.bfloat16)
     grad_state = jnp.pad(cotangent.astype(jnp.float32) * live, extra)
     layer_grads = [None] * layer_count
-    for layer_index in reversed(range(layer_count)):
-        w_qkv, w_proj, w_fc1, w_fc2, gains, biases, fc1_bias = gathered[layer_index]
-        entry, normed_one, mixed, probs, attended, middle, normed_two, hidden, slope = kept[
-            layer_index
-        ]
-        grad_fc1, grad_fc2, fc1_sums, mlp_sums, grad_middle = mlp_backward(
-            grad_state, middle, normed_two, hidden, slope, w_fc1, w_fc2, gains
+
+    def small_of(mlp, attn):
+        fc1_sums, mlp_sums = mlp
+        gains_grad = jnp.stack([attn[0], mlp_sums[0]])
+        biases_grad = jnp.stack([attn[1], attn[2], attn[3], attn[4], mlp_sums[1], mlp_sums[2]])
+        return (gains_grad, biases_grad, fc1_sums[:, 0].reshape(1, -1))
+
+    def mlp_part(layer_index, mode, grad_state):
+        w_fc1, w_fc2, gains = gathered[layer_index][2:5]
+        middle, normed, hidden, slope = kept[layer_index][5:]
+        *shares, fc1_sums, sums, grad_middle = mlp_backward(
+            mode, devices, me, grad_state, middle, normed, hidden, slope, w_fc1, w_fc2, gains
         )
-        grad_qkv, grad_proj, attn_sums, grad_state = attn_backward(
-            grad_middle, entry, normed_one, mixed, probs, attended, w_qkv, w_proj, gains
+        return shares, (fc1_sums, sums), grad_middle
+
+    def attn_part(layer_index, mode, grad_middle):
+        w_qkv, w_proj, gains = (gathered[layer_index][i] for i in (0, 1, 4))
+        *shares, sums, grad_state = attn_backward(
+            mode, devices, me, grad_middle, *kept[layer_index][:5], w_qkv, w_proj, gains,
+            1 if layer_index else 200
         )
-        gains_grad = jnp.stack([attn_sums[0], mlp_sums[0]])
-        biases_grad = jnp.stack(
-            [attn_sums[1], attn_sums[2], attn_sums[3], attn_sums[4], mlp_sums[1], mlp_sums[2]]
-        )
-        grads = (
-            grad_qkv,
-            grad_proj,
-            grad_fc1,
-            grad_fc2,
-            gains_grad,
-            biases_grad,
-            fc1_sums[:, 0].reshape(1, -1),
-        )
-        packed = pack_grads(grads, shapes, share.shape[0], blob.shape[0])
-        summed = lax.psum_scatter(packed, AXES, scatter_dimension=0, tiled=False)
-        layer_grads[layer_index] = unpack_grads(summed, shapes)
+        return shares, sums, grad_state
+
+    def with_small(shares, mlp, attn):
+        row = small_shares(small_of(mlp, attn), devices)
+        row = jnp.dot(relative, row, preferred_element_type=jnp.float32).astype(jnp.bfloat16)
+        row = small_rows(row, width)
+        count = shares[0].shape[0]
+        return [v.at[:, 4 * cut :].set(row[i * count : (i + 1) * count]) for i, v in enumerate(shares)]
+
+    def owned(attn_sum, mlp_sum):
+        summed = jnp.concatenate([attn_sum[: 4 * cut], mlp_sum, attn_sum[4 * cut :]], 0)
+        return unpack_grads(summed, shapes)
+
+    if direct:
+        shares, mlp, grad_middle = mlp_part(1, "split", grad_state)
+        mlp_one = Exchange(*shares, fsdp_size, HALVES)
+        shares, attn, grad_state = attn_part(1, "split", grad_middle)
+        shares, attn, grad_state = gate((shares, attn, grad_state), mlp_one)
+        mlp_one.step()
+        attn_one = Exchange(*with_small(shares, mlp, attn), fsdp_size, WHOLE)
+        shares, mlp, grad_middle = mlp_part(0, "joined", grad_state)
+        mlp_zero = lax.psum_scatter(shares[0], AXES, scatter_dimension=0, tiled=False)
+        grad_middle, mlp = gate((grad_middle, mlp), mlp_one, attn_one)
+        mlp_one.step()
+        attn_one.step()
+        shares, attn, grad_state = attn_part(0, "split", grad_middle)
+        shares, attn, grad_state = gate((shares, attn, grad_state), mlp_one, attn_one)
+        late = mlp_one.sums() + attn_one.sums()
+        late = Exchange(jnp.concatenate(late, 3), None, fsdp_size, (("z",),))
+        late.step()
+        attn_zero = Exchange(*with_small(shares, mlp, attn), fsdp_size, WHOLE)
+        attn_zero.step()
+        arrived = attn_zero.pending
+        late.pending, arrived = lax.optimization_barrier((late.pending, arrived))
+        attn_zero.step()
+        late = late.result()
+        layer_grads[1] = owned(late[8 * cut :], late[: 8 * cut])
+        layer_grads[0] = owned(attn_zero.result(), mlp_zero)
+    else:
+        for layer_index in reversed(range(layer_count)):
+            mlp_shares, mlp, grad_middle = mlp_part(layer_index, "plain", grad_state)
+            attn_shares, attn, grad_state = attn_part(layer_index, "plain", grad_middle)
+            grads = (*attn_shares, *mlp_shares, *small_of(mlp, attn))
+            packed = pack_grads(grads, shapes, share.shape[0], devices)
+            summed = lax.psum_scatter(packed, AXES, scatter_dimension=0, tiled=False)
+            layer_grads[layer_index] = unpack_grads(summed, shapes)
     stacked = tuple((jnp.stack([entry[member] for entry in layer_grads]) for member in range(7)))
     return (block_output, grad_state[:, :seq_len], *stacked)
 
@@ -536,7 +736,7 @@
         P(None, None, ("dp", "fsdp")),
     )
     return jax.shard_map(
-        on_device,
+        partial(on_device, mesh.shape["dp"], mesh.shape["fsdp"]),
         mesh=mesh,
         in_specs=placed,
         out_specs=(

time: 761 us -> 603 us (0.79)
  waiting for transfers between devices: 391 us -> 217 us
  local copies, waits for them, and re-layouts: 121 us -> 79.5 us
  starting transfers between devices: 0.16 us -> 34.8 us
  other arithmetic: 17.8 us -> 32 us
  Pallas kernels: 212 us -> 221 us
    reduce_scatter x2 -> x1, waiting for transfers between devices: 239 us -> 15.4 us  [on_device(): lax.psum_scatter(shares[0], AXES, scatter_dimension=0, tiled=False)]
    ppermute x0 -> x19, waiting for transfers between devices: none -> 49.9 us  [swap(): return lax.ppermute(value, axis, [(i, i ^ mask) for i in range(size)])]
    ppermute x0 -> x19, starting transfers between devices: none -> 34.7 us  [swap(): return lax.ppermute(value, axis, [(i, i ^ mask) for i in range(size)])]
    scatter x10 -> x4, local copies, waits for them, and re-layouts: 35.9 us -> 3.38 us  [with_small(): v.at[:, 4 * cut:].set(row[i * count:(i + 1) * count])]
    convert_element_type x0 -> x11, other arithmetic: none -> 18.7 us  [total_of(): return sum((v.astype(jnp.float32) for v in values)).astype(jnp.bfloat16)]
    transpose x6, local copies, waits for them, and re-layouts: 11.1 us -> 0.59 us  [the longest x4 0.36 us: small_shares(): v.reshape(v.shape[0], devices, -1).transpose(1, 0, 2)]
    pallas_call x4, Pallas kernels: 126 us -> 135 us  [the longest x2 75.3 us: mlp_backward(): pl.pallas_call(partial(mlp_backward_kernel, mode, cut), grid=(blocks,), i...]
  transfers between devices with their start and end apart: 4 -> 22, of which waited for: 4 -> 7; matrix products, arithmetic and copies ran while one was open for 7% -> 10% of each run, Pallas kernels for 14% -> 24%
where the time goes in v3:
time: 603 us; the launch traced here: 599 us
  Pallas kernels  221 us (37%)
  waiting for transfers between devices  217 us (36%)
  local copies, waits for them, and re-layouts  79.5 us (13%)
  starting transfers between devices  34.8 us (6%)
  other arithmetic  32 us (5%)
  between operations  15.5 us (3%)
    all_gather x2, waiting for transfers between devices, on_device(): blob = lax.all_gather(share, AXES, axis=0, tiled=False)  151 us
    pallas_call x2, Pallas kernels, mlp_backward(): pl.pallas_call(partial(mlp_backward_kernel, mode, cut), grid=(blocks,), i...  75.3 us
    pallas_call x2, Pallas kernels, attn_backward(): pl.pallas_call(partial(attn_backward_kernel, mode, cut), grid=(slots,), i...  59.9 us
    ppermute x19, waiting for transfers between devices, swap(): return lax.ppermute(value, axis, [(i, i ^ mask) for i in range(size)])  49.9 us
    pallas_call x2, Pallas kernels, mlp_forward(): pl.pallas_call(mlp_forward_kernel, grid=(blocks,), in_specs=[whole(middle...  49 us
    pallas_call x2, Pallas kernels, attn_forward(): pl.pallas_call(partial(attn_forward_kernel, seq_len), grid=(slots,), in_s...  36.4 us
    ppermute x19, starting transfers between devices, swap(): return lax.ppermute(value, axis, [(i, i ^ mask) for i in range(size)])  34.7 us
    convert_element_type x11, other arithmetic, total_of(): return sum((v.astype(jnp.float32) for v in values)).astype(jnp.bfloat16)  18.7 us
  transfers between devices with their start and end apart: 22, of which 7 were waited for; matrix products, arithmetic and copies ran while one was open for 10% of the time, Pallas kernels for 24%

profile of v3, /device:TPU:0, one launch (start us, length us, event | category | flops | bytes accessed | tf_op | source)
XLA Modules:
  0.0 599.3 jit_solution(10227447649010219953)
XLA Ops:
  18.3 105.9 %all-gather.7.cloned.1.call-done = bf16[9728,768]{1,0:T(8,128)(2,1)} async-done(((bf16[304,768]{1,0:T(8,128)(2,1)}), bf16[9728,768]{1,0:T(8,128)(2,1)}) %all-gather.7.cloned.1.call-update) | async-done | bytes 14942224 | tf_op jit(solution)/shard_map/all_gather | solution.py:636
  124.2 4.0 slice.442
  133.8 6.8 %fusion.31 = (bf16[32,96,768]{2,1,0:T(8,128)(2,1)S(1)}, bf16[32,96,768]{2,1,0:T(8,128)(2,1)}) fusion(bf16[32,304,768]{2,1,0:T(8,128)(2,1)} %bitcast.163), kind=kLoop, calls=%fused_computation.117 | loop fusion | bytes 18874368 | tf_op jit(solution)/shard_map/slice | solution.py:479
  143.8 18.4 %attn_forward.2 = (bf16[4,208,768]{2,1,0:T(8,128)(2,1)}, bf16[4,208,2304]{2,1,0:T(8,128)(2,1)}, bf16[4,12,208,208]{3,2,1,0:T(8,128)(2,1)}, bf16[4,208,768]{2,1,0:T(8,128)(2,1)}, f32[4,208,768]{2,1,0:T(8,128)}) custom-call(f32[4,208,768]{2,1,0:T(8,128)} %pad_convert_fusion.x_ref, bf16[2304,768]{1,0:T(8,128)(2,1)} %bitcast.175, bf16[768,768]{1,0:T(8,128)(2,1)} %bitcast.190, ...), custom_call_target="tpu_custom_call" | custom-call | flops 17999998976 | bytes 1048576 | tf_op jit(solution)/shard_map/attn_forward/pallas_call | solution.py:141
  162.2 25.1 %mlp_forward.2 = (bf16[4,208,768]{2,1,0:T(8,128)(2,1)}, bf16[4,208,3072]{2,1,0:T(8,128)(2,1)}, bf16[4,208,3072]{2,1,0:T(8,128)(2,1)}, f32[4,208,768]{2,1,0:T(8,128)}) custom-call(f32[4,208,768]{2,1,0:T(8,128)} %get-tuple-element.121.middle_ref, bf16[3072,768]{1,0:T(8,128)(2,1)} %bitcast.150, bf16[4,768,768]{2,1,0:T(8,128)(2,1)} %bitcast.146, ...), custom_call_target="tpu_custom_call" | custom-call | flops 24000000000 | bytes 1048576 | tf_op jit(solution)/shard_map/mlp_forward/pallas_call | solution.py:194
  187.3 45.4 %all-gather.5.cloned.1.call-done = bf16[9728,768]{1,0:T(8,128)(2,1)} async-done(((bf16[304,768]{1,0:T(8,128)(2,1)}), bf16[9728,768]{1,0:T(8,128)(2,1)}) %all-gather.5.cloned.1.call-update) | async-done | bytes 14942224 | tf_op jit(solution)/shard_map/all_gather | solution.py:636
  232.6 4.0 slice.450
  240.5 8.0 %fusion.30 = (bf16[32,96,768]{2,1,0:T(8,128)(2,1)}, bf16[32,96,768]{2,1,0:T(8,128)(2,1)}) fusion(bf16[32,304,768]{2,1,0:T(8,128)(2,1)} %bitcast.159), kind=kLoop, calls=%fused_computation.116 | loop fusion | bytes 18874368 | tf_op jit(solution)/shard_map/slice | solution.py:479
  250.4 4.8 copy.95
  255.8 18.0 %attn_forward.3 = (bf16[4,208,768]{2,1,0:T(8,128)(2,1)}, bf16[4,208,2304]{2,1,0:T(8,128)(2,1)}, bf16[4,12,208,208]{3,2,1,0:T(8,128)(2,1)}, bf16[4,208,768]{2,1,0:T(8,128)(2,1)}, f32[4,208,768]{2,1,0:T(8,128)}) custom-call(f32[4,208,768]{2,1,0:T(8,128)} %get-tuple-element.123.x_ref, bf16[2304,768]{1,0:T(8,128)(2,1)} %bitcast.164, bf16[768,768]{1,0:T(8,128)(2,1)} %bitcast.173, ...), custom_call_target="tpu_custom_call" | custom-call | flops 17999998976 | bytes 1048576 | tf_op jit(solution)/shard_map/attn_forward/pallas_call | solution.py:141
  273.9 23.9 %mlp_forward.3 = (bf16[4,208,768]{2,1,0:T(8,128)(2,1)}, bf16[4,208,3072]{2,1,0:T(8,128)(2,1)}, bf16[4,208,3072]{2,1,0:T(8,128)(2,1)}, f32[4,208,768]{2,1,0:T(8,128)}) custom-call(f32[4,208,768]{2,1,0:T(8,128)} %get-tuple-element.125.middle_ref, bf16[3072,768]{1,0:T(8,128)(2,1)} %bitcast.152, bf16[4,768,768]{2,1,0:T(8,128)(2,1)} %bitcast.148, ...), custom_call_target="tpu_custom_call" | custom-call | flops 24000000000 | bytes 1048576 | tf_op jit(solution)/shard_map/mlp_forward/pallas_call | solution.py:194
  297.8 3.2 convert_multiply_fusion
  302.8 37.6 %mlp_backward.2 = (bf16[16,192,768]{2,1,0:T(8,128)(2,1)}, bf16[16,192,768]{2,1,0:T(8,128)(2,1)}, f32[4,8,768]{2,1,0:T(8,128)}, f32[8,768]{1,0:T(8,128)}, f32[4,208,768]{2,1,0:T(8,128)}) custom-call(s32[1]{0:T(128)} %bitcast.45.me_ref, f32[4,208,768]{2,1,0:T(8,128)} %pad.45.grad_ref, f32[4,208,768]{2,1,0:T(8,128)} %get-tuple-element.125.middle_ref, ...), custom_call_target="tpu_custom_call" | custom-call | flops 1000000000 | bytes 1048576 | tf_op jit(solution)/shard_map/mlp_backward/pallas_call | solution.py:324
  342.5 29.5 %attn_backward.2 = (bf16[16,112,768]{2,1,0:T(8,128)(2,1)}, bf16[16,112,768]{2,1,0:T(8,128)(2,1)}, f32[8,768]{1,0:T(8,128)}, f32[4,208,768]{2,1,0:T(8,128)}) custom-call(s32[1]{0:T(128)} %bitcast.45.me_ref, f32[4,208,768]{2,1,0:T(8,128)} %get-tuple-element.130.grad_ref, f32[4,208,768]{2,1,0:T(8,128)} %get-tuple-element.123.x_ref, ...), custom_call_target="tpu_custom_call" | custom-call | flops 1000000000 | bytes 1048576 | tf_op jit(solution)/shard_map/attn_backward/pallas_call | solution.py:438
  374.8 4.4 add_convert_fusion.2
  384.4 37.7 %mlp_backward.3 = (bf16[32,192,768]{2,1,0:T(8,128)(2,1)}, f32[4,8,768]{2,1,0:T(8,128)}, f32[8,768]{1,0:T(8,128)}, f32[4,208,768]{2,1,0:T(8,128)}) custom-call(s32[1]{0:T(128)} %bitcast.45.me_ref, f32[4,208,768]{2,1,0:T(8,128)} %get-tuple-element.140.grad_ref, f32[4,208,768]{2,1,0:T(8,128)} %get-tuple-element.121.middle_ref, ...), custom_call_target="tpu_custom_call" | custom-call | flops 1000000000 | bytes 1048576 | tf_op jit(solution)/shard_map/mlp_backward/pallas_call | solution.py:324
  431.7 2.7 add_convert_fusion.1
  440.8 30.3 %attn_backward.3 = (bf16[16,112,768]{2,1,0:T(8,128)(2,1)}, bf16[16,112,768]{2,1,0:T(8,128)(2,1)}, f32[8,768]{1,0:T(8,128)}, f32[4,208,768]{2,1,0:T(8,128)}) custom-call(s32[1]{0:T(128)} %bitcast.45.me_ref, f32[4,208,768]{2,1,0:T(8,128)} %get-tuple-element.153.grad_ref, f32[4,208,768]{2,1,0:T(8,128)} %pad_convert_fusion.x_ref, ...), custom_call_target="tpu_custom_call" | custom-call | flops 199999995904 | bytes 1048576 | tf_op jit(solution)/shard_map/attn_backward/pallas_call | solution.py:438
  472.4 3.0 collective-permute-done.8
  490.5 29.2 %collective-permute-done.16 = bf16[1,1,1,304,768]{4,3,2,1,0:T(8,128)(2,1)S(1)} collective-permute-done((bf16[1,1,1,304,768]{4,3,2,1,0:T(8,128)(2,1)S(1)}, bf16[1,1,1,304,768]{4,3,2,1,0:T(8,128)(2,1)S(1)}, u32[]{:S(2)}, u32[]{:S(2)}) %collective-permute-start.16) | collective-permute-done | bytes 466976 | tf_op jit(solution)/shard_map/ppermute | solution.py:549
  526.2 8.3 %collective-permute-done.18 = bf16[1,1,1,304,768]{4,3,2,1,0:T(8,128)(2,1)S(1)} collective-permute-done((bf16[1,1,1,304,768]{4,3,2,1,0:T(8,128)(2,1)S(1)}, bf16[1,1,1,304,768]{4,3,2,1,0:T(8,128)(2,1)S(1)}, u32[]{:S(2)}, u32[]{:S(2)}) %collective-permute-start.18) | collective-permute-done | bytes 466976 | tf_op jit(solution)/shard_map/ppermute | solution.py:549
  542.0 15.1 %collective-permute-start.14 = (bf16[1,1,1,112,768]{4,3,2,1,0:T(8,128)(2,1)}, bf16[1,1,1,112,768]{4,3,2,1,0:T(8,128)(2,1)S(1)}, u32[]{:S(2)}, u32[]{:S(2)}) collective-permute-start(bf16[1,1,1,112,768]{4,3,2,1,0:T(8,128)(2,1)} %get-tuple-element.242), channel_id=1, source_target_pairs={{0,4},{1,5},{2,6},{3,7},{4,0},{5,1},{6,2},{7,3},{8,12},{9,13},{10,... | collective-permute-start | bytes 516104 | tf_op jit(solution)/shard_map/ppermute | solution.py:549
  559.7 9.3 %collective-permute-done.14 = bf16[1,1,1,112,768]{4,3,2,1,0:T(8,128)(2,1)S(1)} collective-permute-done((bf16[1,1,1,112,768]{4,3,2,1,0:T(8,128)(2,1)}, bf16[1,1,1,112,768]{4,3,2,1,0:T(8,128)(2,1)S(1)}, u32[]{:S(2)}, u32[]{:S(2)}) %collective-permute-start.14) | collective-permute-done | bytes 172064 | tf_op jit(solution)/shard_map/ppermute | solution.py:549
  570.1 15.4 %reduce-scatter.2.cloned.1.call-done = bf16[1,192,768]{2,1,0:T(8,128)(2,1)} async-done(((bf16[32,192,768]{2,1,0:T(8,128)(2,1)}), bf16[1,192,768]{2,1,0:T(8,128)(2,1)}) %reduce-scatter.2.cloned.1.call-update) | async-done | bytes 294928 | tf_op jit(solution)/shard_map/reduce_scatter | solution.py:696
  (242 shorter events, 93.8 us)
Async XLA Ops:
  7.2 117.0 %all-gather.7.cloned.1.call-start = ((), (), s32[]{:S(2)}) async-start(), calls=%async_computation.3 | async-start | bytes 15409152 | tf_op jit(solution)/shard_map/all_gather | solution.py:636
  14.7 217.9 %all-gather.5.cloned.1.call-start = ((), (), s32[]{:S(2)}) async-start(), calls=%async_computation.2 | async-start | bytes 15409152 | tf_op jit(solution)/shard_map/all_gather | solution.py:636
  15.7 569.7 %reduce-scatter.2.cloned.1.call-start = ((), (), s32[]{:S(2)}) async-start(), calls=%async_computation.1 | async-start | bytes 9732096 | tf_op jit(solution)/shard_map/reduce_scatter | solution.py:696
  340.4 31.7 %collective-permute-start = (bf16[16,192,768]{2,1,0:T(8,128)(2,1)}, bf16[16,192,768]{2,1,0:T(8,128)(2,1)}, u32[]{:S(2)}, u32[]{:S(2)}) collective-permute-start(bf16[16,192,768]{2,1,0:T(8,128)(2,1)} %get-tuple-element.139), channel_id=1, source_target_pairs={{0,1},{1,0},{2,3},{3,2},{4,5},{5,4},{6,7},{7,6},{8,9},{9,8},{10,11... | collective-permute-start | bytes 14155784 | tf_op jit(solution)/shard_map/ppermute | solution.py:549
  374.6 49.4 %collective-permute-start.3 = (bf16[16,112,768]{2,1,0:T(8,128)(2,1)}, bf16[16,112,768]{2,1,0:T(8,128)(2,1)}, u32[]{:S(2)}, u32[]{:S(2)}) collective-permute-start(bf16[16,112,768]{2,1,0:T(8,128)(2,1)} %constant_dynamic-update-slice_fusion.5), channel_id=1, source_target_pairs={{0,1},{1,0},{2,3},{3,2},{4,5},{5,4},{6,7},{7,6},{8,9},{9,8},{10,11... | collective-permute-start | bytes 8257544 | tf_op jit(solution)/shard_map/ppermute | solution.py:549
  380.4 43.5 %collective-permute-start.1 = (bf16[2,1,4,96,768]{4,3,2,1,0:T(8,128)(2,1)}, bf16[2,1,4,96,768]{4,3,2,1,0:T(8,128)(2,1)}, u32[]{:S(2)}, u32[]{:S(2)}) collective-permute-start(bf16[2,1,4,96,768]{4,3,2,1,0:T(8,128)(2,1)} %slice.537), channel_id=1, source_target_pairs={{0,8},{8,0},{16,24},{24,16},{1,9},{9,1},{17,25},{25,17},{2,10},{10... | collective-permute-start | bytes 3538952 | tf_op jit(solution)/shard_map/ppermute | solution.py:549
  383.0 40.9 %collective-permute-start.2 = (bf16[1,2,4,96,768]{4,3,2,1,0:T(8,128)(2,1)}, bf16[1,2,4,96,768]{4,3,2,1,0:T(8,128)(2,1)}, u32[]{:S(2)}, u32[]{:S(2)}) collective-permute-start(bf16[1,2,4,96,768]{4,3,2,1,0:T(8,128)(2,1)} %bitcast.49), channel_id=1, source_target_pairs={{0,16},{8,24},{16,0},{24,8},{1,17},{9,25},{17,1},{25,9},{2,18},{10... | collective-permute-start | bytes 3538952 | tf_op jit(solution)/shard_map/ppermute | solution.py:549
  426.4 46.0 %collective-permute-start.4 = (bf16[1,1,4,96,768]{4,3,2,1,0:T(8,128)(2,1)}, bf16[1,1,4,96,768]{4,3,2,1,0:T(8,128)(2,1)}, u32[]{:S(2)}, u32[]{:S(2)}) collective-permute-start(bf16[1,1,4,96,768]{4,3,2,1,0:T(8,128)(2,1)} %slice.545), channel_id=1, source_target_pairs={{0,16},{8,24},{16,0},{24,8},{1,17},{9,25},{17,1},{25,9},{2,18},{10... | collective-permute-start | bytes 1769480 | tf_op jit(solution)/shard_map/ppermute | solution.py:549
  430.7 41.7 %collective-permute-start.5 = (bf16[1,1,4,96,768]{4,3,2,1,0:T(8,128)(2,1)}, bf16[1,1,4,96,768]{4,3,2,1,0:T(8,128)(2,1)}, u32[]{:S(2)}, u32[]{:S(2)}) collective-permute-start(bf16[1,1,4,96,768]{4,3,2,1,0:T(8,128)(2,1)} %slice.547), channel_id=1, source_target_pairs={{0,8},{8,0},{16,24},{24,16},{1,9},{9,1},{17,25},{25,17},{2,10},{10... | collective-permute-start | bytes 1769480 | tf_op jit(solution)/shard_map/ppermute | solution.py:549
  437.3 35.1 %collective-permute-start.6 = (bf16[1,1,4,112,768]{4,3,2,1,0:T(8,128)(2,1)}, bf16[1,1,4,112,768]{4,3,2,1,0:T(8,128)(2,1)}, u32[]{:S(2)}, u32[]{:S(2)}) collective-permute-start(bf16[1,1,4,112,768]{4,3,2,1,0:T(8,128)(2,1)} %get-tuple-element.230), channel_id=1, source_target_pairs={{0,8},{8,0},{16,24},{24,16},{1,9},{9,1},{17,25},{25,17},{2,10},{10... | collective-permute-start | bytes 2064392 | tf_op jit(solution)/shard_map/ppermute | solution.py:549
  438.3 34.1 %collective-permute-start.7 = (bf16[1,1,4,112,768]{4,3,2,1,0:T(8,128)(2,1)}, bf16[1,1,4,112,768]{4,3,2,1,0:T(8,128)(2,1)}, u32[]{:S(2)}, u32[]{:S(2)}) collective-permute-start(bf16[1,1,4,112,768]{4,3,2,1,0:T(8,128)(2,1)} %get-tuple-element.229), channel_id=1, source_target_pairs={{0,16},{8,24},{16,0},{24,8},{1,17},{9,25},{17,1},{25,9},{2,18},{10... | collective-permute-start | bytes 2064392 | tf_op jit(solution)/shard_map/ppermute | solution.py:549
  439.2 36.2 %collective-permute-start.8 = (bf16[1,1,4,112,768]{4,3,2,1,0:T(8,128)(2,1)}, bf16[1,1,4,112,768]{4,3,2,1,0:T(8,128)(2,1)}, u32[]{:S(2)}, u32[]{:S(2)}) collective-permute-start(bf16[1,1,4,112,768]{4,3,2,1,0:T(8,128)(2,1)} %get-tuple-element.228), channel_id=1, source_target_pairs={{0,24},{8,16},{16,8},{24,0},{1,25},{9,17},{17,9},{25,1},{2,26},{10... | collective-permute-start | bytes 2064392 | tf_op jit(solution)/shard_map/ppermute | solution.py:549
  478.0 6.5 %collective-permute-start.9 = (bf16[16,112,768]{2,1,0:T(8,128)(2,1)}, bf16[16,112,768]{2,1,0:T(8,128)(2,1)S(1)}, u32[]{:S(2)}, u32[]{:S(2)}) collective-permute-start(bf16[16,112,768]{2,1,0:T(8,128)(2,1)} %constant_dynamic-update-slice_fusion.2), channel_id=1, source_target_pairs={{0,1},{1,0},{2,3},{3,2},{4,5},{5,4},{6,7},{7,6},{8,9},{9,8},{10,11... | collective-permute-start | bytes 8257544 | tf_op jit(solution)/shard_map/ppermute | solution.py:549
  482.7 37.1 %collective-permute-start.16 = (bf16[1,1,1,304,768]{4,3,2,1,0:T(8,128)(2,1)S(1)}, bf16[1,1,1,304,768]{4,3,2,1,0:T(8,128)(2,1)S(1)}, u32[]{:S(2)}, u32[]{:S(2)}) collective-permute-start(bf16[1,1,1,304,768]{4,3,2,1,0:T(8,128)(2,1)S(1)} %get-tuple-element.235), channel_id=1, source_target_pairs={{0,2},{1,3},{2,0},{3,1},{4,6},{5,7},{6,4},{7,5},{8,10},{9,11},{10,... | collective-permute-start | bytes 1400840 | tf_op jit(solution)/shard_map/ppermute | solution.py:549
  485.2 36.9 %copy-start.1 = (bf16[4,197,768]{2,1,0:T(8,128)(2,1)S(1)}, bf16[4,197,768]{2,1,0:T(8,128)(2,1)}, u32[]{:S(2)}) copy-start(bf16[4,197,768]{2,1,0:T(8,128)(2,1)} %get-tuple-element.258) | copy-start | bytes 3631108
  485.3 38.4 %copy-start.10 = (f32[4,208,768]{2,1,0:T(8,128)S(1)}, f32[4,208,768]{2,1,0:T(8,128)}, u32[]{:S(2)}) copy-start(f32[4,208,768]{2,1,0:T(8,128)} %get-tuple-element.166) | copy-start | bytes 7667716
  485.4 49.1 %collective-permute-start.10 = (bf16[1,1,4,112,768]{4,3,2,1,0:T(8,128)(2,1)S(1)}, bf16[1,1,4,112,768]{4,3,2,1,0:T(8,128)(2,1)S(1)}, u32[]{:S(2)}, u32[]{:S(2)}) collective-permute-start(bf16[1,1,4,112,768]{4,3,2,1,0:T(8,128)(2,1)S(1)} %get-tuple-element.227), channel_id=1, source_target_pairs={{0,8},{8,0},{16,24},{24,16},{1,9},{9,1},{17,25},{25,17},{2,10},{10... | collective-permute-start | bytes 2064392 | tf_op jit(solution)/shard_map/ppermute | solution.py:549
  487.7 46.8 %collective-permute-start.11 = (bf16[1,1,4,112,768]{4,3,2,1,0:T(8,128)(2,1)S(1)}, bf16[1,1,4,112,768]{4,3,2,1,0:T(8,128)(2,1)S(1)}, u32[]{:S(2)}, u32[]{:S(2)}) collective-permute-start(bf16[1,1,4,112,768]{4,3,2,1,0:T(8,128)(2,1)S(1)} %get-tuple-element.226), channel_id=1, source_target_pairs={{0,16},{8,24},{16,0},{24,8},{1,17},{9,25},{17,1},{25,9},{2,18},{10... | collective-permute-start | bytes 2064392 | tf_op jit(solution)/shard_map/ppermute | solution.py:549
  489.3 45.2 %collective-permute-start.12 = (bf16[1,1,4,112,768]{4,3,2,1,0:T(8,128)(2,1)S(1)}, bf16[1,1,4,112,768]{4,3,2,1,0:T(8,128)(2,1)S(1)}, u32[]{:S(2)}, u32[]{:S(2)}) collective-permute-start(bf16[1,1,4,112,768]{4,3,2,1,0:T(8,128)(2,1)S(1)} %get-tuple-element.225), channel_id=1, source_target_pairs={{0,24},{8,16},{16,8},{24,0},{1,25},{9,17},{17,9},{25,1},{2,26},{10... | collective-permute-start | bytes 2064392 | tf_op jit(solution)/shard_map/ppermute | solution.py:549
  489.3 36.9 %collective-permute-start.17 = (bf16[1,1,1,304,768]{4,3,2,1,0:T(8,128)(2,1)S(1)}, bf16[1,1,1,304,768]{4,3,2,1,0:T(8,128)(2,1)S(1)}, u32[]{:S(2)}, u32[]{:S(2)}) collective-permute-start(bf16[1,1,1,304,768]{4,3,2,1,0:T(8,128)(2,1)S(1)} %get-tuple-element.234), channel_id=1, source_target_pairs={{0,4},{1,5},{2,6},{3,7},{4,0},{5,1},{6,2},{7,3},{8,12},{9,13},{10,... | collective-permute-start | bytes 1400840 | tf_op jit(solution)/shard_map/ppermute | solution.py:549
  519.8 14.7 %collective-permute-start.18 = (bf16[1,1,1,304,768]{4,3,2,1,0:T(8,128)(2,1)S(1)}, bf16[1,1,1,304,768]{4,3,2,1,0:T(8,128)(2,1)S(1)}, u32[]{:S(2)}, u32[]{:S(2)}) collective-permute-start(bf16[1,1,1,304,768]{4,3,2,1,0:T(8,128)(2,1)S(1)} %get-tuple-element.233), channel_id=1, source_target_pairs={{0,6},{1,7},{2,4},{3,5},{4,2},{5,3},{6,0},{7,1},{8,14},{9,15},{10,... | collective-permute-start | bytes 1400840 | tf_op jit(solution)/shard_map/ppermute | solution.py:549
  539.7 20.0 %collective-permute-start.15 = (bf16[1,1,1,112,768]{4,3,2,1,0:T(8,128)(2,1)}, bf16[1,1,1,112,768]{4,3,2,1,0:T(8,128)(2,1)S(1)}, u32[]{:S(2)}, u32[]{:S(2)}) collective-permute-start(bf16[1,1,1,112,768]{4,3,2,1,0:T(8,128)(2,1)} %get-tuple-element.241), channel_id=1, source_target_pairs={{0,6},{1,7},{2,4},{3,5},{4,2},{5,3},{6,0},{7,1},{8,14},{9,15},{10,... | collective-permute-start | bytes 516104 | tf_op jit(solution)/shard_map/ppermute | solution.py:549
  542.0 27.0 %collective-permute-start.14 = (bf16[1,1,1,112,768]{4,3,2,1,0:T(8,128)(2,1)}, bf16[1,1,1,112,768]{4,3,2,1,0:T(8,128)(2,1)S(1)}, u32[]{:S(2)}, u32[]{:S(2)}) collective-permute-start(bf16[1,1,1,112,768]{4,3,2,1,0:T(8,128)(2,1)} %get-tuple-element.242), channel_id=1, source_target_pairs={{0,4},{1,5},{2,6},{3,7},{4,0},{5,1},{6,2},{7,3},{8,12},{9,13},{10,... | collective-permute-start | bytes 516104 | tf_op jit(solution)/shard_map/ppermute | solution.py:549
  557.1 11.9 %collective-permute-start.13 = (bf16[1,1,1,112,768]{4,3,2,1,0:T(8,128)(2,1)S(1)}, bf16[1,1,1,112,768]{4,3,2,1,0:T(8,128)(2,1)S(1)}, u32[]{:S(2)}, u32[]{:S(2)}) collective-permute-start(bf16[1,1,1,112,768]{4,3,2,1,0:T(8,128)(2,1)S(1)} %get-tuple-element.240), channel_id=1, source_target_pairs={{0,2},{1,3},{2,0},{3,1},{4,6},{5,7},{6,4},{7,5},{8,10},{9,11},{10,... | collective-permute-start | bytes 516104 | tf_op jit(solution)/shard_map/ppermute | solution.py:549
  (21 other events, 212.7 us)
Sparse Core Ops, SparseCore 0:
  14.8 109.3 all-gather.6
  127.8 104.7 all-gather.4
  422.3 163.1 reduce-scatter.1

commit v4 on v3

--- a/solution.py
+++ b/solution.py
@@ -146,7 +146,7 @@
         out_specs=[slot_block(o.shape) for o in outs],
         out_shape=outs,
         compiler_params=params(),
-        cost_estimate=worth(18),
+        cost_estimate=worth(1),
         name="attn_forward",
     )(state, w_qkv, w_proj, gains, biases)
 
@@ -205,7 +205,7 @@
         out_specs=[whole(middle.shape), wide_spec, wide_spec, whole(middle.shape)],
         out_shape=outs,
         compiler_params=params(),
-        cost_estimate=worth(24),
+        cost_estimate=worth(1),
         name="mlp_forward",
     )(middle, w_fc1, w_fc2, gains, biases, fc1_bias)
 
@@ -455,6 +455,65 @@
     )(me, *sliced, w_qkv, w_proj, gains)
 
 
+def spread(share, place, refs):
+    at = 0
+    for ref in refs:
+        rows = ref.shape[-2]
+        for block in range(ref.shape[0]) if len(ref.shape) == 4 else [None]:
+            piece = share[at : at + rows].astype(jnp.bfloat16)
+            at += rows
+            if block is None:
+                ref[place] = piece
+            else:
+                ref[block, place] = piece
+
+
+def unpack_kernel(blob_ref, *refs):
+    for i in range(blob_ref.shape[0]):
+        spread(blob_ref[i].astype(jnp.float32), i, refs)
+
+
+def unpack_relative_kernel(count, me_ref, *refs):
+    chips = pl.num_programs(0)
+    for i in range(count):
+        place = 2 * chips * (i // 2) + 2 * pl.program_id(0) + i % 2
+        spread(refs[i][0].astype(jnp.float32), place ^ me_ref[0], refs[count:])
+
+
+def unpack_whole(blob, shapes):
+    devices, rows, width = blob.shape
+    step = 4
+    specs = [
+        pl.BlockSpec((step, *s[1:]), lambda i: (i, 0, 0))
+        if len(s) == 3
+        else pl.BlockSpec((s[0], step, *s[2:]), lambda i: (0, i, 0, 0))
+        for s in shapes
+    ]
+    return pl.pallas_call(
+        unpack_kernel,
+        grid=(devices // step,),
+        in_specs=[pl.BlockSpec((step, rows, width), lambda i: (i, 0, 0))],
+        out_specs=specs,
+        out_shape=[jax.ShapeDtypeStruct(s, jnp.bfloat16) for s in shapes],
+        compiler_params=params(),
+        cost_estimate=worth(1),
+        name="unpack_whole",
+    )(blob)
+
+
+def unpack_relative(pieces, me, shapes):
+    return pl.pallas_call(
+        partial(unpack_relative_kernel, len(pieces)),
+        grid=(pieces[0].shape[0],),
+        in_specs=[pl.BlockSpec(memory_space=pltpu.SMEM)] + [slot_block(p.shape) for p in pieces],
+        out_specs=[whole(s) for s in shapes],
+        out_shape=[jax.ShapeDtypeStruct(s, jnp.bfloat16) for s in shapes],
+        compiler_params=params(),
+        cost_estimate=worth(1),
+        name="unpack_relative",
+    )(me, *pieces)
+
+
 AXES = ("dp", "fsdp")
 
 
@@ -479,15 +538,21 @@
     cut = blob[:, at : at + blocks * fc2[1]].reshape(devices, blocks, fc2[1], width)
     parts.append(cut.transpose(1, 0, 2, 3).reshape(blocks, devices * fc2[1], width))
     at += blocks * fc2[1]
-    small = blob[:, at:].reshape(devices, -1)
-    start = 0
-    for rows, columns in (gains, biases, fc1_bias):
+    small = unpack_small(blob[:, at:], (gains, biases, fc1_bias))
+    small[2] = small[2].reshape(blocks, 1, width)
+    return tuple(parts) + tuple(small)
+
+
+def unpack_small(small, shapes):
+    devices = small.shape[0]
+    small = small.reshape(devices, -1)
+    parts, start = [], 0
+    for rows, columns in shapes:
         piece = small[:, start : start + rows * columns].reshape(devices, rows, columns)
         piece = piece.transpose(1, 0, 2).astype(jnp.float32)
         parts.append(piece.reshape(rows, devices * columns))
         start += rows * columns
-    parts[-1] = parts[-1].reshape(blocks, 1, width)
-    return tuple(parts)
+    return parts
 
 
 def pack_grads(grads, shapes, total_rows, devices):
@@ -630,24 +695,72 @@
     me = me.astype(jnp.int32).reshape(1)
     extra = ((0, 0), (0, -seq_len % TILE_ROWS), (0, 0))
     state = jnp.pad(images.astype(jnp.float32), extra)
-    gathered = []
-    for layer_index in range(layer_count):
-        share = pack_layer(*(w[layer_index] for w in weights))
+    blocks = shapes[3][0] // width
+    every = [(layer_count * n, m) for n, m in shapes[4:]]
+    share_rows = -(-sum(n * m for n, m in every) // width)
+    share_rows = -(-share_rows // TILE_ROWS) * TILE_ROWS
+    ahead = [(devices, 3 * cut, width), (devices, cut, width)]
+    behind = [(devices, 4 * cut, width), (blocks, devices, cut, width)]
+    little = [(devices, share_rows, width)]
+
+    def attn_of(layer_index, state):
+        w_qkv, w_proj, _, _, gains, biases, _ = gathered[layer_index]
+        return (state, *attn_forward(state, w_qkv, w_proj, gains, biases, seq_len))
+
+    def mlp_of(layer_index, middle):
+        _, _, w_fc1, w_fc2, gains, biases, fc1_bias = gathered[layer_index]
+        return mlp_forward(middle, w_fc1, w_fc2, gains, biases, fc1_bias)
+
+    shares = [pack_layer(*(w[i] for w in weights)) for i in range(layer_count)]
+    share = shares[0]
+    if direct:
+        row = jnp.concatenate([w.reshape(1, -1) for w in weights[4:]], 1)
+        row = jnp.pad(row, ((0, 0), (0, share_rows * width - row.shape[1])))
+        share = jnp.concatenate([share[: 12 * cut], row.reshape(-1, width)], 0)
         blob = lax.all_gather(share, AXES, axis=0, tiled=False)
-        gathered.append(blob)
-    kept = []
-    for layer_index in range(layer_count):
-        blob, state = lax.optimization_barrier((gathered[layer_index], state))
-        gathered[layer_index] = unpack_layer(blob, shapes)
-        w_qkv, w_proj, w_fc1, w_fc2, gains, biases, fc1_bias = gathered[layer_index]
-        normed_one, mixed, probs, attended, middle = attn_forward(
-            state, w_qkv, w_proj, gains, biases, seq_len
-        )
-        normed_two, hidden, slope, final = mlp_forward(
-            middle, w_fc1, w_fc2, gains, biases, fc1_bias
-        )
-        kept.append((state, normed_one, mixed, probs, attended, middle, normed_two, hidden, slope))
-        state = final
+        late = shares[1][4 * cut : 12 * cut]
+        blob_one = lax.all_gather(shares[1][: 4 * cut], AXES, axis=0, tiled=False)
+        blob, late = lax.optimization_barrier((blob, late))
+        rows = [late] + [swap(late, "fsdp", 2 * i, fsdp_size) for i in range(1, fsdp_size // 2)]
+        *parts, small = unpack_whole(blob, ahead + behind + little)
+        parts = [v.reshape(-1, width) for v in parts[:3]] + [parts[3].reshape(blocks, -1, width)]
+        little_all = unpack_small(small, every)
+        little_of = [
+            [v[i * n : (i + 1) * n] for v, (n, _) in zip(little_all, shapes[4:])]
+            for i in range(layer_count)
+        ]
+        for i in range(layer_count):
+            little_of[i][2] = little_of[i][2].reshape(blocks, 1, width)
+        parts, little_of = lax.optimization_barrier((parts, little_of))
+        gathered = [(*parts, *little_of[0]), None]
+        *saved, middle = attn_of(0, state)
+        middle, rows = lax.optimization_barrier((middle, rows))
+        rows = jnp.stack(rows)
+        near = [rows] + [swap(rows, "dp", i, dp_size) for i in range(1, dp_size)]
+        *more, final = mlp_of(0, middle)
+        kept = [(*saved, middle, *more)]
+        blob_one, final = lax.optimization_barrier((blob_one, final))
+        w_qkv, w_proj = unpack_whole(blob_one, ahead)
+        w_qkv, near = lax.optimization_barrier((w_qkv, near))
+        pieces = [v for n in near for v in (n, swap(n, "fsdp", 1, fsdp_size))]
+        w_qkv, w_proj = w_qkv.reshape(-1, width), w_proj.reshape(-1, width)
+        gathered[1] = (w_qkv, w_proj, None, None, *little_of[1])
+        *saved, middle = attn_of(1, final)
+        middle, pieces = lax.optimization_barrier((middle, pieces))
+        w_fc1, w_fc2 = unpack_relative(pieces, me, behind)
+        w_fc1, w_fc2 = w_fc1.reshape(-1, width), w_fc2.reshape(blocks, -1, width)
+        gathered[1] = (w_qkv, w_proj, w_fc1, w_fc2, *gathered[1][4:])
+        *more, state = mlp_of(1, middle)
+        kept.append((*saved, middle, *more))
+    else:
+        gathered = [lax.all_gather(v, AXES, axis=0, tiled=False) for v in shares]
+        kept = []
+        for layer_index in range(layer_count):
+            blob, state = lax.optimization_barrier((gathered[layer_index], state))
+            gathered[layer_index] = unpack_layer(blob, shapes)
+            *saved, middle = attn_of(layer_index, state)
+            *more, state = mlp_of(layer_index, middle)
+            kept.append((*saved, middle, *more))
     block_output = (state[:, :seq_len] * live).astype(jnp.bfloat16)
     grad_state = jnp.pad(cotangent.astype(jnp.float32) * live, extra)
     layer_grads = [None] * layer_count

time: 603 us -> 585 us (0.970)
  local copies, waits for them, and re-layouts: 79.5 us -> 42.5 us
  Pallas kernels: 221 us -> 246 us
  waiting for transfers between devices: 217 us -> 195 us
  starting transfers between devices: 34.8 us -> 43.6 us
    all_gather x2 -> x1, waiting for transfers between devices: 151 us -> 107 us  [on_device(): blob = lax.all_gather(share, AXES, axis=0, tiled=False)]
    pallas_call x0 -> x3, Pallas kernels: none -> 27.4 us  [the longest x2 19.4 us: unpack_whole(): pl.pallas_call(unpack_kernel, grid=(devices // step,), in_specs=[pl.Block...]
    slice x10 -> x13, local copies, waits for them, and re-layouts: 31.4 us -> 4.18 us  [the longest x11 3.1 us: on_device(): v[i * n:(i + 1) * n]]
    ppermute x19 -> x29, waiting for transfers between devices: 49.9 us -> 65.6 us  [swap(): return lax.ppermute(value, axis, [(i, i ^ mask) for i in range(size)])]
    all_gather x0 -> x1, waiting for transfers between devices: none -> 13.7 us  [on_device(): blob_one = lax.all_gather(shares[1][:4 * cut], AXES, axis=0, tiled=False)]
    ppermute x19 -> x29, starting transfers between devices: 34.7 us -> 43.4 us  [swap(): return lax.ppermute(value, axis, [(i, i ^ mask) for i in range(size)])]
    reshape x16 -> x6, local copies, waits for them, and re-layouts: 10.7 us -> 3 us  [the longest x3 1.59 us: on_device(): row = jnp.concatenate([w.reshape(1, -1) for w in weights[4:]], 1)]
    reduce_scatter x1, waiting for transfers between devices: 15.4 us -> 9.3 us  [on_device(): lax.psum_scatter(shares[0], AXES, scatter_dimension=0, tiled=False)]
  transfers between devices with their start and end apart: 22 -> 32, of which waited for: 7 -> 8; matrix products, arithmetic and copies ran while one was open for 10% -> 9% of each run, Pallas kernels for 24% -> 31%
where the time goes in v4:
time: 585 us; the launch traced here: 576 us
  Pallas kernels  246 us (42%)
  waiting for transfers between devices  195 us (33%)
  starting transfers between devices  43.6 us (7%)
  local copies, waits for them, and re-layouts  42.5 us (7%)
  other arithmetic  31.8 us (5%)
  between operations  15.6 us (3%)
    all_gather x1, waiting for transfers between devices, on_device(): blob = lax.all_gather(share, AXES, axis=0, tiled=False)  107 us
    pallas_call x2, Pallas kernels, mlp_backward(): pl.pallas_call(partial(mlp_backward_kernel, mode, cut), grid=(blocks,), i...  75.2 us
    ppermute x29, waiting for transfers between devices, swap(): return lax.ppermute(value, axis, [(i, i ^ mask) for i in range(size)])  65.6 us
    pallas_call x2, Pallas kernels, attn_backward(): pl.pallas_call(partial(attn_backward_kernel, mode, cut), grid=(slots,), i...  59.8 us
    pallas_call x2, Pallas kernels, mlp_forward(): pl.pallas_call(mlp_forward_kernel, grid=(blocks,), in_specs=[whole(middle...  47.8 us
    ppermute x29, starting transfers between devices, swap(): return lax.ppermute(value, axis, [(i, i ^ mask) for i in range(size)])  43.4 us
    pallas_call x2, Pallas kernels, attn_forward(): pl.pallas_call(partial(attn_forward_kernel, seq_len), grid=(slots,), in_s...  36.2 us
    pallas_call x2, Pallas kernels, unpack_whole(): pl.pallas_call(unpack_kernel, grid=(devices // step,), in_specs=[pl.Block...  19.4 us
  transfers between devices with their start and end apart: 32, of which 8 were waited for; matrix products, arithmetic and copies ran while one was open for 9% of the time, Pallas kernels for 31%

profile of v4, /device:TPU:0, one launch (start us, length us, event | category | flops | bytes accessed | tf_op | source)
XLA Modules:
  0.0 575.8 jit_solution(9014479556326934584)
XLA Ops:
  17.2 106.7 %all-gather.7.cloned.1.call-done = bf16[9728,768]{1,0:T(8,128)(2,1)} async-done(((bf16[304,768]{1,0:T(8,128)(2,1)}), bf16[9728,768]{1,0:T(8,128)(2,1)}) %all-gather.7.cloned.1.call-update) | async-done | bytes 14942224 | tf_op jit(solution)/shard_map/all_gather | solution.py:720
  128.3 12.6 %unpack_whole.2 = (bf16[32,72,768]{2,1,0:T(8,128)(2,1)}, bf16[32,24,768]{2,1,0:T(8,128)(2,1)}, bf16[32,96,768]{2,1,0:T(8,128)(2,1)}, bf16[4,32,24,768]{3,2,1,0:T(8,128)(2,1)}, bf16[32,16,768]{2,1,0:T(8,128)(2,1)}) custom-call(bf16[32,304,768]{2,1,0:T(8,128)(2,1)} %bitcast.146), custom_call_target="tpu_custom_call" | custom-call | flops 1000000000 | bytes 1048576 | tf_op jit(solution)/shard_map/unpack_whole/pallas_call | solution.py:492
  147.2 18.1 %attn_forward.2 = (bf16[4,208,768]{2,1,0:T(8,128)(2,1)}, bf16[4,208,2304]{2,1,0:T(8,128)(2,1)}, bf16[4,12,208,208]{3,2,1,0:T(8,128)(2,1)}, bf16[4,208,768]{2,1,0:T(8,128)(2,1)}, f32[4,208,768]{2,1,0:T(8,128)}) custom-call(f32[4,208,768]{2,1,0:T(8,128)} %pad_convert_fusion.x_ref, bf16[2304,768]{1,0:T(8,128)(2,1)} %bitcast.159, bf16[768,768]{1,0:T(8,128)(2,1)} %bitcast.175, ...), custom_call_target="tpu_custom_call" | custom-call | flops 1000000000 | bytes 1048576 | tf_op jit(solution)/shard_map/attn_forward/pallas_call | solution.py:141
  169.0 23.9 %mlp_forward.2 = (bf16[4,208,768]{2,1,0:T(8,128)(2,1)}, bf16[4,208,3072]{2,1,0:T(8,128)(2,1)}, bf16[4,208,3072]{2,1,0:T(8,128)(2,1)}, f32[4,208,768]{2,1,0:T(8,128)}) custom-call(f32[4,208,768]{2,1,0:T(8,128)} %get-tuple-element.169.middle_ref, bf16[3072,768]{1,0:T(8,128)(2,1)} %bitcast.138, bf16[4,768,768]{2,1,0:T(8,128)(2,1)} %bitcast.140, ...), custom_call_target="tpu_custom_call" | custom-call | flops 1000000000 | bytes 1048576 | tf_op jit(solution)/shard_map/mlp_forward/pallas_call | solution.py:194
  192.9 13.7 %all-gather.5.cloned.1.call-done = bf16[3072,768]{1,0:T(8,128)(2,1)} async-done(((bf16[96,768]{1,0:T(8,128)(2,1)}), bf16[3072,768]{1,0:T(8,128)(2,1)}) %all-gather.5.cloned.1.call-update) | async-done | bytes 4718608 | tf_op jit(solution)/shard_map/all_gather | solution.py:722
  206.6 6.8 %unpack_whole.3 = (bf16[32,72,768]{2,1,0:T(8,128)(2,1)}, bf16[32,24,768]{2,1,0:T(8,128)(2,1)}) custom-call(bf16[32,96,768]{2,1,0:T(8,128)(2,1)} %bitcast.155), custom_call_target="tpu_custom_call" | custom-call | flops 1000000000 | bytes 1048576 | tf_op jit(solution)/shard_map/unpack_whole/pallas_call | solution.py:492
  213.4 14.2 %collective-permute-done.4.refs_4_ = bf16[4,192,768]{2,1,0:T(8,128)(2,1)S(1)} collective-permute-done((bf16[4,192,768]{2,1,0:T(8,128)(2,1)S(1)}, bf16[4,192,768]{2,1,0:T(8,128)(2,1)S(1)}, u32[]{:S(2)}, u32[]{:S(2)}) %collective-permute-start.4) | collective-permute-done | bytes 1179680 | tf_op jit(solution)/shard_map/ppermute | solution.py:614
  229.4 18.2 %attn_forward.3 = (bf16[4,208,768]{2,1,0:T(8,128)(2,1)}, bf16[4,208,2304]{2,1,0:T(8,128)(2,1)}, bf16[4,12,208,208]{3,2,1,0:T(8,128)(2,1)}, bf16[4,208,768]{2,1,0:T(8,128)(2,1)}, f32[4,208,768]{2,1,0:T(8,128)}) custom-call(f32[4,208,768]{2,1,0:T(8,128)} %get-tuple-element.174.x_ref, bf16[2304,768]{1,0:T(8,128)(2,1)} %bitcast.147, bf16[768,768]{1,0:T(8,128)(2,1)} %bitcast.157, ...), custom_call_target="tpu_custom_call" | custom-call | flops 1000000000 | bytes 1048576 | tf_op jit(solution)/shard_map/attn_forward/pallas_call | solution.py:141
  247.6 8.0 %unpack_relative.1 = (bf16[32,96,768]{2,1,0:T(8,128)(2,1)}, bf16[4,32,24,768]{3,2,1,0:T(8,128)(2,1)}) custom-call(s32[1]{0:T(128)} %bitcast.37.me_ref, bf16[4,192,768]{2,1,0:T(8,128)(2,1)} %copy-done.2, bf16[4,192,768]{2,1,0:T(8,128)(2,1)} %collective-permute-done.6.refs_1_, bf16[4,192,768]{2,1,0:T(8,128)(2,1)} %copy-done.14, ...), custom_call_target="tpu_custom_call" | custom-call | flops 1000000000 | bytes 1048576 | tf_op jit(solution)/shard_map/unpack_relative/pallas_call | solution.py:505
  255.6 23.9 %mlp_forward.3 = (bf16[4,208,768]{2,1,0:T(8,128)(2,1)}, bf16[4,208,3072]{2,1,0:T(8,128)(2,1)}, bf16[4,208,3072]{2,1,0:T(8,128)(2,1)}, f32[4,208,768]{2,1,0:T(8,128)}) custom-call(f32[4,208,768]{2,1,0:T(8,128)} %get-tuple-element.190.middle_ref, bf16[3072,768]{1,0:T(8,128)(2,1)} %bitcast.142, bf16[4,768,768]{2,1,0:T(8,128)(2,1)} %bitcast.144, ...), custom_call_target="tpu_custom_call" | custom-call | flops 1000000000 | bytes 1048576 | tf_op jit(solution)/shard_map/mlp_forward/pallas_call | solution.py:194
  279.5 3.1 convert_multiply_fusion
  284.4 37.6 %mlp_backward.2 = (bf16[16,192,768]{2,1,0:T(8,128)(2,1)}, bf16[16,192,768]{2,1,0:T(8,128)(2,1)}, f32[4,8,768]{2,1,0:T(8,128)}, f32[8,768]{1,0:T(8,128)}, f32[4,208,768]{2,1,0:T(8,128)}) custom-call(s32[1]{0:T(128)} %bitcast.37.me_ref, f32[4,208,768]{2,1,0:T(8,128)} %pad.35.grad_ref, f32[4,208,768]{2,1,0:T(8,128)} %get-tuple-element.190.middle_ref, ...), custom_call_target="tpu_custom_call" | custom-call | flops 1000000000 | bytes 1048576 | tf_op jit(solution)/shard_map/mlp_backward/pallas_call | solution.py:324
  323.9 29.5 %attn_backward.2 = (bf16[16,112,768]{2,1,0:T(8,128)(2,1)}, bf16[16,112,768]{2,1,0:T(8,128)(2,1)}, f32[8,768]{1,0:T(8,128)}, f32[4,208,768]{2,1,0:T(8,128)}) custom-call(s32[1]{0:T(128)} %bitcast.37.me_ref, f32[4,208,768]{2,1,0:T(8,128)} %get-tuple-element.206.grad_ref, f32[4,208,768]{2,1,0:T(8,128)} %get-tuple-element.174.x_ref, ...), custom_call_target="tpu_custom_call" | custom-call | flops 1000000000 | bytes 1048576 | tf_op jit(solution)/shard_map/attn_backward/pallas_call | solution.py:438
  356.4 4.4 add_convert_fusion.2
  366.0 37.7 %mlp_backward.3 = (bf16[32,192,768]{2,1,0:T(8,128)(2,1)}, f32[4,8,768]{2,1,0:T(8,128)}, f32[8,768]{1,0:T(8,128)}, f32[4,208,768]{2,1,0:T(8,128)}) custom-call(s32[1]{0:T(128)} %bitcast.37.me_ref, f32[4,208,768]{2,1,0:T(8,128)} %get-tuple-element.216.grad_ref, f32[4,208,768]{2,1,0:T(8,128)} %get-tuple-element.169.middle_ref, ...), custom_call_target="tpu_custom_call" | custom-call | flops 1000000000 | bytes 1048576 | tf_op jit(solution)/shard_map/mlp_backward/pallas_call | solution.py:324
  413.0 2.7 add_convert_fusion.1
  422.1 30.3 %attn_backward.3 = (bf16[16,112,768]{2,1,0:T(8,128)(2,1)}, bf16[16,112,768]{2,1,0:T(8,128)(2,1)}, f32[8,768]{1,0:T(8,128)}, f32[4,208,768]{2,1,0:T(8,128)}) custom-call(s32[1]{0:T(128)} %bitcast.37.me_ref, f32[4,208,768]{2,1,0:T(8,128)} %get-tuple-element.229.grad_ref, f32[4,208,768]{2,1,0:T(8,128)} %pad_convert_fusion.x_ref, ...), custom_call_target="tpu_custom_call" | custom-call | flops 199999995904 | bytes 1048576 | tf_op jit(solution)/shard_map/attn_backward/pallas_call | solution.py:438
  453.5 3.2 collective-permute-done.18
  466.4 2.5 collective-permute-start.21
  470.0 31.6 %collective-permute-done.26 = bf16[1,1,1,304,768]{4,3,2,1,0:T(8,128)(2,1)S(1)} collective-permute-done((bf16[1,1,1,304,768]{4,3,2,1,0:T(8,128)(2,1)S(1)}, bf16[1,1,1,304,768]{4,3,2,1,0:T(8,128)(2,1)S(1)}, u32[]{:S(2)}, u32[]{:S(2)}) %collective-permute-start.26) | collective-permute-done | bytes 466976 | tf_op jit(solution)/shard_map/ppermute | solution.py:614
  508.0 8.3 %collective-permute-done.28 = bf16[1,1,1,304,768]{4,3,2,1,0:T(8,128)(2,1)S(1)} collective-permute-done((bf16[1,1,1,304,768]{4,3,2,1,0:T(8,128)(2,1)S(1)}, bf16[1,1,1,304,768]{4,3,2,1,0:T(8,128)(2,1)S(1)}, u32[]{:S(2)}, u32[]{:S(2)}) %collective-permute-start.28) | collective-permute-done | bytes 466976 | tf_op jit(solution)/shard_map/ppermute | solution.py:614
  524.0 16.7 %collective-permute-start.24 = (bf16[1,1,1,112,768]{4,3,2,1,0:T(8,128)(2,1)}, bf16[1,1,1,112,768]{4,3,2,1,0:T(8,128)(2,1)S(1)}, u32[]{:S(2)}, u32[]{:S(2)}) collective-permute-start(bf16[1,1,1,112,768]{4,3,2,1,0:T(8,128)(2,1)} %get-tuple-element.305), channel_id=1, source_target_pairs={{0,4},{1,5},{2,6},{3,7},{4,0},{5,1},{6,2},{7,3},{8,12},{9,13},{10,... | collective-permute-start | bytes 516104 | tf_op jit(solution)/shard_map/ppermute | solution.py:614
  543.3 8.2 %collective-permute-done.24 = bf16[1,1,1,112,768]{4,3,2,1,0:T(8,128)(2,1)S(1)} collective-permute-done((bf16[1,1,1,112,768]{4,3,2,1,0:T(8,128)(2,1)}, bf16[1,1,1,112,768]{4,3,2,1,0:T(8,128)(2,1)S(1)}, u32[]{:S(2)}, u32[]{:S(2)}) %collective-permute-start.24) | collective-permute-done | bytes 172064 | tf_op jit(solution)/shard_map/ppermute | solution.py:614
  552.6 9.3 %reduce-scatter.2.cloned.1.call-done = bf16[1,192,768]{2,1,0:T(8,128)(2,1)} async-done(((bf16[32,192,768]{2,1,0:T(8,128)(2,1)}), bf16[1,192,768]{2,1,0:T(8,128)(2,1)}) %reduce-scatter.2.cloned.1.call-update) | async-done | bytes 294928 | tf_op jit(solution)/shard_map/reduce_scatter | solution.py:809
  (262 shorter events, 88.9 us)
Async XLA Ops:
  7.2 116.7 %all-gather.7.cloned.1.call-start = ((), (), s32[]{:S(2)}) async-start(), calls=%async_computation.3 | async-start | bytes 15409152 | tf_op jit(solution)/shard_map/all_gather | solution.py:720
  14.4 192.2 %all-gather.5.cloned.1.call-start = ((), (), s32[]{:S(2)}) async-start(), calls=%async_computation.2 | async-start | bytes 4866048 | tf_op jit(solution)/shard_map/all_gather | solution.py:722
  15.2 546.7 %reduce-scatter.2.cloned.1.call-start = ((), (), s32[]{:S(2)}) async-start(), calls=%async_computation.1 | async-start | bytes 9732096 | tf_op jit(solution)/shard_map/reduce_scatter | solution.py:809
  123.9 41.4 %collective-permute-start = (bf16[192,768]{1,0:T(8,128)(2,1)S(1)}, bf16[192,768]{1,0:T(8,128)(2,1)S(1)}, u32[]{:S(2)}, u32[]{:S(2)}) collective-permute-start(bf16[192,768]{1,0:T(8,128)(2,1)S(1)} %pad_maximum_fusion.5), channel_id=1, source_target_pairs={{0,2},{1,3},{2,0},{3,1},{4,6},{5,7},{6,4},{7,5},{8,10},{9,11},{10,... | collective-permute-start | bytes 884744 | tf_op jit(solution)/shard_map/ppermute | solution.py:614
  124.4 40.8 %collective-permute-start.1 = (bf16[192,768]{1,0:T(8,128)(2,1)S(1)}, bf16[192,768]{1,0:T(8,128)(2,1)S(1)}, u32[]{:S(2)}, u32[]{:S(2)}) collective-permute-start(bf16[192,768]{1,0:T(8,128)(2,1)S(1)} %pad_maximum_fusion.5), channel_id=1, source_target_pairs={{0,4},{1,5},{2,6},{3,7},{4,0},{5,1},{6,2},{7,3},{8,12},{9,13},{10,... | collective-permute-start | bytes 884744 | tf_op jit(solution)/shard_map/ppermute | solution.py:614
  125.9 39.4 %collective-permute-start.2 = (bf16[192,768]{1,0:T(8,128)(2,1)S(1)}, bf16[192,768]{1,0:T(8,128)(2,1)S(1)}, u32[]{:S(2)}, u32[]{:S(2)}) collective-permute-start(bf16[192,768]{1,0:T(8,128)(2,1)S(1)} %pad_maximum_fusion.5), channel_id=1, source_target_pairs={{0,6},{1,7},{2,4},{3,5},{4,2},{5,3},{6,0},{7,1},{8,14},{9,15},{10,... | collective-permute-start | bytes 884744 | tf_op jit(solution)/shard_map/ppermute | solution.py:614
  165.4 48.0 %collective-permute-start.3 = (bf16[4,192,768]{2,1,0:T(8,128)(2,1)S(1)}, bf16[4,192,768]{2,1,0:T(8,128)(2,1)S(1)}, u32[]{:S(2)}, u32[]{:S(2)}) collective-permute-start(bf16[4,192,768]{2,1,0:T(8,128)(2,1)S(1)} %pad_maximum_fusion.1.refs_0_), channel_id=1, source_target_pairs={{0,8},{8,0},{16,24},{24,16},{1,9},{9,1},{17,25},{25,17},{2,10},{10... | collective-permute-start | bytes 3538952 | tf_op jit(solution)/shard_map/ppermute | solution.py:614
  166.9 60.7 %collective-permute-start.4 = (bf16[4,192,768]{2,1,0:T(8,128)(2,1)S(1)}, bf16[4,192,768]{2,1,0:T(8,128)(2,1)S(1)}, u32[]{:S(2)}, u32[]{:S(2)}) collective-permute-start(bf16[4,192,768]{2,1,0:T(8,128)(2,1)S(1)} %pad_maximum_fusion.1.refs_0_), channel_id=1, source_target_pairs={{0,16},{8,24},{16,0},{24,8},{1,17},{9,25},{17,1},{25,9},{2,18},{10... | collective-permute-start | bytes 3538952 | tf_op jit(solution)/shard_map/ppermute | solution.py:614
  167.5 60.1 %collective-permute-start.5 = (bf16[4,192,768]{2,1,0:T(8,128)(2,1)S(1)}, bf16[4,192,768]{2,1,0:T(8,128)(2,1)}, u32[]{:S(2)}, u32[]{:S(2)}) collective-permute-start(bf16[4,192,768]{2,1,0:T(8,128)(2,1)S(1)} %pad_maximum_fusion.1.refs_0_), channel_id=1, source_target_pairs={{0,24},{8,16},{16,8},{24,0},{1,25},{9,17},{17,9},{25,1},{2,26},{10... | collective-permute-start | bytes 3538952 | tf_op jit(solution)/shard_map/ppermute | solution.py:614
  321.9 31.5 %collective-permute-start.10 = (bf16[16,192,768]{2,1,0:T(8,128)(2,1)}, bf16[16,192,768]{2,1,0:T(8,128)(2,1)}, u32[]{:S(2)}, u32[]{:S(2)}) collective-permute-start(bf16[16,192,768]{2,1,0:T(8,128)(2,1)} %get-tuple-element.215), channel_id=1, source_target_pairs={{0,1},{1,0},{2,3},{3,2},{4,5},{5,4},{6,7},{7,6},{8,9},{9,8},{10,11... | collective-permute-start | bytes 14155784 | tf_op jit(solution)/shard_map/ppermute | solution.py:614
  356.0 49.5 %collective-permute-start.13 = (bf16[16,112,768]{2,1,0:T(8,128)(2,1)}, bf16[16,112,768]{2,1,0:T(8,128)(2,1)}, u32[]{:S(2)}, u32[]{:S(2)}) collective-permute-start(bf16[16,112,768]{2,1,0:T(8,128)(2,1)} %constant_dynamic-update-slice_fusion.5), channel_id=1, source_target_pairs={{0,1},{1,0},{2,3},{3,2},{4,5},{5,4},{6,7},{7,6},{8,9},{9,8},{10,11... | collective-permute-start | bytes 8257544 | tf_op jit(solution)/shard_map/ppermute | solution.py:614
  361.9 43.5 %collective-permute-start.11 = (bf16[2,1,4,96,768]{4,3,2,1,0:T(8,128)(2,1)}, bf16[2,1,4,96,768]{4,3,2,1,0:T(8,128)(2,1)}, u32[]{:S(2)}, u32[]{:S(2)}) collective-permute-start(bf16[2,1,4,96,768]{4,3,2,1,0:T(8,128)(2,1)} %slice.516), channel_id=1, source_target_pairs={{0,8},{8,0},{16,24},{24,16},{1,9},{9,1},{17,25},{25,17},{2,10},{10... | collective-permute-start | bytes 3538952 | tf_op jit(solution)/shard_map/ppermute | solution.py:614
  363.7 41.8 %collective-permute-start.12 = (bf16[1,2,4,96,768]{4,3,2,1,0:T(8,128)(2,1)}, bf16[1,2,4,96,768]{4,3,2,1,0:T(8,128)(2,1)}, u32[]{:S(2)}, u32[]{:S(2)}) collective-permute-start(bf16[1,2,4,96,768]{4,3,2,1,0:T(8,128)(2,1)} %bitcast.42), channel_id=1, source_target_pairs={{0,16},{8,24},{16,0},{24,8},{1,17},{9,25},{17,1},{25,9},{2,18},{10... | collective-permute-start | bytes 3538952 | tf_op jit(solution)/shard_map/ppermute | solution.py:614
  407.9 45.6 %collective-permute-start.14 = (bf16[1,1,4,96,768]{4,3,2,1,0:T(8,128)(2,1)}, bf16[1,1,4,96,768]{4,3,2,1,0:T(8,128)(2,1)}, u32[]{:S(2)}, u32[]{:S(2)}) collective-permute-start(bf16[1,1,4,96,768]{4,3,2,1,0:T(8,128)(2,1)} %slice.524), channel_id=1, source_target_pairs={{0,16},{8,24},{16,0},{24,8},{1,17},{9,25},{17,1},{25,9},{2,18},{10... | collective-permute-start | bytes 1769480 | tf_op jit(solution)/shard_map/ppermute | solution.py:614
  411.5 42.0 %collective-permute-start.15 = (bf16[1,1,4,96,768]{4,3,2,1,0:T(8,128)(2,1)}, bf16[1,1,4,96,768]{4,3,2,1,0:T(8,128)(2,1)}, u32[]{:S(2)}, u32[]{:S(2)}) collective-permute-start(bf16[1,1,4,96,768]{4,3,2,1,0:T(8,128)(2,1)} %slice.526), channel_id=1, source_target_pairs={{0,8},{8,0},{16,24},{24,16},{1,9},{9,1},{17,25},{25,17},{2,10},{10... | collective-permute-start | bytes 1769480 | tf_op jit(solution)/shard_map/ppermute | solution.py:614
  418.6 34.9 %collective-permute-start.16 = (bf16[1,1,4,112,768]{4,3,2,1,0:T(8,128)(2,1)}, bf16[1,1,4,112,768]{4,3,2,1,0:T(8,128)(2,1)}, u32[]{:S(2)}, u32[]{:S(2)}) collective-permute-start(bf16[1,1,4,112,768]{4,3,2,1,0:T(8,128)(2,1)} %get-tuple-element.293), channel_id=1, source_target_pairs={{0,8},{8,0},{16,24},{24,16},{1,9},{9,1},{17,25},{25,17},{2,10},{10... | collective-permute-start | bytes 2064392 | tf_op jit(solution)/shard_map/ppermute | solution.py:614
  419.1 34.4 %collective-permute-start.17 = (bf16[1,1,4,112,768]{4,3,2,1,0:T(8,128)(2,1)}, bf16[1,1,4,112,768]{4,3,2,1,0:T(8,128)(2,1)}, u32[]{:S(2)}, u32[]{:S(2)}) collective-permute-start(bf16[1,1,4,112,768]{4,3,2,1,0:T(8,128)(2,1)} %get-tuple-element.292), channel_id=1, source_target_pairs={{0,16},{8,24},{16,0},{24,8},{1,17},{9,25},{17,1},{25,9},{2,18},{10... | collective-permute-start | bytes 2064392 | tf_op jit(solution)/shard_map/ppermute | solution.py:614
  420.6 36.1 %collective-permute-start.18 = (bf16[1,1,4,112,768]{4,3,2,1,0:T(8,128)(2,1)}, bf16[1,1,4,112,768]{4,3,2,1,0:T(8,128)(2,1)}, u32[]{:S(2)}, u32[]{:S(2)}) collective-permute-start(bf16[1,1,4,112,768]{4,3,2,1,0:T(8,128)(2,1)} %get-tuple-element.291), channel_id=1, source_target_pairs={{0,24},{8,16},{16,8},{24,0},{1,25},{9,17},{17,9},{25,1},{2,26},{10... | collective-permute-start | bytes 2064392 | tf_op jit(solution)/shard_map/ppermute | solution.py:614
  463.2 38.4 %collective-permute-start.26 = (bf16[1,1,1,304,768]{4,3,2,1,0:T(8,128)(2,1)S(1)}, bf16[1,1,1,304,768]{4,3,2,1,0:T(8,128)(2,1)S(1)}, u32[]{:S(2)}, u32[]{:S(2)}) collective-permute-start(bf16[1,1,1,304,768]{4,3,2,1,0:T(8,128)(2,1)S(1)} %get-tuple-element.298), channel_id=1, source_target_pairs={{0,2},{1,3},{2,0},{3,1},{4,6},{5,7},{6,4},{7,5},{8,10},{9,11},{10,... | collective-permute-start | bytes 1400840 | tf_op jit(solution)/shard_map/ppermute | solution.py:614
  465.9 50.4 %collective-permute-start.20 = (bf16[1,1,4,112,768]{4,3,2,1,0:T(8,128)(2,1)S(1)}, bf16[1,1,4,112,768]{4,3,2,1,0:T(8,128)(2,1)S(1)}, u32[]{:S(2)}, u32[]{:S(2)}) collective-permute-start(bf16[1,1,4,112,768]{4,3,2,1,0:T(8,128)(2,1)S(1)} %get-tuple-element.290), channel_id=1, source_target_pairs={{0,8},{8,0},{16,24},{24,16},{1,9},{9,1},{17,25},{25,17},{2,10},{10... | collective-permute-start | bytes 2064392 | tf_op jit(solution)/shard_map/ppermute | solution.py:614
  466.4 49.8 %collective-permute-start.21 = (bf16[1,1,4,112,768]{4,3,2,1,0:T(8,128)(2,1)S(1)}, bf16[1,1,4,112,768]{4,3,2,1,0:T(8,128)(2,1)S(1)}, u32[]{:S(2)}, u32[]{:S(2)}) collective-permute-start(bf16[1,1,4,112,768]{4,3,2,1,0:T(8,128)(2,1)S(1)} %get-tuple-element.289), channel_id=1, source_target_pairs={{0,16},{8,24},{16,0},{24,8},{1,17},{9,25},{17,1},{25,9},{2,18},{10... | collective-permute-start | bytes 2064392 | tf_op jit(solution)/shard_map/ppermute | solution.py:614
  469.0 47.3 %collective-permute-start.22 = (bf16[1,1,4,112,768]{4,3,2,1,0:T(8,128)(2,1)S(1)}, bf16[1,1,4,112,768]{4,3,2,1,0:T(8,128)(2,1)S(1)}, u32[]{:S(2)}, u32[]{:S(2)}) collective-permute-start(bf16[1,1,4,112,768]{4,3,2,1,0:T(8,128)(2,1)S(1)} %get-tuple-element.288), channel_id=1, source_target_pairs={{0,24},{8,16},{16,8},{24,0},{1,25},{9,17},{17,9},{25,1},{2,26},{10... | collective-permute-start | bytes 2064392 | tf_op jit(solution)/shard_map/ppermute | solution.py:614
  469.4 38.5 %collective-permute-start.27 = (bf16[1,1,1,304,768]{4,3,2,1,0:T(8,128)(2,1)S(1)}, bf16[1,1,1,304,768]{4,3,2,1,0:T(8,128)(2,1)S(1)}, u32[]{:S(2)}, u32[]{:S(2)}) collective-permute-start(bf16[1,1,1,304,768]{4,3,2,1,0:T(8,128)(2,1)S(1)} %get-tuple-element.297), channel_id=1, source_target_pairs={{0,4},{1,5},{2,6},{3,7},{4,0},{5,1},{6,2},{7,3},{8,12},{9,13},{10,... | collective-permute-start | bytes 1400840 | tf_op jit(solution)/shard_map/ppermute | solution.py:614
  524.0 27.6 %collective-permute-start.24 = (bf16[1,1,1,112,768]{4,3,2,1,0:T(8,128)(2,1)}, bf16[1,1,1,112,768]{4,3,2,1,0:T(8,128)(2,1)S(1)}, u32[]{:S(2)}, u32[]{:S(2)}) collective-permute-start(bf16[1,1,1,112,768]{4,3,2,1,0:T(8,128)(2,1)} %get-tuple-element.305), channel_id=1, source_target_pairs={{0,4},{1,5},{2,6},{3,7},{4,0},{5,1},{6,2},{7,3},{8,12},{9,13},{10,... | collective-permute-start | bytes 516104 | tf_op jit(solution)/shard_map/ppermute | solution.py:614
  (36 other events, 546.1 us)
Sparse Core Ops, SparseCore 0:
  14.5 109.3 all-gather.6
  127.5 79.0 all-gather.4
  403.8 158.0 reduce-scatter.1

commit v5 on v4

--- a/solution.py
+++ b/solution.py
@@ -713,6 +713,7 @@
 
     shares = [pack_layer(*(w[i] for w in weights)) for i in range(layer_count)]
     share = shares[0]
+    grad_state = jnp.pad(cotangent.astype(jnp.float32) * live, extra)
     if direct:
         row = jnp.concatenate([w.reshape(1, -1) for w in weights[4:]], 1)
         row = jnp.pad(row, ((0, 0), (0, share_rows * width - row.shape[1])))
@@ -739,7 +740,7 @@
         near = [rows] + [swap(rows, "dp", i, dp_size) for i in range(1, dp_size)]
         *more, final = mlp_of(0, middle)
         kept = [(*saved, middle, *more)]
-        blob_one, final = lax.optimization_barrier((blob_one, final))
+        blob_one, final, grad_state = lax.optimization_barrier((blob_one, final, grad_state))
         w_qkv, w_proj = unpack_whole(blob_one, ahead)
         w_qkv, near = lax.optimization_barrier((w_qkv, near))
         pieces = [v for n in near for v in (n, swap(n, "fsdp", 1, fsdp_size))]
@@ -761,8 +762,6 @@
             *saved, middle = attn_of(layer_index, state)
             *more, state = mlp_of(layer_index, middle)
             kept.append((*saved, middle, *more))
-    block_output = (state[:, :seq_len] * live).astype(jnp.bfloat16)
-    grad_state = jnp.pad(cotangent.astype(jnp.float32) * live, extra)
     layer_grads = [None] * layer_count
 
     def small_of(mlp, attn):
@@ -815,6 +814,7 @@
         late = mlp_one.sums() + attn_one.sums()
         late = Exchange(jnp.concatenate(late, 3), None, fsdp_size, (("z",),))
         late.step()
+        attn, state = lax.optimization_barrier((attn, state))
         attn_zero = Exchange(*with_small(shares, mlp, attn), fsdp_size, WHOLE)
         attn_zero.step()
         arrived = attn_zero.pending
@@ -831,6 +831,7 @@
             packed = pack_grads(grads, shapes, share.shape[0], devices)
             summed = lax.psum_scatter(packed, AXES, scatter_dimension=0, tiled=False)
             layer_grads[layer_index] = unpack_grads(summed, shapes)
+    block_output = (state[:, :seq_len] * live).astype(jnp.bfloat16)
     stacked = tuple((jnp.stack([entry[member] for entry in layer_grads]) for member in range(7)))
     return (block_output, grad_state[:, :seq_len], *stacked)
 

time: 585 us -> 579 us (0.990)
    unnamed x69 -> x71, local copies, waits for them, and re-layouts: 15.7 us -> 15.1 us
  transfers between devices with their start and end apart: 32 -> 32, of which waited for: 8 -> 10; matrix products, arithmetic and copies ran while one was open for 9% -> 9% of each run, Pallas kernels for 31% -> 31%
where the time goes in v5:
time: 579 us; the launch traced here: 569 us
  Pallas kernels  246 us (42%)
  waiting for transfers between devices  194 us (34%)
  local copies, waits for them, and re-layouts  41.9 us (7%)
  starting transfers between devices  41.2 us (7%)
  other arithmetic  29.9 us (5%)
  between operations  15.7 us (3%)
    all_gather x1, waiting for transfers between devices, on_device(): blob = lax.all_gather(share, AXES, axis=0, tiled=False)  107 us
    pallas_call x2, Pallas kernels, mlp_backward(): pl.pallas_call(partial(mlp_backward_kernel, mode, cut), grid=(blocks,), i...  75.3 us
    ppermute x29, waiting for transfers between devices, swap(): return lax.ppermute(value, axis, [(i, i ^ mask) for i in range(size)])  70.4 us
    pallas_call x2, Pallas kernels, attn_backward(): pl.pallas_call(partial(attn_backward_kernel, mode, cut), grid=(slots,), i...  59.9 us
    pallas_call x2, Pallas kernels, mlp_forward(): pl.pallas_call(mlp_forward_kernel, grid=(blocks,), in_specs=[whole(middle...  47.8 us
    ppermute x29, starting transfers between devices, swap(): return lax.ppermute(value, axis, [(i, i ^ mask) for i in range(size)])  41.1 us
    pallas_call x2, Pallas kernels, attn_forward(): pl.pallas_call(partial(attn_forward_kernel, seq_len), grid=(slots,), in_s...  36 us
    pallas_call x2, Pallas kernels, unpack_whole(): pl.pallas_call(unpack_kernel, grid=(devices // step,), in_specs=[pl.Block...  19.4 us
  transfers between devices with their start and end apart: 32, of which 10 were waited for; matrix products, arithmetic and copies ran while one was open for 9% of the time, Pallas kernels for 31%

profile of v5, /device:TPU:0, one launch (start us, length us, event | category | flops | bytes accessed | tf_op | source)
XLA Modules:
  0.0 569.5 jit_solution(3430446223657878490)
XLA Ops:
  17.2 106.7 %all-gather.7.cloned.1.call-done = bf16[9728,768]{1,0:T(8,128)(2,1)} async-done(((bf16[304,768]{1,0:T(8,128)(2,1)}), bf16[9728,768]{1,0:T(8,128)(2,1)}) %all-gather.7.cloned.1.call-update) | async-done | bytes 14942224 | tf_op jit(solution)/shard_map/all_gather | solution.py:721
  125.9 2.4 collective-permute-start.2
  128.3 12.6 %unpack_whole.2 = (bf16[32,72,768]{2,1,0:T(8,128)(2,1)}, bf16[32,24,768]{2,1,0:T(8,128)(2,1)}, bf16[32,96,768]{2,1,0:T(8,128)(2,1)}, bf16[4,32,24,768]{3,2,1,0:T(8,128)(2,1)}, bf16[32,16,768]{2,1,0:T(8,128)(2,1)}) custom-call(bf16[32,304,768]{2,1,0:T(8,128)(2,1)} %bitcast.146), custom_call_target="tpu_custom_call" | custom-call | flops 1000000000 | bytes 1048576 | tf_op jit(solution)/shard_map/unpack_whole/pallas_call | solution.py:492
  147.2 18.0 %attn_forward.2 = (bf16[4,208,768]{2,1,0:T(8,128)(2,1)}, bf16[4,208,2304]{2,1,0:T(8,128)(2,1)}, bf16[4,12,208,208]{3,2,1,0:T(8,128)(2,1)}, bf16[4,208,768]{2,1,0:T(8,128)(2,1)}, f32[4,208,768]{2,1,0:T(8,128)}) custom-call(f32[4,208,768]{2,1,0:T(8,128)} %pad_convert_fusion.x_ref, bf16[2304,768]{1,0:T(8,128)(2,1)} %bitcast.159, bf16[768,768]{1,0:T(8,128)(2,1)} %bitcast.175, ...), custom_call_target="tpu_custom_call" | custom-call | flops 1000000000 | bytes 1048576 | tf_op jit(solution)/shard_map/attn_forward/pallas_call | solution.py:141
  172.1 23.8 %mlp_forward.2 = (bf16[4,208,768]{2,1,0:T(8,128)(2,1)}, bf16[4,208,3072]{2,1,0:T(8,128)(2,1)}, bf16[4,208,3072]{2,1,0:T(8,128)(2,1)}, f32[4,208,768]{2,1,0:T(8,128)}) custom-call(f32[4,208,768]{2,1,0:T(8,128)} %get-tuple-element.172.middle_ref, bf16[3072,768]{1,0:T(8,128)(2,1)} %bitcast.138, bf16[4,768,768]{2,1,0:T(8,128)(2,1)} %bitcast.140, ...), custom_call_target="tpu_custom_call" | custom-call | flops 1000000000 | bytes 1048576 | tf_op jit(solution)/shard_map/mlp_forward/pallas_call | solution.py:194
  196.0 10.7 %all-gather.5.cloned.1.call-done = bf16[3072,768]{1,0:T(8,128)(2,1)} async-done(((bf16[96,768]{1,0:T(8,128)(2,1)}), bf16[3072,768]{1,0:T(8,128)(2,1)}) %all-gather.5.cloned.1.call-update) | async-done | bytes 4718608 | tf_op jit(solution)/shard_map/all_gather | solution.py:723
  206.6 6.9 %unpack_whole.3 = (bf16[32,72,768]{2,1,0:T(8,128)(2,1)}, bf16[32,24,768]{2,1,0:T(8,128)(2,1)}) custom-call(bf16[32,96,768]{2,1,0:T(8,128)(2,1)} %bitcast.155), custom_call_target="tpu_custom_call" | custom-call | flops 1000000000 | bytes 1048576 | tf_op jit(solution)/shard_map/unpack_whole/pallas_call | solution.py:492
  213.5 14.1 %collective-permute-done.4.refs_4_ = bf16[4,192,768]{2,1,0:T(8,128)(2,1)S(1)} collective-permute-done((bf16[4,192,768]{2,1,0:T(8,128)(2,1)S(1)}, bf16[4,192,768]{2,1,0:T(8,128)(2,1)S(1)}, u32[]{:S(2)}, u32[]{:S(2)}) %collective-permute-start.4) | collective-permute-done | bytes 1179680 | tf_op jit(solution)/shard_map/ppermute | solution.py:614
  228.7 18.0 %attn_forward.3 = (bf16[4,208,768]{2,1,0:T(8,128)(2,1)}, bf16[4,208,2304]{2,1,0:T(8,128)(2,1)}, bf16[4,12,208,208]{3,2,1,0:T(8,128)(2,1)}, bf16[4,208,768]{2,1,0:T(8,128)(2,1)}, f32[4,208,768]{2,1,0:T(8,128)}) custom-call(f32[4,208,768]{2,1,0:T(8,128)} %get-tuple-element.178.x_ref, bf16[2304,768]{1,0:T(8,128)(2,1)} %bitcast.147, bf16[768,768]{1,0:T(8,128)(2,1)} %bitcast.157, ...), custom_call_target="tpu_custom_call" | custom-call | flops 1000000000 | bytes 1048576 | tf_op jit(solution)/shard_map/attn_forward/pallas_call | solution.py:141
  246.8 8.0 %unpack_relative.1 = (bf16[32,96,768]{2,1,0:T(8,128)(2,1)}, bf16[4,32,24,768]{3,2,1,0:T(8,128)(2,1)}) custom-call(s32[1]{0:T(128)} %bitcast.me_ref, bf16[4,192,768]{2,1,0:T(8,128)(2,1)} %copy-done.1, bf16[4,192,768]{2,1,0:T(8,128)(2,1)} %collective-permute-done.6.refs_1_, bf16[4,192,768]{2,1,0:T(8,128)(2,1)} %copy-done.13, ...), custom_call_target="tpu_custom_call" | custom-call | flops 1000000000 | bytes 1048576 | tf_op jit(solution)/shard_map/unpack_relative/pallas_call | solution.py:505
  254.8 24.0 %mlp_forward.3 = (bf16[4,208,768]{2,1,0:T(8,128)(2,1)}, bf16[4,208,3072]{2,1,0:T(8,128)(2,1)}, bf16[4,208,3072]{2,1,0:T(8,128)(2,1)}, f32[4,208,768]{2,1,0:T(8,128)}) custom-call(f32[4,208,768]{2,1,0:T(8,128)} %get-tuple-element.194.middle_ref, bf16[3072,768]{1,0:T(8,128)(2,1)} %bitcast.142, bf16[4,768,768]{2,1,0:T(8,128)(2,1)} %bitcast.144, ...), custom_call_target="tpu_custom_call" | custom-call | flops 1000000000 | bytes 1048576 | tf_op jit(solution)/shard_map/mlp_forward/pallas_call | solution.py:194
  278.8 37.7 %mlp_backward.2 = (bf16[16,192,768]{2,1,0:T(8,128)(2,1)}, bf16[16,192,768]{2,1,0:T(8,128)(2,1)}, f32[4,8,768]{2,1,0:T(8,128)}, f32[8,768]{1,0:T(8,128)}, f32[4,208,768]{2,1,0:T(8,128)}) custom-call(s32[1]{0:T(128)} %bitcast.me_ref, f32[4,208,768]{2,1,0:T(8,128)} %pad.35.grad_ref, f32[4,208,768]{2,1,0:T(8,128)} %get-tuple-element.194.middle_ref, ...), custom_call_target="tpu_custom_call" | custom-call | flops 1000000000 | bytes 1048576 | tf_op jit(solution)/shard_map/mlp_backward/pallas_call | solution.py:324
  318.4 29.5 %attn_backward.2 = (bf16[16,112,768]{2,1,0:T(8,128)(2,1)}, bf16[16,112,768]{2,1,0:T(8,128)(2,1)}, f32[8,768]{1,0:T(8,128)}, f32[4,208,768]{2,1,0:T(8,128)}) custom-call(s32[1]{0:T(128)} %bitcast.me_ref, f32[4,208,768]{2,1,0:T(8,128)} %get-tuple-element.209.grad_ref, f32[4,208,768]{2,1,0:T(8,128)} %get-tuple-element.178.x_ref, ...), custom_call_target="tpu_custom_call" | custom-call | flops 1000000000 | bytes 1048576 | tf_op jit(solution)/shard_map/attn_backward/pallas_call | solution.py:438
  350.9 4.4 add_convert_fusion.2
  360.5 37.6 %mlp_backward.3 = (bf16[32,192,768]{2,1,0:T(8,128)(2,1)}, f32[4,8,768]{2,1,0:T(8,128)}, f32[8,768]{1,0:T(8,128)}, f32[4,208,768]{2,1,0:T(8,128)}) custom-call(s32[1]{0:T(128)} %bitcast.me_ref, f32[4,208,768]{2,1,0:T(8,128)} %get-tuple-element.219.grad_ref, f32[4,208,768]{2,1,0:T(8,128)} %get-tuple-element.172.middle_ref, ...), custom_call_target="tpu_custom_call" | custom-call | flops 1000000000 | bytes 1048576 | tf_op jit(solution)/shard_map/mlp_backward/pallas_call | solution.py:324
  400.0 3.5 add_convert_fusion.1
  415.3 30.3 %attn_backward.3 = (bf16[16,112,768]{2,1,0:T(8,128)(2,1)}, bf16[16,112,768]{2,1,0:T(8,128)(2,1)}, f32[8,768]{1,0:T(8,128)}, f32[4,208,768]{2,1,0:T(8,128)}) custom-call(s32[1]{0:T(128)} %bitcast.me_ref, f32[4,208,768]{2,1,0:T(8,128)} %get-tuple-element.232.grad_ref, f32[4,208,768]{2,1,0:T(8,128)} %pad_convert_fusion.x_ref, ...), custom_call_target="tpu_custom_call" | custom-call | flops 199999995904 | bytes 1048576 | tf_op jit(solution)/shard_map/attn_backward/pallas_call | solution.py:438
  446.7 2.6 collective-permute-done.15
  463.0 33.0 %collective-permute-done.26 = bf16[1,1,1,304,768]{4,3,2,1,0:T(8,128)(2,1)S(1)} collective-permute-done((bf16[1,1,1,304,768]{4,3,2,1,0:T(8,128)(2,1)S(1)}, bf16[1,1,1,304,768]{4,3,2,1,0:T(8,128)(2,1)S(1)}, u32[]{:S(2)}, u32[]{:S(2)}) %collective-permute-start.26) | collective-permute-done | bytes 466976 | tf_op jit(solution)/shard_map/ppermute | solution.py:614
  496.0 2.4 collective-permute-start.28
  502.7 7.8 %collective-permute-done.28 = bf16[1,1,1,304,768]{4,3,2,1,0:T(8,128)(2,1)S(1)} collective-permute-done((bf16[1,1,1,304,768]{4,3,2,1,0:T(8,128)(2,1)S(1)}, bf16[1,1,1,304,768]{4,3,2,1,0:T(8,128)(2,1)S(1)}, u32[]{:S(2)}, u32[]{:S(2)}) %collective-permute-start.28) | collective-permute-done | bytes 466976 | tf_op jit(solution)/shard_map/ppermute | solution.py:614
  516.5 13.8 %collective-permute-start.23 = (bf16[1,1,1,112,768]{4,3,2,1,0:T(8,128)(2,1)}, bf16[1,1,1,112,768]{4,3,2,1,0:T(8,128)(2,1)S(1)}, u32[]{:S(2)}, u32[]{:S(2)}) collective-permute-start(bf16[1,1,1,112,768]{4,3,2,1,0:T(8,128)(2,1)} %get-tuple-element.309), channel_id=1, source_target_pairs={{0,2},{1,3},{2,0},{3,1},{4,6},{5,7},{6,4},{7,5},{8,10},{9,11},{10,... | collective-permute-start | bytes 516104 | tf_op jit(solution)/shard_map/ppermute | solution.py:614
  536.8 11.7 %collective-permute-done.24 = bf16[1,1,1,112,768]{4,3,2,1,0:T(8,128)(2,1)S(1)} collective-permute-done((bf16[1,1,1,112,768]{4,3,2,1,0:T(8,128)(2,1)}, bf16[1,1,1,112,768]{4,3,2,1,0:T(8,128)(2,1)S(1)}, u32[]{:S(2)}, u32[]{:S(2)}) %collective-permute-start.24) | collective-permute-done | bytes 172064 | tf_op jit(solution)/shard_map/ppermute | solution.py:614
  549.5 6.1 %reduce-scatter.2.cloned.1.call-done = bf16[1,192,768]{2,1,0:T(8,128)(2,1)} async-done(((bf16[32,192,768]{2,1,0:T(8,128)(2,1)}), bf16[1,192,768]{2,1,0:T(8,128)(2,1)}) %reduce-scatter.2.cloned.1.call-update) | async-done | bytes 294928 | tf_op jit(solution)/shard_map/reduce_scatter | solution.py:808
  (265 shorter events, 88.1 us)
Async XLA Ops:
  7.2 116.7 %all-gather.7.cloned.1.call-start = ((), (), s32[]{:S(2)}) async-start(), calls=%async_computation.3 | async-start | bytes 15409152 | tf_op jit(solution)/shard_map/all_gather | solution.py:721
  14.4 192.2 %all-gather.5.cloned.1.call-start = ((), (), s32[]{:S(2)}) async-start(), calls=%async_computation.2 | async-start | bytes 4866048 | tf_op jit(solution)/shard_map/all_gather | solution.py:723
  15.2 540.5 %reduce-scatter.2.cloned.1.call-start = ((), (), s32[]{:S(2)}) async-start(), calls=%async_computation.1 | async-start | bytes 9732096 | tf_op jit(solution)/shard_map/reduce_scatter | solution.py:808
  123.9 41.3 %collective-permute-start = (bf16[192,768]{1,0:T(8,128)(2,1)S(1)}, bf16[192,768]{1,0:T(8,128)(2,1)S(1)}, u32[]{:S(2)}, u32[]{:S(2)}) collective-permute-start(bf16[192,768]{1,0:T(8,128)(2,1)S(1)} %pad_maximum_fusion.5), channel_id=1, source_target_pairs={{0,2},{1,3},{2,0},{3,1},{4,6},{5,7},{6,4},{7,5},{8,10},{9,11},{10,... | collective-permute-start | bytes 884744 | tf_op jit(solution)/shard_map/ppermute | solution.py:614
  124.4 40.8 %collective-permute-start.1 = (bf16[192,768]{1,0:T(8,128)(2,1)S(1)}, bf16[192,768]{1,0:T(8,128)(2,1)S(1)}, u32[]{:S(2)}, u32[]{:S(2)}) collective-permute-start(bf16[192,768]{1,0:T(8,128)(2,1)S(1)} %pad_maximum_fusion.5), channel_id=1, source_target_pairs={{0,4},{1,5},{2,6},{3,7},{4,0},{5,1},{6,2},{7,3},{8,12},{9,13},{10,... | collective-permute-start | bytes 884744 | tf_op jit(solution)/shard_map/ppermute | solution.py:614
  125.9 39.3 %collective-permute-start.2 = (bf16[192,768]{1,0:T(8,128)(2,1)S(1)}, bf16[192,768]{1,0:T(8,128)(2,1)S(1)}, u32[]{:S(2)}, u32[]{:S(2)}) collective-permute-start(bf16[192,768]{1,0:T(8,128)(2,1)S(1)} %pad_maximum_fusion.5), channel_id=1, source_target_pairs={{0,6},{1,7},{2,4},{3,5},{4,2},{5,3},{6,0},{7,1},{8,14},{9,15},{10,... | collective-permute-start | bytes 884744 | tf_op jit(solution)/shard_map/ppermute | solution.py:614
  165.4 48.1 %collective-permute-start.3 = (bf16[4,192,768]{2,1,0:T(8,128)(2,1)S(1)}, bf16[4,192,768]{2,1,0:T(8,128)(2,1)S(1)}, u32[]{:S(2)}, u32[]{:S(2)}) collective-permute-start(bf16[4,192,768]{2,1,0:T(8,128)(2,1)S(1)} %pad_maximum_fusion.1.refs_0_), channel_id=1, source_target_pairs={{0,8},{8,0},{16,24},{24,16},{1,9},{9,1},{17,25},{25,17},{2,10},{10... | collective-permute-start | bytes 3538952 | tf_op jit(solution)/shard_map/ppermute | solution.py:614
  166.9 60.7 %collective-permute-start.4 = (bf16[4,192,768]{2,1,0:T(8,128)(2,1)S(1)}, bf16[4,192,768]{2,1,0:T(8,128)(2,1)S(1)}, u32[]{:S(2)}, u32[]{:S(2)}) collective-permute-start(bf16[4,192,768]{2,1,0:T(8,128)(2,1)S(1)} %pad_maximum_fusion.1.refs_0_), channel_id=1, source_target_pairs={{0,16},{8,24},{16,0},{24,8},{1,17},{9,25},{17,1},{25,9},{2,18},{10... | collective-permute-start | bytes 3538952 | tf_op jit(solution)/shard_map/ppermute | solution.py:614
  167.5 60.1 %collective-permute-start.5 = (bf16[4,192,768]{2,1,0:T(8,128)(2,1)S(1)}, bf16[4,192,768]{2,1,0:T(8,128)(2,1)}, u32[]{:S(2)}, u32[]{:S(2)}) collective-permute-start(bf16[4,192,768]{2,1,0:T(8,128)(2,1)S(1)} %pad_maximum_fusion.1.refs_0_), channel_id=1, source_target_pairs={{0,24},{8,16},{16,8},{24,0},{1,25},{9,17},{17,9},{25,1},{2,26},{10... | collective-permute-start | bytes 3538952 | tf_op jit(solution)/shard_map/ppermute | solution.py:614
  316.4 31.5 %collective-permute-start.10 = (bf16[16,192,768]{2,1,0:T(8,128)(2,1)}, bf16[16,192,768]{2,1,0:T(8,128)(2,1)}, u32[]{:S(2)}, u32[]{:S(2)}) collective-permute-start(bf16[16,192,768]{2,1,0:T(8,128)(2,1)} %get-tuple-element.218), channel_id=1, source_target_pairs={{0,1},{1,0},{2,3},{3,2},{4,5},{5,4},{6,7},{7,6},{8,9},{9,8},{10,11... | collective-permute-start | bytes 14155784 | tf_op jit(solution)/shard_map/ppermute | solution.py:614
  350.4 49.5 %collective-permute-start.13 = (bf16[16,112,768]{2,1,0:T(8,128)(2,1)}, bf16[16,112,768]{2,1,0:T(8,128)(2,1)}, u32[]{:S(2)}, u32[]{:S(2)}) collective-permute-start(bf16[16,112,768]{2,1,0:T(8,128)(2,1)} %constant_dynamic-update-slice_fusion.5), channel_id=1, source_target_pairs={{0,1},{1,0},{2,3},{3,2},{4,5},{5,4},{6,7},{7,6},{8,9},{9,8},{10,11... | collective-permute-start | bytes 8257544 | tf_op jit(solution)/shard_map/ppermute | solution.py:614
  356.5 43.5 %collective-permute-start.12 = (bf16[1,2,4,96,768]{4,3,2,1,0:T(8,128)(2,1)}, bf16[1,2,4,96,768]{4,3,2,1,0:T(8,128)(2,1)}, u32[]{:S(2)}, u32[]{:S(2)}) collective-permute-start(bf16[1,2,4,96,768]{4,3,2,1,0:T(8,128)(2,1)} %bitcast.42), channel_id=1, source_target_pairs={{0,16},{8,24},{16,0},{24,8},{1,17},{9,25},{17,1},{25,9},{2,18},{10... | collective-permute-start | bytes 3538952 | tf_op jit(solution)/shard_map/ppermute | solution.py:614
  358.2 41.8 %collective-permute-start.11 = (bf16[2,1,4,96,768]{4,3,2,1,0:T(8,128)(2,1)}, bf16[2,1,4,96,768]{4,3,2,1,0:T(8,128)(2,1)}, u32[]{:S(2)}, u32[]{:S(2)}) collective-permute-start(bf16[2,1,4,96,768]{4,3,2,1,0:T(8,128)(2,1)} %slice.516), channel_id=1, source_target_pairs={{0,8},{8,0},{16,24},{24,16},{1,9},{9,1},{17,25},{25,17},{2,10},{10... | collective-permute-start | bytes 3538952 | tf_op jit(solution)/shard_map/ppermute | solution.py:614
  404.9 44.6 %collective-permute-start.16 = (bf16[1,1,4,112,768]{4,3,2,1,0:T(8,128)(2,1)}, bf16[1,1,4,112,768]{4,3,2,1,0:T(8,128)(2,1)}, u32[]{:S(2)}, u32[]{:S(2)}) collective-permute-start(bf16[1,1,4,112,768]{4,3,2,1,0:T(8,128)(2,1)} %get-tuple-element.299), channel_id=1, source_target_pairs={{0,8},{8,0},{16,24},{24,16},{1,9},{9,1},{17,25},{25,17},{2,10},{10... | collective-permute-start | bytes 2064392 | tf_op jit(solution)/shard_map/ppermute | solution.py:614
  405.3 44.3 %collective-permute-start.17 = (bf16[1,1,4,112,768]{4,3,2,1,0:T(8,128)(2,1)}, bf16[1,1,4,112,768]{4,3,2,1,0:T(8,128)(2,1)}, u32[]{:S(2)}, u32[]{:S(2)}) collective-permute-start(bf16[1,1,4,112,768]{4,3,2,1,0:T(8,128)(2,1)} %get-tuple-element.298), channel_id=1, source_target_pairs={{0,16},{8,24},{16,0},{24,8},{1,17},{9,25},{17,1},{25,9},{2,18},{10... | collective-permute-start | bytes 2064392 | tf_op jit(solution)/shard_map/ppermute | solution.py:614
  406.7 42.9 %collective-permute-start.18 = (bf16[1,1,4,112,768]{4,3,2,1,0:T(8,128)(2,1)}, bf16[1,1,4,112,768]{4,3,2,1,0:T(8,128)(2,1)}, u32[]{:S(2)}, u32[]{:S(2)}) collective-permute-start(bf16[1,1,4,112,768]{4,3,2,1,0:T(8,128)(2,1)} %get-tuple-element.297), channel_id=1, source_target_pairs={{0,24},{8,16},{16,8},{24,0},{1,25},{9,17},{17,9},{25,1},{2,26},{10... | collective-permute-start | bytes 2064392 | tf_op jit(solution)/shard_map/ppermute | solution.py:614
  411.0 38.3 %collective-permute-start.15 = (bf16[1,1,4,96,768]{4,3,2,1,0:T(8,128)(2,1)}, bf16[1,1,4,96,768]{4,3,2,1,0:T(8,128)(2,1)}, u32[]{:S(2)}, u32[]{:S(2)}) collective-permute-start(bf16[1,1,4,96,768]{4,3,2,1,0:T(8,128)(2,1)} %slice.526), channel_id=1, source_target_pairs={{0,8},{8,0},{16,24},{24,16},{1,9},{9,1},{17,25},{25,17},{2,10},{10... | collective-permute-start | bytes 1769480 | tf_op jit(solution)/shard_map/ppermute | solution.py:614
  413.9 35.7 %collective-permute-start.14 = (bf16[1,1,4,96,768]{4,3,2,1,0:T(8,128)(2,1)}, bf16[1,1,4,96,768]{4,3,2,1,0:T(8,128)(2,1)}, u32[]{:S(2)}, u32[]{:S(2)}) collective-permute-start(bf16[1,1,4,96,768]{4,3,2,1,0:T(8,128)(2,1)} %slice.524), channel_id=1, source_target_pairs={{0,16},{8,24},{16,0},{24,8},{1,17},{9,25},{17,1},{25,9},{2,18},{10... | collective-permute-start | bytes 1769480 | tf_op jit(solution)/shard_map/ppermute | solution.py:614
  456.1 39.9 %collective-permute-start.26 = (bf16[1,1,1,304,768]{4,3,2,1,0:T(8,128)(2,1)S(1)}, bf16[1,1,1,304,768]{4,3,2,1,0:T(8,128)(2,1)S(1)}, u32[]{:S(2)}, u32[]{:S(2)}) collective-permute-start(bf16[1,1,1,304,768]{4,3,2,1,0:T(8,128)(2,1)S(1)} %get-tuple-element.304), channel_id=1, source_target_pairs={{0,2},{1,3},{2,0},{3,1},{4,6},{5,7},{6,4},{7,5},{8,10},{9,11},{10,... | collective-permute-start | bytes 1400840 | tf_op jit(solution)/shard_map/ppermute | solution.py:614
  458.6 52.0 %collective-permute-start.20 = (bf16[1,1,4,112,768]{4,3,2,1,0:T(8,128)(2,1)S(1)}, bf16[1,1,4,112,768]{4,3,2,1,0:T(8,128)(2,1)S(1)}, u32[]{:S(2)}, u32[]{:S(2)}) collective-permute-start(bf16[1,1,4,112,768]{4,3,2,1,0:T(8,128)(2,1)S(1)} %get-tuple-element.296), channel_id=1, source_target_pairs={{0,8},{8,0},{16,24},{24,16},{1,9},{9,1},{17,25},{25,17},{2,10},{10... | collective-permute-start | bytes 2064392 | tf_op jit(solution)/shard_map/ppermute | solution.py:614
  460.1 50.4 %collective-permute-start.21 = (bf16[1,1,4,112,768]{4,3,2,1,0:T(8,128)(2,1)S(1)}, bf16[1,1,4,112,768]{4,3,2,1,0:T(8,128)(2,1)S(1)}, u32[]{:S(2)}, u32[]{:S(2)}) collective-permute-start(bf16[1,1,4,112,768]{4,3,2,1,0:T(8,128)(2,1)S(1)} %get-tuple-element.295), channel_id=1, source_target_pairs={{0,16},{8,24},{16,0},{24,8},{1,17},{9,25},{17,1},{25,9},{2,18},{10... | collective-permute-start | bytes 2064392 | tf_op jit(solution)/shard_map/ppermute | solution.py:614
  460.7 49.9 %collective-permute-start.22 = (bf16[1,1,4,112,768]{4,3,2,1,0:T(8,128)(2,1)S(1)}, bf16[1,1,4,112,768]{4,3,2,1,0:T(8,128)(2,1)S(1)}, u32[]{:S(2)}, u32[]{:S(2)}) collective-permute-start(bf16[1,1,4,112,768]{4,3,2,1,0:T(8,128)(2,1)S(1)} %get-tuple-element.294), channel_id=1, source_target_pairs={{0,24},{8,16},{16,8},{24,0},{1,25},{9,17},{17,9},{25,1},{2,26},{10... | collective-permute-start | bytes 2064392 | tf_op jit(solution)/shard_map/ppermute | solution.py:614
  462.2 40.6 %collective-permute-start.27 = (bf16[1,1,1,304,768]{4,3,2,1,0:T(8,128)(2,1)S(1)}, bf16[1,1,1,304,768]{4,3,2,1,0:T(8,128)(2,1)S(1)}, u32[]{:S(2)}, u32[]{:S(2)}) collective-permute-start(bf16[1,1,1,304,768]{4,3,2,1,0:T(8,128)(2,1)S(1)} %get-tuple-element.303), channel_id=1, source_target_pairs={{0,4},{1,5},{2,6},{3,7},{4,0},{5,1},{6,2},{7,3},{8,12},{9,13},{10,... | collective-permute-start | bytes 1400840 | tf_op jit(solution)/shard_map/ppermute | solution.py:614
  516.5 20.3 %collective-permute-start.23 = (bf16[1,1,1,112,768]{4,3,2,1,0:T(8,128)(2,1)}, bf16[1,1,1,112,768]{4,3,2,1,0:T(8,128)(2,1)S(1)}, u32[]{:S(2)}, u32[]{:S(2)}) collective-permute-start(bf16[1,1,1,112,768]{4,3,2,1,0:T(8,128)(2,1)} %get-tuple-element.309), channel_id=1, source_target_pairs={{0,2},{1,3},{2,0},{3,1},{4,6},{5,7},{6,4},{7,5},{8,10},{9,11},{10,... | collective-permute-start | bytes 516104 | tf_op jit(solution)/shard_map/ppermute | solution.py:614
  (37 other events, 470.7 us)
Sparse Core Ops, SparseCore 0:
  14.5 109.3 all-gather.6
  127.5 79.1 all-gather.4
  398.3 157.3 reduce-scatter.1
